TPU v7x, 512 devices: a whole 4x4x16 slice. The times are simulated.
512 devices in a mesh: ctx: 32 (over y_hi, z), tp: 16 (over x, y_lo, core).
Axes of the slice: x: 4, y: 4 (y_hi: 2, y_lo: 2; y = y_hi * 2 + y_lo), z: 16, core: 2. Of those that a mesh axis runs over, the one named last changes fastest.
Arguments:
- queries: bfloat16 [4096, 12288], P('ctx', 'tp'), may hold values from -8 to 8
- keys: bfloat16 [4096, 1024], P('ctx'), may hold values from -16 to 16
- values: bfloat16 [4096, 1024], P('ctx'), may hold values from -6 to 6
- doc_ids: int32 [4096], replicated, may hold values from 0 to 3, never falling along the last dimension, each value on 1 to 2560 neighbouring positions
- replica_of: int32 [4], replicated, may hold values from 0 to 31, as said below
- step_query: bfloat16 [4, 12288], P(None, 'tp'), may hold values from -8 to 8
- step_key: bfloat16 [4, 1024], replicated, may hold values from -16 to 16
- step_value: bfloat16 [4, 1024], replicated, may hold values from -6 to 6
- out_weight: bfloat16 [12288, 12288], P('tp', 'ctx'), may hold values from -0.0546875 to 0.0546875
Outputs:
- context: bfloat16 [4096, 12288], P('ctx', 'tp')
- next_hidden: bfloat16 [32, 12288], P(None, 'ctx')
- replica_keys: bfloat16 [32, 1024, 2560], P('ctx', 'tp')
- replica_values: bfloat16 [32, 1024, 2560], P('ctx', 'tp')
Inputs may be any that keep to these rules, and one draw needn't show every extreme that they name: `doc_ids`: documents occupy whole runs of positions in rising order; each has 1 to 2560 positions, and one has exactly 2560. `replica_of`: the documents name distinct replicas.
All inputs are finite; a program needn't handle non-finite values.
Results may differ from a plain program's by a relative error of at most 0.02.
Values may be sent and summed in bfloat16 or wider, within the bound.
No kernel may reach another device: no remote copies, remote signals or barrier semaphores. Data moves between devices by JAX's collectives and lax.ppermute only.
A program may use at most 64 MiB of HBM per device.

v0:
```python
import math

import jax
import jax.numpy as jnp
from jax import lax
from jax.sharding import PartitionSpec as P

H = 96
KVH = 8
HD = 128


def local(queries, keys, values, doc_ids, replica_of, step_query, step_key, step_value, out_weight):
    row_count = queries.shape[0]
    heads_dev = queries.shape[1] // HD
    group_size = H // KVH
    kv_dev = max(1, heads_dev // group_size)
    per_kv = heads_dev // kv_dev
    score_scale = 1.0 / math.sqrt(HD)
    cache_most = 5 * (row_count * lax.axis_size("ctx")) // 8
    column_width = keys.shape[1] // lax.axis_size("tp")
    ctx_index = lax.axis_index("ctx")
    tp_index = lax.axis_index("tp")
    first_kv = tp_index * heads_dev // group_size
    column_offset = tp_index * column_width - first_kv * HD
    key_own = lax.dynamic_slice_in_dim(keys, first_kv * HD, kv_dev * HD, 1)
    value_own = lax.dynamic_slice_in_dim(values, first_kv * HD, kv_dev * HD, 1)
    query_pos = ctx_index * row_count + jnp.arange(row_count, dtype=jnp.int32)
    query_doc = lax.dynamic_slice_in_dim(doc_ids, ctx_index * row_count, row_count, 0)
    grouped = queries.reshape(row_count, kv_dev, per_kv, HD).transpose(1, 2, 0, 3)
    grouped = grouped.reshape(kv_dev, per_kv * row_count, HD)
    row_pos = jnp.tile(query_pos, per_kv)
    row_doc = jnp.tile(query_doc, per_kv)
    match_rows = (replica_of == ctx_index).astype(jnp.int32)
    has_request = jnp.sum(match_rows) > 0
    my_doc = jnp.sum(match_rows * jnp.arange(replica_of.shape[0], dtype=jnp.int32))
    doc_start = jnp.sum((doc_ids < my_doc).astype(jnp.int32))
    doc_length = jnp.sum((doc_ids == my_doc).astype(jnp.int32))
    attend_init = (
        jnp.full((kv_dev, per_kv * row_count), -1e30, jnp.float32),
        jnp.zeros((kv_dev, per_kv * row_count), jnp.float32),
        jnp.zeros((kv_dev, per_kv * row_count, HD), jnp.float32),
    )
    cache_init = (
        jnp.zeros((cache_most, kv_dev * HD), jnp.bfloat16),
        jnp.zeros((cache_most, kv_dev * HD), jnp.bfloat16),
    )
    key_piece = lax.all_gather(key_own, "ctx", axis=0, tiled=True)
    value_piece = lax.all_gather(value_own, "ctx", axis=0, tiled=True)
    piece_rows = key_piece.shape[0]
    key_pos = jnp.arange(piece_rows, dtype=jnp.int32)
    key_doc = doc_ids
    allowed = (key_doc[None, :] == row_doc[:, None]) & (key_pos[None, :] <= row_pos[:, None])

    def update(old_state):
        row_top, row_total, accumulated = old_state
        key_heads = key_piece.reshape(piece_rows, kv_dev, HD)
        value_heads = value_piece.reshape(piece_rows, kv_dev, HD)
        scores = (
            jnp.einsum("kqd,pkd->kqp", grouped, key_heads, preferred_element_type=jnp.float32)
            * score_scale
        )
        masked = jnp.where(allowed[None], scores, -1e30)
        new_top = jnp.maximum(row_top, jnp.max(masked, axis=-1))
        weights = jnp.where(allowed[None], jnp.exp(scores - new_top[..., None]), 0.0)
        row_total = jnp.sum(weights, axis=-1)
        added = jnp.einsum(
            "kqp,pkd->kqd",
            weights.astype(jnp.bfloat16),
            value_heads,
            preferred_element_type=jnp.float32,
        )
        accumulated = added
        return (new_top, row_total, accumulated)

    attend_state = lax.cond(jnp.any(allowed), update, lambda old_state: old_state, attend_init)
    place_key_piece = lax.all_gather(key_own, "ctx", axis=0, tiled=True)
    place_value_piece = lax.all_gather(value_own, "ctx", axis=0, tiled=True)
    place_piece_rows = place_key_piece.shape[0]
    key_pos = jnp.arange(place_piece_rows, dtype=jnp.int32)
    key_doc = doc_ids
    keep_rows = (key_doc == my_doc) & has_request
    offset = jnp.where(keep_rows, key_pos - doc_start, cache_most)
    cache_keys = cache_init[0].at[offset].set(place_key_piece, mode="drop")
    cache_values = cache_init[1].at[offset].set(place_value_piece, mode="drop")
    cache_state = (cache_keys, cache_values)
    row_top, row_total, accumulated = attend_state
    context = (accumulated / row_total[..., None]).reshape(kv_dev, per_kv, row_count, HD)
    context = context.transpose(2, 0, 1, 3).reshape(row_count, heads_dev * HD).astype(jnp.bfloat16)
    delivered_keys = lax.dynamic_slice_in_dim(cache_state[0], column_offset, column_width, 1)
    delivered_values = lax.dynamic_slice_in_dim(cache_state[1], column_offset, column_width, 1)
    replica_keys = jnp.transpose(delivered_keys, (1, 0))[None]
    replica_values = jnp.transpose(delivered_values, (1, 0))[None]
    cache_keys = cache_state[0].reshape(cache_most, kv_dev, HD)
    cache_values = cache_state[1].reshape(cache_most, kv_dev, HD)
    query_row = lax.dynamic_slice_in_dim(step_query, my_doc, 1, 0).reshape(kv_dev, per_kv, HD)
    own_key = lax.dynamic_slice(step_key, (my_doc, first_kv * HD), (1, kv_dev * HD))
    own_value = lax.dynamic_slice(step_value, (my_doc, first_kv * HD), (1, kv_dev * HD))
    cached = (
        jnp.einsum("kgd,mkd->kgm", query_row, cache_keys, preferred_element_type=jnp.float32)
        * score_scale
    )
    own_score = (
        jnp.einsum("kgd,kd->kg", query_row, own_key, preferred_element_type=jnp.float32)
        * score_scale
    )
    valid_slots = jnp.arange(cache_most, dtype=jnp.int32) < doc_length
    step_top = jnp.maximum(
        jnp.max(jnp.where(valid_slots[None, None], cached, -1e30), axis=-1), own_score
    )
    weights = jnp.where(valid_slots[None, None], jnp.exp(cached - step_top[..., None]), 0.0)
    own_prob = jnp.exp(own_score - step_top)
    step_total = jnp.sum(weights, axis=-1) + own_prob
    own_rounded = lax.optimization_barrier(own_prob.astype(jnp.bfloat16)).astype(jnp.float32)
    mixed_sum = jnp.einsum(
        "kgm,mkd->kgd",
        weights.astype(jnp.bfloat16),
        cache_values,
        preferred_element_type=jnp.float32,
    )
    mixed_sum = mixed_sum + own_rounded[..., None] * own_value.astype(jnp.float32)[:, None, :]
    decode_row = (mixed_sum / step_total[..., None]).reshape(1, heads_dev * HD)
    decode_row = jnp.where(has_request, decode_row, 0.0).astype(jnp.bfloat16)
    gathered = lax.all_gather(decode_row, "ctx", axis=0, tiled=True)
    partial_value = jnp.dot(gathered, out_weight, preferred_element_type=jnp.float32)
    next_hidden = lax.psum(partial_value.astype(jnp.bfloat16), "tp")
    return (context, next_hidden, replica_keys, replica_values)


def solution(mesh):
    placed = (
        P("ctx", "tp"),
        P("ctx", None),
        P("ctx", None),
        P(),
        P(),
        P(None, "tp"),
        P(),
        P(),
        P("tp", "ctx"),
    )
    return jax.shard_map(
        local,
        mesh=mesh,
        in_specs=placed,
        out_specs=(P("ctx", "tp"), P(None, "ctx"), P("ctx", "tp", None), P("ctx", "tp", None)),
        check_vma=False,
    )
```

profile of v0, /device:TPU:1, one launch (start us, length us, event | category | flops | bytes accessed | tf_op | source)
XLA Modules:
  0.0 469.9 jit_solution(6769226028582171456)
XLA Ops:
  7.3 1.4 constant_dynamic-slice_fusion.1
  8.8 1.4 constant_dynamic-slice_fusion
  10.2 0.8 dynamic_slice.24
  11.0 7.0 %fusion.9 = (pred[768,4096]{1,0:T(32,128)(4,1)}, pred[]{:T(512)}) fusion(s32[768]{0:T(1024)S(1)} %get-tuple-element.62, s32[4096]{0:T(1024)} %param.14, s32[768]{0:T(1024)S(1)} %get-tuple-element.63), kind=kLoop, calls=%fused_computation.12 | loop fusion | flops 12582911 | bytes 3168257 | tf_op jit(solution)/shard_map/and | solution.py:53
  18.6 1.1 copy.31
  19.7 1.3 fusion.28
  23.6 0.7 dynamic-slice_reduce_fusion
  24.3 0.8 bitcast_convert_fusion
  25.1 2.1 convert_reduce_fusion.1
  27.1 0.7 iota_compare_fusion.1
  27.8 0.9 fusion.13
  29.3 121.5 %all-gather.4.cloned.1.call-done = bf16[4096,128]{1,0:T(8,128)(2,1)} async-done(((bf16[128,128]{1,0:T(8,128)(2,1)}), bf16[4096,128]{1,0:T(8,128)(2,1)}) %all-gather.4.cloned.1.call-update) | async-done | bytes 1048592 | tf_op jit(solution)/shard_map/all_gather | solution.py:48
  150.8 140.9 %all-gather.6.cloned.1.call-done = bf16[4096,128]{1,0:T(8,128)(2,1)} async-done(((bf16[128,128]{1,0:T(8,128)(2,1)}), bf16[4096,128]{1,0:T(8,128)(2,1)}) %all-gather.6.cloned.1.call-update) | async-done | bytes 1048592 | tf_op jit(solution)/shard_map/all_gather | solution.py:49
  291.8 12.9 %conditional.1 = (f32[1,768]{1,0:T(1,128)S(1)}, f32[1,768,128]{2,1,0:T(8,128)S(1)}) conditional(s32[]{:T(128)} %convert_element_type.57, () %tuple.16, (bf16[1,6,128,128]{2,3,1,0:T(8,128)(2,1)S(1)}, bf16[4096,128]{1,0:T(8,128)(2,1)}, pred[768,4096]{1,0:T(32,128)(4,1)}, bf16[4096,128]{1,0:T(8,128)(2,1)}) %tuple.40), branch_computations={%region_1.2_spmd, %region_2.0_spmd} | conditional | flops 1645214976 | bytes 67067976 | solution.py:76
  291.9 4.9 %select_reduce_fusion = (f32[768]{0:T(1024)S(1)}, f32[768,4096]{1,0:T(8,128)S(1)}) fusion(pred[768,4096]{1,0:T(32,128)(4,1)} %get-tuple-element.9, bf16[768,128]{1,0:T(8,128)(2,1)S(1)} %bitcast.54, bf16[4096,128]{1,0:T(8,128)(2,1)} %get-tuple-element.11), kind=kOutput, calls=%fused_computation.3 | convolution fusion | flops 814742784 | bytes 16976896 | tf_op jit(solution)/shard_map/cond/branch_1_fun/kqd,pkd->kqp/dot_general | solution.py:60
  296.9 3.8 fusion.1
  300.7 3.9 fusion.4
  305.0 0.8 copy.34
  305.8 11.3 %scatter_custom_fusion = bf16[2560,128]{1,0:T(8,128)(2,1)S(1)} fusion(s32[4096]{0:T(1024)S(1)} %compare_select_fusion, bf16[4096,128]{1,0:T(8,128)(2,1)} %all-gather.4.cloned.1.call-done, bf16[]{:T(256)} %constant.22.clone.1), kind=kCustom, calls=%fused_computation.26 | custom fusion | bytes 655872 | tf_op jit(solution)/shard_map/scatter | solution.py:84
  318.0 11.3 %scatter_custom_fusion.1 = bf16[2560,128]{1,0:T(8,128)(2,1)S(1)} fusion(s32[4096]{0:T(1024)S(1)} %compare_select_fusion, bf16[4096,128]{1,0:T(8,128)(2,1)} %all-gather.6.cloned.1.call-done, bf16[]{:T(256)} %constant.22.clone.1), kind=kCustom, calls=%fused_computation.24 | custom fusion | bytes 655872 | tf_op jit(solution)/shard_map/scatter | solution.py:85
  329.9 58.7 %all-gather = bf16[32,1,768]{2,1,0:T(2,128)(2,1)S(1)} all-gather(bf16[1,1,768]{2,1,0:T(2,128)(2,1)S(1)} %reshape.167), channel_id=1, replica_groups=mesh['ctx'=32,'tp'=16] {'ctx'}, dimensions={0}, use_global_device_ids=true | all-gather | bytes 50688 | tf_op jit(solution)/shard_map/all_gather | solution.py:124
  388.8 72.3 %psum.7 = bf16[32,384]{1,0:T(8,128)(2,1)} all-reduce(bf16[32,384]{1,0:T(8,128)(2,1)S(1)} %convolution_convert_fusion), channel_id=1, replica_groups=mesh['ctx'=32,'tp'=16] {'tp'}, use_global_device_ids=true, to_apply=%region_13.14 | all-reduce | flops 12288 | bytes 49152 | tf_op jit(solution)/shard_map/psum | solution.py:126
  461.1 1.0 copy.35
  462.1 1.0 copy.36
  (29 shorter events, 2.9 us)
Async XLA Ops:
  7.2 381.4 %copy-start = (bf16[768,384]{1,0:T(8,128)(2,1)S(1)}, bf16[768,384]{1,0:T(8,128)(2,1)}, u32[]{:S(2)}) copy-start(bf16[768,384]{1,0:T(8,128)(2,1)} %param.19) | copy-start | bytes 1769476
  7.2 143.7 %all-gather.4.cloned.1.call-start = ((), (), s32[]{:S(2)}) async-start(), calls=%async_computation | async-start | bytes 1081344 | tf_op jit(solution)/shard_map/all_gather | solution.py:48
  8.7 283.0 %all-gather.6.cloned.1.call-start = ((), (), s32[]{:S(2)}) async-start(), calls=%async_computation.1 | async-start | bytes 1081344 | tf_op jit(solution)/shard_map/all_gather | solution.py:49
  291.9 4.9 %copy-start.1 = (pred[768,4096]{1,0:T(32,128)(4,1)S(1)}, pred[768,4096]{1,0:T(32,128)(4,1)}, u32[]{:S(2)}) copy-start(pred[768,4096]{1,0:T(32,128)(4,1)} %get-tuple-element.9) | copy-start | bytes 9437188 | tf_op jit(solution)/shard_map/cond
  296.8 3.8 copy-start.2
Sparse Core Ops, SparseCore 0:
  11.7 139.1 all-gather.3
  154.5 137.1 all-gather.5
where the time goes:
time: 473 us; the launch traced here: 470 us
  waiting for transfers between devices  262 us (55%)
  blocking collectives  131 us (28%)
  local copies, waits for them, and re-layouts  31.6 us (7%)
  between operations  17.4 us (4%)
  other arithmetic  16.7 us (4%)
  matrix products  10.5 us (2%)
    all_gather x1, waiting for transfers between devices, local(): value_piece = lax.all_gather(value_own, 'ctx', axis=0, tiled=True)  141 us
    all_gather x1, waiting for transfers between devices, local(): key_piece = lax.all_gather(key_own, 'ctx', axis=0, tiled=True)  122 us
    psum x1, blocking collectives, local(): next_hidden = lax.psum(partial_value.astype(jnp.bfloat16), 'tp')  72.3 us
    all_gather x1, blocking collectives, local(): gathered = lax.all_gather(decode_row, 'ctx', axis=0, tiled=True)  58.7 us
    scatter x1, local copies, waits for them, and re-layouts, local(): cache_values = cache_init[1].at[offset].set(place_value_piece, mode='drop')  11.3 us
    scatter x1, local copies, waits for them, and re-layouts, local(): cache_keys = cache_init[0].at[offset].set(place_key_piece, mode='drop')  11.3 us
  transfers between devices with their start and end apart: 2, of which 2 were waited for; matrix products, arithmetic and copies ran while one was open for 4% of the time, Pallas kernels for 0%

commit v1 on v0

v1 whole, which is shorter than its diff:
```python
import math

import jax
import jax.numpy as jnp
import numpy as np
from jax import lax
from jax.experimental import pallas as pl
from jax.experimental.pallas import tpu as pltpu
from jax.sharding import Mesh
from jax.sharding import PartitionSpec as P

H = 96
KVH = 8
HD = 128
NDOC = 4
ROWS = 128
NB = 32
MOST = 2560
HEADS = 6
SCALE = 1.0 / math.sqrt(HD)
CTX = ("yh", "z1", "z0")
TP = ("x", "yl", "c")
NEG = -1e30


def pick_kernel(meta, keys, values, out):
    out[...] = jnp.where(meta[1] == 0, keys[...], values[...])


def pick(meta, keys, values):
    head = pl.BlockSpec((ROWS, HD), lambda i, m: (0, m[2]))
    return pl.pallas_call(
        pick_kernel,
        out_shape=jax.ShapeDtypeStruct((ROWS, HD), jnp.bfloat16),
        grid_spec=pltpu.PrefetchScalarGridSpec(
            num_scalar_prefetch=1,
            grid=(1,),
            in_specs=[head, head],
            out_specs=pl.BlockSpec((ROWS, HD), lambda i, m: (0, 0)),
        ),
        name="pick",
    )(meta, keys, values)


def attend_kernel(
    meta, replica_of, doc_ids, queries, step_query, step_key, step_value, weight,
    own0, own1, own2, own3, own4, got0, got1, got2, got3, got4,
    context, terms, replica_keys, replica_values,
    cache, q48, top, total, acc,
):
    ctx, core, z0 = meta[0], meta[1], meta[3]
    classes = ((own0, got0, 0, 0, 8), (own1, got1, 3, 0, 8), (own2, got2, 1, 0, 8), (own3, got3, 2, 0, 4), (own4, got4, 2, 4, 8))
    for own, got, shift, first, last in classes:
        rest = lax.rem(z0 + shift, 4)
        for g in range(first, last):
            cache[core, (g // 4) * 16 + (g % 4) * 4 + rest] = own[g - first]
            cache[1 - core, (g // 4) * 16 + (g % 4) * 4 + rest] = got[g - first]
    cache[:, NB] = jnp.zeros((2, ROWS, HD), jnp.bfloat16)
    ids = doc_ids[...]
    starts = [jnp.int32(0)] + [jnp.sum((ids < d).astype(jnp.int32)) for d in range(1, NDOC)]
    ends = starts[1:] + [jnp.int32(NB * ROWS)]

    q48[...] = jnp.zeros_like(q48)
    steps = step_query[...].astype(jnp.float32)
    for h in range(HEADS):
        q48[h * 8 : h * 8 + NDOC, :] = steps[:, h * HD : (h + 1) * HD]
    q = q48[...]
    pad = jnp.zeros((8 - NDOC, HD), jnp.float32)
    own_key = jnp.concatenate([step_key[...].astype(jnp.float32), pad] * HEADS, axis=0)
    own_value = jnp.concatenate([step_value[...].astype(jnp.float32), pad] * HEADS, axis=0)
    doc_row = lax.broadcasted_iota(jnp.int32, (HEADS * 8, 1), 0) % 8
    low = jnp.full((HEADS * 8, 1), NB * ROWS, jnp.int32)
    high = jnp.zeros((HEADS * 8, 1), jnp.int32)
    for d in range(NDOC):
        low = jnp.where(doc_row == d, starts[d], low)
        high = jnp.where(doc_row == d, ends[d], high)
    all_keys = cache[0, :NB].reshape(NB * ROWS, HD)
    all_values = cache[1, :NB].reshape(NB * ROWS, HD)
    nums = lax.dot_general(q.astype(jnp.bfloat16), all_keys, (((1,), (1,)), ((), ())), preferred_element_type=jnp.float32)
    nums = nums * SCALE
    place = lax.broadcasted_iota(jnp.int32, (HEADS * 8, NB * ROWS), 1)
    nums = jnp.where((place >= low) & (place < high), nums, NEG)
    own_score = jnp.sum(q * own_key, axis=1, keepdims=True) * SCALE
    step_top = jnp.maximum(jnp.max(nums, axis=1, keepdims=True), own_score)
    probs = jnp.exp(nums - step_top)
    own_prob = jnp.exp(own_score - step_top)
    step_total = jnp.sum(probs, axis=1, keepdims=True) + own_prob
    mixed = jnp.dot(probs.astype(jnp.bfloat16), all_values, preferred_element_type=jnp.float32)
    mixed = mixed + own_prob.astype(jnp.bfloat16).astype(jnp.float32) * own_value
    attended = mixed / step_total
    wide = jnp.concatenate([attended[h * 8 : (h + 1) * 8, :] for h in range(HEADS)], axis=1)
    term = jnp.dot(wide.astype(jnp.bfloat16), weight[...], preferred_element_type=jnp.float32)
    for k in range(16):
        terms[k] = term

    row = ctx * ROWS + lax.broadcasted_iota(jnp.int32, (ROWS, 1), 0)
    row_start = jnp.zeros((ROWS, 1), jnp.int32)
    first = jnp.int32(0)
    for d in range(1, NDOC):
        row_start = jnp.where(row >= starts[d], starts[d], row_start)
        first = jnp.where(ctx * ROWS >= starts[d], starts[d], first)
    top[...] = jnp.full_like(top, NEG)
    total[...] = jnp.zeros_like(total)
    acc[...] = jnp.zeros_like(acc)
    block0 = first // ROWS
    factor = SCALE * math.log2(math.e)

    def chunk(i, carry):
        at = block0 + 2 * i
        key2 = cache[0, pl.ds(at, 2)].reshape(2 * ROWS, HD)
        value2 = cache[1, pl.ds(at, 2)].reshape(2 * ROWS, HD)
        col = at * ROWS + lax.broadcasted_iota(jnp.int32, (ROWS, 2 * ROWS), 1)
        allowed = (col <= row) & (col >= row_start)
        for h in range(HEADS):
            part = queries[:, h * HD : (h + 1) * HD]
            s = lax.dot_general(part, key2, (((1,), (1,)), ((), ())), preferred_element_type=jnp.float32)
            s = jnp.where(allowed, s * factor, NEG)
            old = top[h]
            new = jnp.maximum(old, jnp.max(s, axis=1, keepdims=True))
            p = jnp.exp2(s - new[:, :1])
            alpha = jnp.exp2(old - new)
            total[h] = total[h] * alpha + jnp.sum(p, axis=1, keepdims=True)
            acc[h] = acc[h] * alpha + jnp.dot(p.astype(jnp.bfloat16), value2, preferred_element_type=jnp.float32)
            top[h] = new
        return carry

    lax.fori_loop(0, (ctx - block0 + 2) // 2, chunk, 0)
    for h in range(HEADS):
        context[:, h * HD : (h + 1) * HD] = (acc[h] / total[h]).astype(jnp.bfloat16)

    asked = jnp.int32(0)
    start = jnp.int32(0)
    length = jnp.int32(0)
    for d in range(NDOC):
        mine = replica_of[d] == ctx
        asked = jnp.where(mine, 1, asked)
        start = jnp.where(mine, starts[d], start)
        length = jnp.where(mine, ends[d] - starts[d], length)

    @pl.when(asked == 0)
    def _():
        replica_keys[...] = jnp.zeros_like(replica_keys)
        replica_values[...] = jnp.zeros_like(replica_values)

    @pl.when(asked == 1)
    def _():
        offset = lax.rem(start, ROWS)
        begin = start // ROWS
        r = lax.broadcasted_iota(jnp.int32, (2 * ROWS, ROWS), 0)
        s = lax.broadcasted_iota(jnp.int32, (2 * ROWS, ROWS), 1)
        hot = (r == s + offset).astype(jnp.bfloat16)
        slot = lax.broadcasted_iota(jnp.int32, (HD // 2, ROWS), 1)
        for i in range(MOST // ROWS):
            at = jnp.minimum(begin + i, NB - 1)
            live = slot + i * ROWS < length
            for which, out in ((0, replica_keys), (1, replica_values)):
                source = cache[which, pl.ds(at, 2)].reshape(2 * ROWS, HD)
                moved = lax.dot_general(source, hot, (((0,), (0,)), ((), ())), preferred_element_type=jnp.float32)
                moved = jnp.where(core == 0, moved[: HD // 2], moved[HD // 2 :])
                out[:, i * ROWS : (i + 1) * ROWS] = jnp.where(live, moved, 0.0).astype(jnp.bfloat16)


def attend(meta, replica_of, doc_ids, queries, step_query, step_key, step_value, weight, own, got):
    def whole(x):
        return pl.BlockSpec(x.shape, lambda i, m, n, nd=len(x.shape): (0,) * nd)

    head = pl.BlockSpec((NDOC, HD), lambda i, m, n: (0, m[2]))
    outs = (
        jax.ShapeDtypeStruct((ROWS, HEADS * HD), jnp.bfloat16),
        jax.ShapeDtypeStruct((16, 8, weight.shape[1]), jnp.float32),
        jax.ShapeDtypeStruct((HD // 2, MOST), jnp.bfloat16),
        jax.ShapeDtypeStruct((HD // 2, MOST), jnp.bfloat16),
    )
    return pl.pallas_call(
        attend_kernel,
        out_shape=outs,
        grid_spec=pltpu.PrefetchScalarGridSpec(
            num_scalar_prefetch=2,
            grid=(1,),
            in_specs=[whole(doc_ids), whole(queries), whole(step_query), head, head, whole(weight)] + [whole(x) for x in own + got],
            out_specs=[whole(x) for x in outs],
            scratch_shapes=[
                pltpu.VMEM((2, NB + 1, ROWS, HD), jnp.bfloat16),
                pltpu.VMEM((HEADS * 8, HD), jnp.float32),
                pltpu.VMEM((HEADS, ROWS, HD), jnp.float32),
                pltpu.VMEM((HEADS, ROWS, HD), jnp.float32),
                pltpu.VMEM((HEADS, ROWS, HD), jnp.float32),
            ],
        ),
        compiler_params=pltpu.CompilerParams(vmem_limit_bytes=40 * 1024 * 1024),
        name="attend",
    )(meta, replica_of, doc_ids, queries, step_query, step_key, step_value, weight, *own, *got)


def local(queries, keys, values, doc_ids, replica_of, step_query, step_key, step_value, out_weight):
    x, yl, core = lax.axis_index("x"), lax.axis_index("yl"), lax.axis_index("c")
    z0 = lax.axis_index("z0")
    ctx = lax.axis_index("yh") * 16 + lax.axis_index("z1") * 4 + z0
    meta = jnp.stack([ctx, core, x * 2 + yl, z0]).astype(jnp.int32)
    mine = pick(meta, keys, values)

    def along_z(a, by):
        return lax.ppermute(a, ("z1", "z0"), [(i, (i + by) % 16) for i in range(16)])

    def across(a):
        return lax.ppermute(a, "c", [(0, 1), (1, 0)])

    far = lax.all_to_all(jnp.broadcast_to(mine[None], (8, ROWS, HD)), ("yh", "z1"), 0, 0)
    own = [far, along_z(far, 1), along_z(far, -1), along_z(far[:4], 2), along_z(far[4:], -2)]
    got = [across(a) for a in own]
    context, terms, replica_keys, replica_values = attend(
        meta, replica_of, doc_ids.reshape(NB, ROWS), queries, step_query, step_key, step_value, out_weight, own, got
    )
    parts = lax.all_to_all(terms, TP, 0, 0)
    projected = jnp.sum(parts, axis=0)
    replicas = jnp.arange(NB, dtype=jnp.int32)
    next_hidden = jnp.zeros((NB, out_weight.shape[1]), jnp.float32)
    for d in range(NDOC):
        next_hidden = jnp.where((replicas == replica_of[d])[:, None], projected[d][None, :], next_hidden)
    return (context, next_hidden.astype(jnp.bfloat16), replica_keys[None], replica_values[None])


def solution(mesh):
    fine = Mesh(np.asarray(mesh.devices).reshape(2, 4, 4, 4, 2, 2), CTX + TP)
    placed = (
        P(CTX, TP),
        P(CTX, None),
        P(CTX, None),
        P(),
        P(),
        P(None, TP),
        P(),
        P(),
        P(TP, CTX),
    )
    return jax.shard_map(
        local,
        mesh=fine,
        in_specs=placed,
        out_specs=(P(CTX, TP), P(None, CTX), P(CTX, TP, None), P(CTX, TP, None)),
        check_vma=False,
    )
```

time: 473 us -> 97.1 us (0.21)
  the two profiles are of different devices: /device:TPU:1 before, /device:TPU:49 now
where the time goes in v1:
time: 97.1 us; the launch traced here: 96.4 us
  blocking collectives  35.5 us (37%)
  starting transfers between devices  32.3 us (33%)
  Pallas kernels  17.5 us (18%)
  waiting for transfers between devices  4.56 us (5%)
  other arithmetic  3.86 us (4%)
  local copies, waits for them, and re-layouts  1.79 us (2%)
    all_to_all x1, blocking collectives, local(): lax.all_to_all(jnp.broadcast_to(mine[None], (8, ROWS, HD)), ('yh', 'z1'),...  35.5 us
    pallas_call x1, Pallas kernels, attend(): pl.pallas_call(attend_kernel, out_shape=outs, grid_spec=pltpu.PrefetchSca...  15.5 us
    ppermute x5, starting transfers between devices, across(): return lax.ppermute(a, 'c', [(0, 1), (1, 0)])  14.3 us
    ppermute x4, starting transfers between devices, along_z(): lax.ppermute(a, ('z1', 'z0'), [(i, (i + by) % 16) for i in range(16)])  12.8 us
    all_to_all x1, starting transfers between devices, local(): parts = lax.all_to_all(terms, TP, 0, 0)  5.18 us
    all_to_all x1, waiting for transfers between devices, local(): parts = lax.all_to_all(terms, TP, 0, 0)  4.25 us
    eq x2, other arithmetic, local(): replicas == replica_of[d]  2.53 us
    pallas_call x1, Pallas kernels, pick(): pl.pallas_call(pick_kernel, out_shape=jax.ShapeDtypeStruct((ROWS, HD), jn...  2.06 us
  transfers between devices with their start and end apart: 10, of which 2 were waited for; matrix products, arithmetic and copies ran while one was open for 3% of the time, Pallas kernels for 0%

profile of v1, /device:TPU:49, one launch (start us, length us, event | category | flops | bytes accessed | tf_op | source)
XLA Modules:
  0.0 96.4 jit_solution(16707357150349282546)
XLA Ops:
  0.6 0.6 pad_add_fusion.meta
  1.3 2.1 %pick.1 = bf16[128,128]{1,0:T(8,128)(2,1)} custom-call(s32[4]{0:T(128)} %pad_add_fusion.meta, bf16[128,1024]{1,0:T(8,128)(2,1)} %keys.1, bf16[128,1024]{1,0:T(8,128)(2,1)} %values.1), custom_call_target="tpu_custom_call" | custom-call | tf_op jit(solution)/shard_map/pick/pallas_call | solution.py:32
  3.3 0.8 broadcast_in_dim.73
  4.1 35.5 %all_to_all.10.own0 = bf16[8,128,128]{2,1,0:T(8,128)(2,1)S(1)} all-to-all(bf16[8,128,128]{2,1,0:T(8,128)(2,1)S(1)} %broadcast_in_dim.73), channel_id=1, replica_groups=mesh['yh'=2,'z1'=4,'z0'=4,'x'=4,'yl'=2,'c'=2] {'yh','z1'}, dimensions={0} | all-to-all | bytes 524288 | tf_op jit(solution)/shard_map/all_to_all | solution.py:208
  39.6 2.0 %collective-permute-start = (bf16[8,128,128]{2,1,0:T(8,128)(2,1)S(1)}, bf16[8,128,128]{2,1,0:T(8,128)(2,1)S(1)}, u32[]{:S(2)}, u32[]{:S(2)}) collective-permute-start(bf16[8,128,128]{2,1,0:T(8,128)(2,1)S(1)} %all_to_all.10.own0), channel_id=1, source_target_pairs={{0,16},{16,32},{32,48},{48,64},{64,80},{80,96},{96,112},{112,128},... | collective-permute-start | bytes 786440 | tf_op jit(solution)/shard_map/ppermute | solution.py:203
  41.7 3.4 %collective-permute-start.1 = (bf16[8,128,128]{2,1,0:T(8,128)(2,1)S(1)}, bf16[8,128,128]{2,1,0:T(8,128)(2,1)S(1)}, u32[]{:S(2)}, u32[]{:S(2)}) collective-permute-start(bf16[8,128,128]{2,1,0:T(8,128)(2,1)S(1)} %all_to_all.10.own0), channel_id=1, source_target_pairs={{0,240},{16,0},{32,16},{48,32},{64,48},{80,64},{96,80},{112,96},{1... | collective-permute-start | bytes 786440 | tf_op jit(solution)/shard_map/ppermute | solution.py:203
  45.1 0.0 copy-start.2
  45.1 0.0 copy-start.4
  45.1 1.9 %collective-permute-start.2 = (bf16[4,128,128]{2,1,0:T(8,128)(2,1)S(1)}, bf16[4,128,128]{2,1,0:T(8,128)(2,1)S(1)}, u32[]{:S(2)}, u32[]{:S(2)}) collective-permute-start(bf16[4,128,128]{2,1,0:T(8,128)(2,1)S(1)} %get-tuple-element.17), channel_id=1, source_target_pairs={{0,32},{16,48},{32,64},{48,80},{64,96},{80,112},{96,128},{112,144}... | collective-permute-start | bytes 393224 | tf_op jit(solution)/shard_map/ppermute | solution.py:203
  47.1 5.5 %collective-permute-start.3 = (bf16[4,128,128]{2,1,0:T(8,128)(2,1)S(1)}, bf16[4,128,128]{2,1,0:T(8,128)(2,1)S(1)}, u32[]{:S(2)}, u32[]{:S(2)}) collective-permute-start(bf16[4,128,128]{2,1,0:T(8,128)(2,1)S(1)} %get-tuple-element.16), channel_id=1, source_target_pairs={{0,224},{16,240},{32,0},{48,16},{64,32},{80,48},{96,64},{112,80},{... | collective-permute-start | bytes 393224 | tf_op jit(solution)/shard_map/ppermute | solution.py:203
  52.6 5.6 %collective-permute-start.4 = (bf16[8,128,128]{2,1,0:T(8,128)(2,1)S(1)}, bf16[8,128,128]{2,1,0:T(8,128)(2,1)S(1)}, u32[]{:S(2)}, u32[]{:S(2)}) collective-permute-start(bf16[8,128,128]{2,1,0:T(8,128)(2,1)S(1)} %all_to_all.10.own0), channel_id=1, source_target_pairs={{0,1},{1,0},{2,3},{3,2},{4,5},{5,4},{6,7},{7,6},{8,9},{9,8},{10,11... | collective-permute-start | bytes 786440 | tf_op jit(solution)/shard_map/ppermute | solution.py:206
  58.2 1.9 %collective-permute-start.5 = (bf16[8,128,128]{2,1,0:T(8,128)(2,1)S(1)}, bf16[8,128,128]{2,1,0:T(8,128)(2,1)S(1)}, u32[]{:S(2)}, u32[]{:S(2)}) collective-permute-start(bf16[8,128,128]{2,1,0:T(8,128)(2,1)S(1)} %collective-permute-done.own1), channel_id=1, source_target_pairs={{0,1},{1,0},{2,3},{3,2},{4,5},{5,4},{6,7},{7,6},{8,9},{9,8},{10,11... | collective-permute-start | bytes 786440 | tf_op jit(solution)/shard_map/ppermute | solution.py:206
  60.1 2.4 %collective-permute-start.6 = (bf16[8,128,128]{2,1,0:T(8,128)(2,1)S(1)}, bf16[8,128,128]{2,1,0:T(8,128)(2,1)S(1)}, u32[]{:S(2)}, u32[]{:S(2)}) collective-permute-start(bf16[8,128,128]{2,1,0:T(8,128)(2,1)S(1)} %collective-permute-done.1.own2), channel_id=1, source_target_pairs={{0,1},{1,0},{2,3},{3,2},{4,5},{5,4},{6,7},{7,6},{8,9},{9,8},{10,11... | collective-permute-start | bytes 786440 | tf_op jit(solution)/shard_map/ppermute | solution.py:206
  62.6 1.9 %collective-permute-start.7 = (bf16[4,128,128]{2,1,0:T(8,128)(2,1)S(1)}, bf16[4,128,128]{2,1,0:T(8,128)(2,1)S(1)}, u32[]{:S(2)}, u32[]{:S(2)}) collective-permute-start(bf16[4,128,128]{2,1,0:T(8,128)(2,1)S(1)} %collective-permute-done.2.own3), channel_id=1, source_target_pairs={{0,1},{1,0},{2,3},{3,2},{4,5},{5,4},{6,7},{7,6},{8,9},{9,8},{10,11... | collective-permute-start | bytes 393224 | tf_op jit(solution)/shard_map/ppermute | solution.py:206
  64.5 2.4 %collective-permute-start.8 = (bf16[4,128,128]{2,1,0:T(8,128)(2,1)S(1)}, bf16[4,128,128]{2,1,0:T(8,128)(2,1)S(1)}, u32[]{:S(2)}, u32[]{:S(2)}) collective-permute-start(bf16[4,128,128]{2,1,0:T(8,128)(2,1)S(1)} %collective-permute-done.3.own4), channel_id=1, source_target_pairs={{0,1},{1,0},{2,3},{3,2},{4,5},{5,4},{6,7},{7,6},{8,9},{9,8},{10,11... | collective-permute-start | bytes 393224 | tf_op jit(solution)/shard_map/ppermute | solution.py:206
  66.9 0.7 fusion.1
  67.6 0.3 collective-permute-done.8.got4
  68.0 0.3 copy-done.7
  68.2 15.5 %attend.1 = (bf16[128,768]{1,0:T(8,128)(2,1)}, f32[16,8,384]{2,1,0:T(8,128)}, bf16[64,2560]{1,0:T(8,128)(2,1)}, bf16[64,2560]{1,0:T(8,128)(2,1)}) custom-call(s32[4]{0:T(128)S(1)} %copy-done.7, s32[4]{0:T(128)S(1)} %copy-done.3, s32[32,128]{1,0:T(8,128)S(1)} %bitcast.11, bf16[128,768]{1,0:T(8,128)(2,1)S(1)} %copy-done.1, bf16[4,768]{1,0:T(4,128)(2,1)S(1)} %copy-done.6, ...), custom_call_target="tpu_custom_call" | custom-call | tf_op jit(solution)/shard_map/attend/pallas_call | solution.py:174
  83.7 5.2 %all-to-all-start.1 = ((f32[16,8,384]{2,1,0:T(8,128)}), f32[16,8,384]{2,1,0:T(8,128)S(1)}, u32[]{:S(2)}, u32[]{:S(2)}) async-start(f32[16,8,384]{2,1,0:T(8,128)} %get-tuple-element.9), calls=%async_computation.1 | async-start | bytes 393216 | tf_op jit(solution)/shard_map/all_to_all | solution.py:214
  88.9 1.2 %iota_compare_fusion = (pred[32]{0:T(512)(128)(4,1)S(1)}, pred[32]{0:T(512)(128)(4,1)S(1)}) fusion(s32[]{:T(128)} %bitcast.8, s32[]{:T(128)} %bitcast.7), kind=kLoop, calls=%fused_computation.6 | loop fusion | flops 64 | bytes 72 | tf_op jit(solution)/shard_map/eq | solution.py:219
  90.1 1.3 %iota_compare_fusion.2 = (pred[32]{0:T(512)(128)(4,1)S(1)}, pred[32]{0:T(512)(128)(4,1)S(1)}) fusion(s32[]{:T(128)} %bitcast.6, s32[]{:T(128)} %bitcast.5), kind=kLoop, calls=%fused_computation.8 | loop fusion | flops 64 | bytes 72 | tf_op jit(solution)/shard_map/eq | solution.py:219
  91.4 4.2 %all-to-all-done.1 = f32[16,8,384]{2,1,0:T(8,128)S(1)} async-done(((f32[16,8,384]{2,1,0:T(8,128)}), f32[16,8,384]{2,1,0:T(8,128)S(1)}, u32[]{:S(2)}, u32[]{:S(2)}) %all-to-all-start.1) | async-done | bytes 196640 | tf_op jit(solution)/shard_map/all_to_all | solution.py:214
  95.7 0.7 select_convert_fusion
  (24 shorter events, 0.1 us)
Async XLA Ops:
  4.1 63.8 %copy-start = (bf16[768,384]{1,0:T(8,128)(2,1)S(1)}, bf16[768,384]{1,0:T(8,128)(2,1)}, u32[]{:S(2)}) copy-start(bf16[768,384]{1,0:T(8,128)(2,1)} %weight.1) | copy-start | bytes 1769476
  39.6 28.3 %copy-start.1 = (bf16[128,768]{1,0:T(8,128)(2,1)S(1)}, bf16[128,768]{1,0:T(8,128)(2,1)}, u32[]{:S(2)}) copy-start(bf16[128,768]{1,0:T(8,128)(2,1)} %queries.1) | copy-start | bytes 589828
  39.6 18.6 %collective-permute-start = (bf16[8,128,128]{2,1,0:T(8,128)(2,1)S(1)}, bf16[8,128,128]{2,1,0:T(8,128)(2,1)S(1)}, u32[]{:S(2)}, u32[]{:S(2)}) collective-permute-start(bf16[8,128,128]{2,1,0:T(8,128)(2,1)S(1)} %all_to_all.10.own0), channel_id=1, source_target_pairs={{0,16},{16,32},{32,48},{48,64},{64,80},{80,96},{96,112},{112,128},... | collective-permute-start | bytes 786440 | tf_op jit(solution)/shard_map/ppermute | solution.py:203
  41.7 18.4 %collective-permute-start.1 = (bf16[8,128,128]{2,1,0:T(8,128)(2,1)S(1)}, bf16[8,128,128]{2,1,0:T(8,128)(2,1)S(1)}, u32[]{:S(2)}, u32[]{:S(2)}) collective-permute-start(bf16[8,128,128]{2,1,0:T(8,128)(2,1)S(1)} %all_to_all.10.own0), channel_id=1, source_target_pairs={{0,240},{16,0},{32,16},{48,32},{64,48},{80,64},{96,80},{112,96},{1... | collective-permute-start | bytes 786440 | tf_op jit(solution)/shard_map/ppermute | solution.py:203
  45.1 22.9 %copy-start.2 = (s32[4096]{0:T(1024)S(1)}, s32[4096]{0:T(1024)}, u32[]{:S(2)}) copy-start(s32[4096]{0:T(1024)} %param.12) | copy-start | bytes 49156
  45.1 22.9 %copy-start.4 = (bf16[4,1024]{1,0:T(4,128)(2,1)S(1)}, bf16[4,1024]{1,0:T(4,128)(2,1)}, u32[]{:S(2)}) copy-start(bf16[4,1024]{1,0:T(4,128)(2,1)} %step_key.1) | copy-start | bytes 24580
  45.1 22.9 %copy-start.5 = (bf16[4,1024]{1,0:T(4,128)(2,1)S(1)}, bf16[4,1024]{1,0:T(4,128)(2,1)}, u32[]{:S(2)}) copy-start(bf16[4,1024]{1,0:T(4,128)(2,1)} %step_value.1) | copy-start | bytes 24580
  45.1 21.8 %copy-start.3 = (s32[4]{0:T(128)S(1)}, s32[4]{0:T(128)}, u32[]{:S(2)}) copy-start(s32[4]{0:T(128)} %replica_of.1) | copy-start | bytes 52
  45.1 22.8 %copy-start.6 = (bf16[4,768]{1,0:T(4,128)(2,1)S(1)}, bf16[4,768]{1,0:T(4,128)(2,1)}, u32[]{:S(2)}) copy-start(bf16[4,768]{1,0:T(4,128)(2,1)} %step_query.1) | copy-start | bytes 18436
  45.1 17.4 %collective-permute-start.2 = (bf16[4,128,128]{2,1,0:T(8,128)(2,1)S(1)}, bf16[4,128,128]{2,1,0:T(8,128)(2,1)S(1)}, u32[]{:S(2)}, u32[]{:S(2)}) collective-permute-start(bf16[4,128,128]{2,1,0:T(8,128)(2,1)S(1)} %get-tuple-element.17), channel_id=1, source_target_pairs={{0,32},{16,48},{32,64},{48,80},{64,96},{80,112},{96,128},{112,144}... | collective-permute-start | bytes 393224 | tf_op jit(solution)/shard_map/ppermute | solution.py:203
  47.1 17.4 %collective-permute-start.3 = (bf16[4,128,128]{2,1,0:T(8,128)(2,1)S(1)}, bf16[4,128,128]{2,1,0:T(8,128)(2,1)S(1)}, u32[]{:S(2)}, u32[]{:S(2)}) collective-permute-start(bf16[4,128,128]{2,1,0:T(8,128)(2,1)S(1)} %get-tuple-element.16), channel_id=1, source_target_pairs={{0,224},{16,240},{32,0},{48,16},{64,32},{80,48},{96,64},{112,80},{... | collective-permute-start | bytes 393224 | tf_op jit(solution)/shard_map/ppermute | solution.py:203
  52.6 15.3 %collective-permute-start.4 = (bf16[8,128,128]{2,1,0:T(8,128)(2,1)S(1)}, bf16[8,128,128]{2,1,0:T(8,128)(2,1)S(1)}, u32[]{:S(2)}, u32[]{:S(2)}) collective-permute-start(bf16[8,128,128]{2,1,0:T(8,128)(2,1)S(1)} %all_to_all.10.own0), channel_id=1, source_target_pairs={{0,1},{1,0},{2,3},{3,2},{4,5},{5,4},{6,7},{7,6},{8,9},{9,8},{10,11... | collective-permute-start | bytes 786440 | tf_op jit(solution)/shard_map/ppermute | solution.py:206
  58.2 9.7 %collective-permute-start.5 = (bf16[8,128,128]{2,1,0:T(8,128)(2,1)S(1)}, bf16[8,128,128]{2,1,0:T(8,128)(2,1)S(1)}, u32[]{:S(2)}, u32[]{:S(2)}) collective-permute-start(bf16[8,128,128]{2,1,0:T(8,128)(2,1)S(1)} %collective-permute-done.own1), channel_id=1, source_target_pairs={{0,1},{1,0},{2,3},{3,2},{4,5},{5,4},{6,7},{7,6},{8,9},{9,8},{10,11... | collective-permute-start | bytes 786440 | tf_op jit(solution)/shard_map/ppermute | solution.py:206
  60.1 7.8 %collective-permute-start.6 = (bf16[8,128,128]{2,1,0:T(8,128)(2,1)S(1)}, bf16[8,128,128]{2,1,0:T(8,128)(2,1)S(1)}, u32[]{:S(2)}, u32[]{:S(2)}) collective-permute-start(bf16[8,128,128]{2,1,0:T(8,128)(2,1)S(1)} %collective-permute-done.1.own2), channel_id=1, source_target_pairs={{0,1},{1,0},{2,3},{3,2},{4,5},{5,4},{6,7},{7,6},{8,9},{9,8},{10,11... | collective-permute-start | bytes 786440 | tf_op jit(solution)/shard_map/ppermute | solution.py:206
  62.6 5.0 %collective-permute-start.7 = (bf16[4,128,128]{2,1,0:T(8,128)(2,1)S(1)}, bf16[4,128,128]{2,1,0:T(8,128)(2,1)S(1)}, u32[]{:S(2)}, u32[]{:S(2)}) collective-permute-start(bf16[4,128,128]{2,1,0:T(8,128)(2,1)S(1)} %collective-permute-done.2.own3), channel_id=1, source_target_pairs={{0,1},{1,0},{2,3},{3,2},{4,5},{5,4},{6,7},{7,6},{8,9},{9,8},{10,11... | collective-permute-start | bytes 393224 | tf_op jit(solution)/shard_map/ppermute | solution.py:206
  64.5 3.4 %collective-permute-start.8 = (bf16[4,128,128]{2,1,0:T(8,128)(2,1)S(1)}, bf16[4,128,128]{2,1,0:T(8,128)(2,1)S(1)}, u32[]{:S(2)}, u32[]{:S(2)}) collective-permute-start(bf16[4,128,128]{2,1,0:T(8,128)(2,1)S(1)} %collective-permute-done.3.own4), channel_id=1, source_target_pairs={{0,1},{1,0},{2,3},{3,2},{4,5},{5,4},{6,7},{7,6},{8,9},{9,8},{10,11... | collective-permute-start | bytes 393224 | tf_op jit(solution)/shard_map/ppermute | solution.py:206
  67.6 0.6 copy-start.7
  83.7 12.0 %all-to-all-start.1 = ((f32[16,8,384]{2,1,0:T(8,128)}), f32[16,8,384]{2,1,0:T(8,128)S(1)}, u32[]{:S(2)}, u32[]{:S(2)}) async-start(f32[16,8,384]{2,1,0:T(8,128)} %get-tuple-element.9), calls=%async_computation.1 | async-start | bytes 393216 | tf_op jit(solution)/shard_map/all_to_all | solution.py:214

commit v2 on v1

v2 whole, which is shorter than its diff:
```python
import math

import jax
import jax.numpy as jnp
import numpy as np
from jax import lax
from jax.experimental import pallas as pl
from jax.experimental.pallas import tpu as pltpu
from jax.sharding import Mesh
from jax.sharding import PartitionSpec as P

H = 96
KVH = 8
HD = 128
NDOC = 4
ROWS = 128
NB = 32
MOST = 2560
HEADS = 6
SCALE = 1.0 / math.sqrt(HD)
CTX = ("yh", "z1", "z0")
TP = ("x", "yl", "c")
NEG = -1e30


def position():
    z0 = lax.axis_index("z0")
    ctx = lax.axis_index("yh") * 16 + lax.axis_index("z1") * 4 + z0
    return ctx, lax.axis_index("c"), lax.axis_index("x") * 2 + lax.axis_index("yl"), z0


def pick_kernel(keys, values, out, half, sem):
    _, core, head, _ = position()
    columns = pl.ds(pl.multiple_of(head * HD, HD), HD)
    for which, source in ((0, keys), (1, values)):

        @pl.when(core == which)
        def _():
            copy = pltpu.make_async_copy(source.at[:, columns], half, sem)
            copy.start()
            copy.wait()

    for g in range(8):
        out[g] = half[...]


def pick(keys, values):
    return pl.pallas_call(
        pick_kernel,
        out_shape=jax.ShapeDtypeStruct((8, ROWS, HD), jnp.bfloat16),
        in_specs=[pl.BlockSpec(memory_space=pltpu.HBM)] * 2,
        out_specs=pl.BlockSpec(memory_space=pltpu.VMEM),
        scratch_shapes=[pltpu.VMEM((ROWS, HD), jnp.bfloat16), pltpu.SemaphoreType.DMA],
        compiler_params=pltpu.CompilerParams(vmem_limit_bytes=60 * 1024 * 1024),
        name="pick",
    )(keys, values)


def doc_bounds(doc_ids):
    ids = doc_ids[...]
    starts = [jnp.int32(0)] + [jnp.sum((ids < d).astype(jnp.int32)) for d in range(1, NDOC)]
    return starts, starts[1:] + [jnp.int32(NB * ROWS)]


def decode_kernel(doc_ids, step_query, step_key, step_value, weight, far, near, across, other, terms, q48):
    _, core, head, z0 = position()
    columns = pl.ds(pl.multiple_of(head * HD, HD), HD)
    side = 1 - 2 * core
    starts, ends = doc_bounds(doc_ids)
    q48[...] = jnp.zeros_like(q48)
    steps = step_query[...].astype(jnp.float32)
    for h in range(HEADS):
        q48[h * 8 : h * 8 + NDOC, :] = steps[:, h * HD : (h + 1) * HD]
    q = q48[...]
    pad = jnp.zeros((8 - NDOC, HD), jnp.float32)
    own_key = jnp.concatenate([step_key[:, columns].astype(jnp.float32), pad] * HEADS, axis=0)
    own_value = jnp.concatenate([step_value[:, columns].astype(jnp.float32), pad] * HEADS, axis=0)
    doc_row = lax.broadcasted_iota(jnp.int32, (HEADS * 8, 1), 0) % 8
    low = jnp.full((HEADS * 8, 1), NB * ROWS, jnp.int32)
    high = jnp.zeros((HEADS * 8, 1), jnp.int32)
    for d in range(NDOC):
        low = jnp.where(doc_row == d, starts[d], low)
        high = jnp.where(doc_row == d, ends[d], high)
    narrow = q.astype(jnp.bfloat16)
    groups = (
        (far[0], far[1], 8, z0, 0),
        (near[0], near[1], 8, z0 + 4 + side, 0),
        (other[0, :8], other[1, :8], 8, z0 + 4 - side, 0),
        (across[0], across[1], 4, z0 + 2, core),
        (other[0, 8:], other[1, 8:], 4, z0 + 2, 1 - core),
    )
    nums, tops = [], []
    for keys, _, count, kind, first in groups:
        at = lax.broadcasted_iota(jnp.int32, (1, count * ROWS), 1)
        place = (at // (4 * ROWS) + first) * (16 * ROWS) + (at // ROWS % 4) * (4 * ROWS) + lax.rem(kind, 4) * ROWS + at % ROWS
        s = lax.dot_general(narrow, keys.reshape(count * ROWS, HD), (((1,), (1,)), ((), ())), preferred_element_type=jnp.float32)
        s = jnp.where((place >= low) & (place < high), s * SCALE, NEG)
        nums.append(s)
        tops.append(jnp.max(s, axis=1, keepdims=True))
    own_score = jnp.sum(q * own_key, axis=1, keepdims=True) * SCALE
    top = own_score
    for t in tops:
        top = jnp.maximum(top, t)
    own_prob = jnp.exp(own_score - top)
    total = own_prob
    mixed = own_prob.astype(jnp.bfloat16).astype(jnp.float32) * own_value
    for s, (_, values, count, _, _) in zip(nums, groups):
        p = jnp.exp(s - top)
        total = total + jnp.sum(p, axis=1, keepdims=True)
        mixed = mixed + jnp.dot(p.astype(jnp.bfloat16), values.reshape(count * ROWS, HD), preferred_element_type=jnp.float32)
    attended = mixed / total
    wide = jnp.concatenate([attended[h * 8 : (h + 1) * 8, :] for h in range(HEADS)], axis=1)
    term = jnp.dot(wide.astype(jnp.bfloat16), weight[...], preferred_element_type=jnp.float32)
    for k in range(16):
        terms[k] = term


def decode(doc_ids, step_query, step_key, step_value, weight, parts):
    return pl.pallas_call(
        decode_kernel,
        out_shape=jax.ShapeDtypeStruct((16, 8, weight.shape[1]), jnp.float32),
        scratch_shapes=[pltpu.VMEM((HEADS * 8, HD), jnp.float32)],
        compiler_params=pltpu.CompilerParams(vmem_limit_bytes=12 * 1024 * 1024),
        cost_estimate=pl.CostEstimate(flops=10**8, bytes_accessed=4 * 10**6, transcendentals=2 * 10**5),
        name="decode",
    )(doc_ids, step_query, step_key, step_value, weight, *parts)


STEP = 4


def prefill_kernel(
    replica_of, doc_ids, queries, far, near, across, other,
    context, replica_keys, replica_values,
    cache, flat, acc,
):
    ctx, core, _, z0 = position()
    side = 1 - 2 * core
    for which in range(2):
        for g in range(8):
            at = (g // 4) * 16 + (g % 4) * 4
            cache[which, at + z0] = far[which, g]
            cache[which, at + lax.rem(z0 + 4 + side, 4)] = near[which, g]
            cache[which, at + lax.rem(z0 + 4 - side, 4)] = other[which, g]
        for g in range(4):
            at = g * 4 + lax.rem(z0 + 2, 4)
            cache[which, at + core * 16] = across[which, g]
            cache[which, at + (1 - core) * 16] = other[which, 8 + g]
        for b in range(NB, NB + STEP - 1):
            cache[which, b] = jnp.zeros((ROWS, HD), jnp.bfloat16)
    starts, ends = doc_bounds(doc_ids)
    for h in range(HEADS):
        flat[h * ROWS : (h + 1) * ROWS, :] = queries[:, h * HD : (h + 1) * HD]

    row = ctx * ROWS + lax.broadcasted_iota(jnp.int32, (1, ROWS), 1)
    row_start = jnp.zeros((1, ROWS), jnp.int32)
    first = jnp.int32(0)
    for d in range(1, NDOC):
        row_start = jnp.where(row >= starts[d], starts[d], row_start)
        first = jnp.where(ctx * ROWS >= starts[d], starts[d], first)
    block0 = first // ROWS
    factor = SCALE * math.log2(math.e)
    acc[...] = jnp.zeros_like(acc)

    def step(i, carry):
        old, total = carry
        at = block0 + STEP * i
        key = cache[0, pl.ds(at, STEP)].reshape(STEP * ROWS, HD)
        value = cache[1, pl.ds(at, STEP)].reshape(STEP * ROWS, HD)
        place = at * ROWS + lax.broadcasted_iota(jnp.int32, (STEP * ROWS, ROWS), 0)
        bias = jnp.where((place <= row) & (place >= row_start), 0.0, NEG)
        s = lax.dot_general(key, flat[...], (((1,), (1,)), ((), ())), preferred_element_type=jnp.float32)
        s = s * factor + jnp.concatenate([bias] * HEADS, axis=1)
        new = jnp.maximum(old, jnp.max(s, axis=0, keepdims=True))
        p = jnp.exp2(s - new)
        alpha = jnp.exp2(old - new)
        total = total * alpha + jnp.sum(p, axis=0, keepdims=True)
        acc[...] = acc[...] * alpha + lax.dot_general(
            value, p.astype(jnp.bfloat16), (((0,), (0,)), ((), ())), preferred_element_type=jnp.float32
        )
        return new, total

    wide = (1, HEADS * ROWS)
    _, total = lax.fori_loop(
        0, (ctx - block0 + STEP) // STEP, step, (jnp.full(wide, NEG, jnp.float32), jnp.zeros(wide, jnp.float32))
    )
    mixed = acc[...] / total
    for h in range(HEADS):
        context[:, h * HD : (h + 1) * HD] = jnp.transpose(mixed[:, h * ROWS : (h + 1) * ROWS]).astype(jnp.bfloat16)

    asked = jnp.int32(0)
    start = jnp.int32(0)
    length = jnp.int32(0)
    for d in range(NDOC):
        mine = replica_of[d] == ctx
        asked = jnp.where(mine, 1, asked)
        start = jnp.where(mine, starts[d], start)
        length = jnp.where(mine, ends[d] - starts[d], length)

    @pl.when(asked == 0)
    def _():
        replica_keys[...] = jnp.zeros_like(replica_keys)
        replica_values[...] = jnp.zeros_like(replica_values)

    @pl.when(asked == 1)
    def _():
        offset = lax.rem(start, ROWS)
        begin = start // ROWS
        r = lax.broadcasted_iota(jnp.int32, (2 * ROWS, ROWS), 0)
        s = lax.broadcasted_iota(jnp.int32, (2 * ROWS, ROWS), 1)
        hot = (r == s + offset).astype(jnp.bfloat16)
        slot = lax.broadcasted_iota(jnp.int32, (HD // 2, ROWS), 1)
        for i in range(MOST // ROWS):
            at = jnp.minimum(begin + i, NB - 1)
            live = slot + i * ROWS < length
            for which, out in ((0, replica_keys), (1, replica_values)):
                source = cache[which, pl.ds(at, 2)].reshape(2 * ROWS, HD)
                moved = lax.dot_general(source, hot, (((0,), (0,)), ((), ())), preferred_element_type=jnp.float32)
                moved = jnp.where(core == 0, moved[: HD // 2], moved[HD // 2 :])
                out[:, i * ROWS : (i + 1) * ROWS] = jnp.where(live, moved, 0.0).astype(jnp.bfloat16)


def prefill(replica_of, doc_ids, queries, parts):
    vmem = pl.BlockSpec(memory_space=pltpu.VMEM)
    return pl.pallas_call(
        prefill_kernel,
        out_shape=(
            jax.ShapeDtypeStruct((ROWS, HEADS * HD), jnp.bfloat16),
            jax.ShapeDtypeStruct((HD // 2, MOST), jnp.bfloat16),
            jax.ShapeDtypeStruct((HD // 2, MOST), jnp.bfloat16),
        ),
        in_specs=[pl.BlockSpec(memory_space=pltpu.SMEM)] + [vmem] * 6,
        scratch_shapes=[
            pltpu.VMEM((2, NB + STEP - 1, ROWS, HD), jnp.bfloat16),
            pltpu.VMEM((HEADS * ROWS, HD), jnp.bfloat16),
            pltpu.VMEM((HD, HEADS * ROWS), jnp.float32),
        ],
        compiler_params=pltpu.CompilerParams(vmem_limit_bytes=16 * 1024 * 1024),
        cost_estimate=pl.CostEstimate(flops=2 * 10**9, bytes_accessed=4 * 10**6, transcendentals=2 * 10**6),
        name="prefill",
    )(replica_of, doc_ids, queries, *parts)


def finish_kernel(replica_of, summed, out):
    projected = jnp.sum(summed[...], axis=0)
    replica = lax.broadcasted_iota(jnp.int32, out.shape, 0)
    rows = jnp.zeros(out.shape, jnp.float32)
    for d in range(NDOC):
        rows = jnp.where(replica == replica_of[d], projected[d : d + 1], rows)
    out[...] = rows.astype(jnp.bfloat16)


def finish(replica_of, summed):
    return pl.pallas_call(
        finish_kernel,
        out_shape=jax.ShapeDtypeStruct((NB, summed.shape[2]), jnp.bfloat16),
        in_specs=[pl.BlockSpec(memory_space=pltpu.SMEM), pl.BlockSpec(memory_space=pltpu.VMEM)],
        compiler_params=pltpu.CompilerParams(vmem_limit_bytes=2 * 1024 * 1024),
        name="finish",
    )(replica_of, summed)


def from_sides(a, by):
    pairs = []
    for yh in range(2):
        for z in range(16):
            for t in range(16):
                core = t % 2
                source = (z + (by if core == 0 else -by)) % 16
                pairs.append(((yh * 16 + source) * 16 + t, (yh * 16 + z) * 16 + t))
    return lax.ppermute(a, CTX + TP, pairs)


def local(queries, keys, values, doc_ids, replica_of, step_query, step_key, step_value, out_weight):
    half = lax.all_to_all(pick(keys, values), ("yh", "z1"), 0, 0)
    far = lax.all_gather(half, "c", axis=0)
    near = from_sides(far, 1)
    across = from_sides(lax.dynamic_slice_in_dim(far, lax.axis_index("c") * 4, 4, 1), 2)
    both = jnp.concatenate(lax.optimization_barrier((near, across)), axis=1)
    other = lax.ppermute(both, "c", [(0, 1), (1, 0)])
    parts = [far, near, across, other]
    blocks = doc_ids.reshape(NB, ROWS)
    terms = decode(blocks, step_query, step_key, step_value, out_weight, parts)
    summed = lax.all_to_all(terms, TP, 0, 0)
    context, replica_keys, replica_values = prefill(replica_of, blocks, queries, parts)
    next_hidden = finish(replica_of, summed)
    return (context, next_hidden, replica_keys[None], replica_values[None])


def solution(mesh):
    fine = Mesh(np.asarray(mesh.devices).reshape(2, 4, 4, 4, 2, 2), CTX + TP)
    placed = (
        P(CTX, TP),
        P(CTX, None),
        P(CTX, None),
        P(),
        P(),
        P(None, TP),
        P(),
        P(),
        P(TP, CTX),
    )
    return jax.shard_map(
        local,
        mesh=fine,
        in_specs=placed,
        out_specs=(P(CTX, TP), P(None, CTX), P(CTX, TP, None), P(CTX, TP, None)),
        check_vma=False,
    )
```

time: 97.1 us -> 82.8 us (0.85)
  the two profiles are of different devices: /device:TPU:49 before, /device:TPU:1 now
where the time goes in v2:
time: 82.8 us; the launch traced here: 82.4 us
  blocking collectives  40.5 us (49%)
  starting transfers between devices  18.7 us (23%)
  waiting for transfers between devices  15.1 us (18%)
  Pallas kernels  7.17 us (9%)
    all_to_all x1, blocking collectives, local(): half = lax.all_to_all(pick(keys, values), ('yh', 'z1'), 0, 0)  33.2 us
    ppermute x2, starting transfers between devices, from_sides(): return lax.ppermute(a, CTX + TP, pairs)  9.11 us
    ppermute x2, waiting for transfers between devices, from_sides(): return lax.ppermute(a, CTX + TP, pairs)  9.09 us
    all_gather x1, blocking collectives, local(): far = lax.all_gather(half, 'c', axis=0)  7.29 us
    all_to_all x1, starting transfers between devices, local(): summed = lax.all_to_all(terms, TP, 0, 0)  4.94 us
    ppermute x1, starting transfers between devices, local(): other = lax.ppermute(both, 'c', [(0, 1), (1, 0)])  4.66 us
    all_to_all x1, waiting for transfers between devices, local(): summed = lax.all_to_all(terms, TP, 0, 0)  4.12 us
    pallas_call x1, Pallas kernels, prefill(): pl.pallas_call(prefill_kernel, out_shape=(jax.ShapeDtypeStruct((ROWS, HEA...  2.65 us
  transfers between devices with their start and end apart: 4, of which 3 were waited for; matrix products, arithmetic and copies ran while one was open for 0% of the time, Pallas kernels for 3%

profile of v2, /device:TPU:1, one launch (start us, length us, event | category | flops | bytes accessed | tf_op | source)
XLA Modules:
  0.0 82.4 jit_solution(9729029555140496003)
XLA Ops:
  0.6 1.5 %pick.1 = bf16[8,128,128]{2,1,0:T(8,128)(2,1)} custom-call(bf16[128,1024]{1,0:T(8,128)(2,1)} %keys.1, bf16[128,1024]{1,0:T(8,128)(2,1)} %values.1), custom_call_target="tpu_custom_call" | custom-call | tf_op jit(solution)/shard_map/pick/pallas_call | solution.py:48
  2.2 33.2 %all_to_all.10 = bf16[8,128,128]{2,1,0:T(8,128)(2,1)S(1)} all-to-all(bf16[8,128,128]{2,1,0:T(8,128)(2,1)} %pick.1), channel_id=1, replica_groups=mesh['yh'=2,'z1'=4,'z0'=4,'x'=4,'yl'=2,'c'=2] {'yh','z1'}, dimensions={0} | all-to-all | bytes 524288 | tf_op jit(solution)/shard_map/all_to_all | solution.py:275
  35.4 7.3 %all-gather = bf16[16,128,128]{2,1,0:T(8,128)(2,1)S(1)} all-gather(bf16[8,128,128]{2,1,0:T(8,128)(2,1)S(1)} %all_to_all.10), channel_id=2, replica_groups=mesh['yh'=2,'z1'=4,'z0'=4,'x'=4,'yl'=2,'c'=2] {'c'}, dimensions={0}, use_global_device_ids=true | all-gather | bytes 786432 | tf_op jit(solution)/shard_map/all_gather | solution.py:276
  42.7 6.5 %collective-permute-start = (bf16[2,8,128,128]{3,2,1,0:T(8,128)(2,1)S(1)}, bf16[2,8,128,128]{3,2,1,0:T(8,128)(2,1)S(1)}, u32[]{:S(2)}, u32[]{:S(2)}) collective-permute-start(bf16[2,8,128,128]{3,2,1,0:T(8,128)(2,1)S(1)} %bitcast.4), channel_id=1, source_target_pairs={{16,0},{241,1},{18,2},{243,3},{20,4},{245,5},{22,6},{247,7},{24,8}... | collective-permute-start | bytes 1572872 | tf_op jit(solution)/shard_map/ppermute | solution.py:271
  49.2 0.0 copy-start
  49.3 0.0 copy-start.1
  49.3 0.0 copy-start.2
  49.3 0.0 copy-start.3
  49.3 2.6 %collective-permute-start.1 = (bf16[2,4,128,128]{3,2,1,0:T(8,128)(2,1)S(1)}, bf16[2,4,128,128]{3,2,1,0:T(8,128)(2,1)S(1)}, u32[]{:S(2)}, u32[]{:S(2)}) collective-permute-start(bf16[2,4,128,128]{3,2,1,0:T(8,128)(2,1)S(1)} %constant_dynamic-slice_fusion), channel_id=1, source_target_pairs={{32,0},{225,1},{34,2},{227,3},{36,4},{229,5},{38,6},{231,7},{40,8}... | collective-permute-start | bytes 786440 | tf_op jit(solution)/shard_map/ppermute | solution.py:271
  51.9 9.1 %collective-permute-done.1.across = bf16[2,4,128,128]{3,2,1,0:T(8,128)(2,1)S(1)} collective-permute-done((bf16[2,4,128,128]{3,2,1,0:T(8,128)(2,1)S(1)}, bf16[2,4,128,128]{3,2,1,0:T(8,128)(2,1)S(1)}, u32[]{:S(2)}, u32[]{:S(2)}) %collective-permute-start.1) | collective-permute-done | bytes 262176 | tf_op jit(solution)/shard_map/ppermute | solution.py:271
  61.0 0.0 collective-permute-done.near
  61.0 0.1 pad_maximum_fusion
  61.0 4.7 %collective-permute-start.2 = (bf16[2,12,128,128]{3,2,1,0:T(8,128)(2,1)S(1)}, bf16[2,12,128,128]{3,2,1,0:T(8,128)(2,1)S(1)}, u32[]{:S(2)}, u32[]{:S(2)}) collective-permute-start(bf16[2,12,128,128]{3,2,1,0:T(8,128)(2,1)S(1)} %pad_maximum_fusion), channel_id=1, source_target_pairs={{0,1},{1,0},{2,3},{3,2},{4,5},{5,4},{6,7},{7,6},{8,9},{9,8},{10,11... | collective-permute-start | bytes 2359304 | tf_op jit(solution)/shard_map/ppermute | solution.py:280
  65.7 1.9 %collective-permute-done.2.other = bf16[2,12,128,128]{3,2,1,0:T(8,128)(2,1)S(1)} collective-permute-done((bf16[2,12,128,128]{3,2,1,0:T(8,128)(2,1)S(1)}, bf16[2,12,128,128]{3,2,1,0:T(8,128)(2,1)S(1)}, u32[]{:S(2)}, u32[]{:S(2)}) %collective-permute-start.2) | collective-permute-done | bytes 786464 | tf_op jit(solution)/shard_map/ppermute | solution.py:280
  67.6 0.0 copy-done
  67.6 0.0 copy-done.1
  67.6 0.0 copy-done.2
  67.6 0.0 copy-done.3
  67.6 0.0 copy-done.4
  67.6 1.8 %decode.1 = f32[16,8,384]{2,1,0:T(8,128)} custom-call(s32[32,128]{1,0:T(8,128)S(1)} %bitcast.8, bf16[4,768]{1,0:T(4,128)(2,1)S(1)} %copy-done.4, bf16[4,1024]{1,0:T(4,128)(2,1)S(1)} %copy-done.2, bf16[4,1024]{1,0:T(4,128)(2,1)S(1)} %copy-done.3, bf16[768,384]{1,0:T(8,128)(2,1)S(1)} %copy-done, bf16[2,8,128,128]{3,2,1,0:T(8,128)(2,1)S(1)} %bitcast.6, ...), custom_call_target="tpu_custom_call" | custom-call | flops 100000000 | bytes 4000000 | tf_op jit(solution)/shard_map/decode/pallas_call | solution.py:119
  69.5 4.9 %all-to-all-start.1 = ((f32[16,8,384]{2,1,0:T(8,128)}), f32[16,8,384]{2,1,0:T(8,128)S(1)}, u32[]{:S(2)}, u32[]{:S(2)}) async-start(f32[16,8,384]{2,1,0:T(8,128)} %decode.1), calls=%async_computation.1 | async-start | bytes 393216 | tf_op jit(solution)/shard_map/all_to_all | solution.py:284
  74.4 2.6 %prefill.1 = (bf16[128,768]{1,0:T(8,128)(2,1)}, bf16[64,2560]{1,0:T(8,128)(2,1)}, bf16[64,2560]{1,0:T(8,128)(2,1)}) custom-call(s32[4]{0:T(128)S(1)} %copy-done.5, s32[32,128]{1,0:T(8,128)S(1)} %bitcast.9, bf16[128,768]{1,0:T(8,128)(2,1)S(1)} %copy-done.6, bf16[2,8,128,128]{3,2,1,0:T(8,128)(2,1)S(1)} %bitcast.7, ...), custom_call_target="tpu_custom_call" | custom-call | flops 2000000000 | bytes 4000000 | tf_op jit(solution)/shard_map/prefill/pallas_call | solution.py:225
  77.1 4.1 %all-to-all-done.1.summed = f32[16,8,384]{2,1,0:T(8,128)S(1)} async-done(((f32[16,8,384]{2,1,0:T(8,128)}), f32[16,8,384]{2,1,0:T(8,128)S(1)}, u32[]{:S(2)}, u32[]{:S(2)}) %all-to-all-start.1) | async-done | bytes 196640 | tf_op jit(solution)/shard_map/all_to_all | solution.py:284
  81.2 1.2 %finish.1 = bf16[32,384]{1,0:T(8,128)(2,1)} custom-call(s32[4]{0:T(128)S(1)} %copy-done.5, f32[16,8,384]{2,1,0:T(8,128)S(1)} %all-to-all-done.1.summed), custom_call_target="tpu_custom_call" | custom-call | tf_op jit(solution)/shard_map/finish/pallas_call | solution.py:254
  (6 shorter events, 0.0 us)
Async XLA Ops:
  42.7 18.3 %collective-permute-start = (bf16[2,8,128,128]{3,2,1,0:T(8,128)(2,1)S(1)}, bf16[2,8,128,128]{3,2,1,0:T(8,128)(2,1)S(1)}, u32[]{:S(2)}, u32[]{:S(2)}) collective-permute-start(bf16[2,8,128,128]{3,2,1,0:T(8,128)(2,1)S(1)} %bitcast.4), channel_id=1, source_target_pairs={{16,0},{241,1},{18,2},{243,3},{20,4},{245,5},{22,6},{247,7},{24,8}... | collective-permute-start | bytes 1572872 | tf_op jit(solution)/shard_map/ppermute | solution.py:271
  49.2 18.4 %copy-start = (bf16[768,384]{1,0:T(8,128)(2,1)S(1)}, bf16[768,384]{1,0:T(8,128)(2,1)}, u32[]{:S(2)}) copy-start(bf16[768,384]{1,0:T(8,128)(2,1)} %weight.1) | copy-start | bytes 1769476
  49.3 18.4 %copy-start.1 = (s32[4096]{0:T(1024)S(1)}, s32[4096]{0:T(1024)}, u32[]{:S(2)}) copy-start(s32[4096]{0:T(1024)} %param.12) | copy-start | bytes 49156
  49.3 18.4 %copy-start.2 = (bf16[4,1024]{1,0:T(4,128)(2,1)S(1)}, bf16[4,1024]{1,0:T(4,128)(2,1)}, u32[]{:S(2)}) copy-start(bf16[4,1024]{1,0:T(4,128)(2,1)} %step_key.1) | copy-start | bytes 24580
  49.3 18.3 %copy-start.3 = (bf16[4,1024]{1,0:T(4,128)(2,1)S(1)}, bf16[4,1024]{1,0:T(4,128)(2,1)}, u32[]{:S(2)}) copy-start(bf16[4,1024]{1,0:T(4,128)(2,1)} %step_value.1) | copy-start | bytes 24580
  49.3 11.7 %collective-permute-start.1 = (bf16[2,4,128,128]{3,2,1,0:T(8,128)(2,1)S(1)}, bf16[2,4,128,128]{3,2,1,0:T(8,128)(2,1)S(1)}, u32[]{:S(2)}, u32[]{:S(2)}) collective-permute-start(bf16[2,4,128,128]{3,2,1,0:T(8,128)(2,1)S(1)} %constant_dynamic-slice_fusion), channel_id=1, source_target_pairs={{32,0},{225,1},{34,2},{227,3},{36,4},{229,5},{38,6},{231,7},{40,8}... | collective-permute-start | bytes 786440 | tf_op jit(solution)/shard_map/ppermute | solution.py:271
  61.0 6.6 %copy-start.4 = (bf16[4,768]{1,0:T(4,128)(2,1)S(1)}, bf16[4,768]{1,0:T(4,128)(2,1)}, u32[]{:S(2)}) copy-start(bf16[4,768]{1,0:T(4,128)(2,1)} %step_query.1) | copy-start | bytes 18436
  61.0 6.6 %collective-permute-start.2 = (bf16[2,12,128,128]{3,2,1,0:T(8,128)(2,1)S(1)}, bf16[2,12,128,128]{3,2,1,0:T(8,128)(2,1)S(1)}, u32[]{:S(2)}, u32[]{:S(2)}) collective-permute-start(bf16[2,12,128,128]{3,2,1,0:T(8,128)(2,1)S(1)} %pad_maximum_fusion), channel_id=1, source_target_pairs={{0,1},{1,0},{2,3},{3,2},{4,5},{5,4},{6,7},{7,6},{8,9},{9,8},{10,11... | collective-permute-start | bytes 2359304 | tf_op jit(solution)/shard_map/ppermute | solution.py:280
  69.5 4.9 %copy-start.5 = (s32[4]{0:T(128)S(1)}, s32[4]{0:T(128)}, u32[]{:S(2)}) copy-start(s32[4]{0:T(128)} %replica_of.3) | copy-start | bytes 52
  69.5 4.9 %copy-start.6 = (bf16[128,768]{1,0:T(8,128)(2,1)S(1)}, bf16[128,768]{1,0:T(8,128)(2,1)}, u32[]{:S(2)}) copy-start(bf16[128,768]{1,0:T(8,128)(2,1)} %queries.1) | copy-start | bytes 589828
  69.5 11.7 %all-to-all-start.1 = ((f32[16,8,384]{2,1,0:T(8,128)}), f32[16,8,384]{2,1,0:T(8,128)S(1)}, u32[]{:S(2)}, u32[]{:S(2)}) async-start(f32[16,8,384]{2,1,0:T(8,128)} %decode.1), calls=%async_computation.1 | async-start | bytes 393216 | tf_op jit(solution)/shard_map/all_to_all | solution.py:284

commit v3 on v2

--- a/solution.py
+++ b/solution.py
@@ -40,14 +40,14 @@
             copy.start()
             copy.wait()
 
-    for g in range(8):
+    for g in range(out.shape[0]):
         out[g] = half[...]
 
 
-def pick(keys, values):
+def pick(keys, values, copies):
     return pl.pallas_call(
         pick_kernel,
-        out_shape=jax.ShapeDtypeStruct((8, ROWS, HD), jnp.bfloat16),
+        out_shape=jax.ShapeDtypeStruct((copies, ROWS, HD), jnp.bfloat16),
         in_specs=[pl.BlockSpec(memory_space=pltpu.HBM)] * 2,
         out_specs=pl.BlockSpec(memory_space=pltpu.VMEM),
         scratch_shapes=[pltpu.VMEM((ROWS, HD), jnp.bfloat16), pltpu.SemaphoreType.DMA],
@@ -62,55 +62,63 @@
     return starts, starts[1:] + [jnp.int32(NB * ROWS)]
 
 
-def decode_kernel(doc_ids, step_query, step_key, step_value, weight, far, near, across, other, terms, q48):
+ROW = HEADS * NDOC
+PAD = 32
+
+
+def decode_kernel(
+    doc_ids, step_query, step_key, step_value, weight, far, near, across, other, terms, query, own_key, own_value
+):
     _, core, head, z0 = position()
     columns = pl.ds(pl.multiple_of(head * HD, HD), HD)
     side = 1 - 2 * core
     starts, ends = doc_bounds(doc_ids)
-    q48[...] = jnp.zeros_like(q48)
     steps = step_query[...].astype(jnp.float32)
+    step_keys = step_key[:, columns].astype(jnp.float32)
+    step_values = step_value[:, columns].astype(jnp.float32)
+    for ref in (query, own_key, own_value):
+        ref[ROW:PAD, :] = jnp.zeros((PAD - ROW, HD), jnp.float32)
     for h in range(HEADS):
-        q48[h * 8 : h * 8 + NDOC, :] = steps[:, h * HD : (h + 1) * HD]
-    q = q48[...]
-    pad = jnp.zeros((8 - NDOC, HD), jnp.float32)
-    own_key = jnp.concatenate([step_key[:, columns].astype(jnp.float32), pad] * HEADS, axis=0)
-    own_value = jnp.concatenate([step_value[:, columns].astype(jnp.float32), pad] * HEADS, axis=0)
-    doc_row = lax.broadcasted_iota(jnp.int32, (HEADS * 8, 1), 0) % 8
-    low = jnp.full((HEADS * 8, 1), NB * ROWS, jnp.int32)
-    high = jnp.zeros((HEADS * 8, 1), jnp.int32)
+        rows = slice(h * NDOC, (h + 1) * NDOC)
+        query[rows, :] = steps[:, h * HD : (h + 1) * HD]
+        own_key[rows, :] = step_keys
+        own_value[rows, :] = step_values
+    q = query[...]
+    document = lax.broadcasted_iota(jnp.int32, (PAD, 1), 0) % NDOC
+    low = jnp.zeros((PAD, 1), jnp.int32)
+    high = jnp.zeros((PAD, 1), jnp.int32)
     for d in range(NDOC):
-        low = jnp.where(doc_row == d, starts[d], low)
-        high = jnp.where(doc_row == d, ends[d], high)
+        low = jnp.where(document == d, starts[d], low)
+        high = jnp.where(document == d, ends[d], high)
     narrow = q.astype(jnp.bfloat16)
-    groups = (
-        (far[0], far[1], 8, z0, 0),
-        (near[0], near[1], 8, z0 + 4 + side, 0),
-        (other[0, :8], other[1, :8], 8, z0 + 4 - side, 0),
-        (across[0], across[1], 4, z0 + 2, core),
-        (other[0, 8:], other[1, 8:], 4, z0 + 2, 1 - core),
-    )
+    groups = [(far, 0, z0, 0), (far, 1, z0, 1), (near, 0, z0 + 4 + side, 0), (near, 1, z0 + 4 + side, 1)]
+    groups += [(other, 0, z0 + 4 - side, 0), (other, 1, z0 + 4 - side, 1), (across, 0, z0 + 2, core), (other, 2, z0 + 2, 1 - core)]
+    at = lax.broadcasted_iota(jnp.int32, (1, 4 * ROWS), 1)
+    at = at // ROWS * (4 * ROWS) + at % ROWS
     nums, tops = [], []
-    for keys, _, count, kind, first in groups:
-        at = lax.broadcasted_iota(jnp.int32, (1, count * ROWS), 1)
-        place = (at // (4 * ROWS) + first) * (16 * ROWS) + (at // ROWS % 4) * (4 * ROWS) + lax.rem(kind, 4) * ROWS + at % ROWS
-        s = lax.dot_general(narrow, keys.reshape(count * ROWS, HD), (((1,), (1,)), ((), ())), preferred_element_type=jnp.float32)
+    for ref, index, kind, yh in groups:
+        place = at + (yh * (16 * ROWS) + lax.rem(kind, 4) * ROWS)
+        keys = ref[index, 0].reshape(4 * ROWS, HD)
+        s = lax.dot_general(narrow, keys, (((1,), (1,)), ((), ())), preferred_element_type=jnp.float32)
         s = jnp.where((place >= low) & (place < high), s * SCALE, NEG)
         nums.append(s)
         tops.append(jnp.max(s, axis=1, keepdims=True))
-    own_score = jnp.sum(q * own_key, axis=1, keepdims=True) * SCALE
+    own_score = jnp.sum(q * own_key[...], axis=1, keepdims=True) * SCALE
     top = own_score
     for t in tops:
         top = jnp.maximum(top, t)
     own_prob = jnp.exp(own_score - top)
     total = own_prob
-    mixed = own_prob.astype(jnp.bfloat16).astype(jnp.float32) * own_value
-    for s, (_, values, count, _, _) in zip(nums, groups):
+    mixed = own_prob.astype(jnp.bfloat16).astype(jnp.float32) * own_value[...]
+    for s, (ref, index, _, _) in zip(nums, groups):
         p = jnp.exp(s - top)
         total = total + jnp.sum(p, axis=1, keepdims=True)
-        mixed = mixed + jnp.dot(p.astype(jnp.bfloat16), values.reshape(count * ROWS, HD), preferred_element_type=jnp.float32)
-    attended = mixed / total
-    wide = jnp.concatenate([attended[h * 8 : (h + 1) * 8, :] for h in range(HEADS)], axis=1)
-    term = jnp.dot(wide.astype(jnp.bfloat16), weight[...], preferred_element_type=jnp.float32)
+        values = ref[index, 1].reshape(4 * ROWS, HD)
+        mixed = mixed + jnp.dot(p.astype(jnp.bfloat16), values, preferred_element_type=jnp.float32)
+    query[...] = mixed / total
+    wide = jnp.concatenate([query[h * NDOC : (h + 1) * NDOC, :] for h in range(HEADS)], axis=1)
+    wide = jnp.concatenate([wide, jnp.zeros_like(wide)], axis=0)
+    term = jnp.dot(wide.astype(jnp.bfloat16), weight[...], preferred_element_type=jnp.float32).astype(terms.dtype)
     for k in range(16):
         terms[k] = term
 
@@ -118,8 +126,8 @@
 def decode(doc_ids, step_query, step_key, step_value, weight, parts):
     return pl.pallas_call(
         decode_kernel,
-        out_shape=jax.ShapeDtypeStruct((16, 8, weight.shape[1]), jnp.float32),
-        scratch_shapes=[pltpu.VMEM((HEADS * 8, HD), jnp.float32)],
+        out_shape=jax.ShapeDtypeStruct((16, 8, weight.shape[1]), jnp.bfloat16),
+        scratch_shapes=[pltpu.VMEM((PAD, HD), jnp.float32)] * 3,
         compiler_params=pltpu.CompilerParams(vmem_limit_bytes=12 * 1024 * 1024),
         cost_estimate=pl.CostEstimate(flops=10**8, bytes_accessed=4 * 10**6, transcendentals=2 * 10**5),
         name="decode",
@@ -137,15 +145,15 @@
     ctx, core, _, z0 = position()
     side = 1 - 2 * core
     for which in range(2):
-        for g in range(8):
-            at = (g // 4) * 16 + (g % 4) * 4
-            cache[which, at + z0] = far[which, g]
-            cache[which, at + lax.rem(z0 + 4 + side, 4)] = near[which, g]
-            cache[which, at + lax.rem(z0 + 4 - side, 4)] = other[which, g]
         for g in range(4):
+            for yh in range(2):
+                at = yh * 16 + g * 4
+                cache[which, at + z0] = far[yh, which, g]
+                cache[which, at + lax.rem(z0 + 4 + side, 4)] = near[yh, which, g]
+                cache[which, at + lax.rem(z0 + 4 - side, 4)] = other[yh, which, g]
             at = g * 4 + lax.rem(z0 + 2, 4)
-            cache[which, at + core * 16] = across[which, g]
-            cache[which, at + (1 - core) * 16] = other[which, 8 + g]
+            cache[which, at + core * 16] = across[0, which, g]
+            cache[which, at + (1 - core) * 16] = other[2, which, g]
         for b in range(NB, NB + STEP - 1):
             cache[which, b] = jnp.zeros((ROWS, HD), jnp.bfloat16)
     starts, ends = doc_bounds(doc_ids)
@@ -241,25 +249,6 @@
     )(replica_of, doc_ids, queries, *parts)
 
 
-def finish_kernel(replica_of, summed, out):
-    projected = jnp.sum(summed[...], axis=0)
-    replica = lax.broadcasted_iota(jnp.int32, out.shape, 0)
-    rows = jnp.zeros(out.shape, jnp.float32)
-    for d in range(NDOC):
-        rows = jnp.where(replica == replica_of[d], projected[d : d + 1], rows)
-    out[...] = rows.astype(jnp.bfloat16)
-
-
-def finish(replica_of, summed):
-    return pl.pallas_call(
-        finish_kernel,
-        out_shape=jax.ShapeDtypeStruct((NB, summed.shape[2]), jnp.bfloat16),
-        in_specs=[pl.BlockSpec(memory_space=pltpu.SMEM), pl.BlockSpec(memory_space=pltpu.VMEM)],
-        compiler_params=pltpu.CompilerParams(vmem_limit_bytes=2 * 1024 * 1024),
-        name="finish",
-    )(replica_of, summed)
-
-
 def from_sides(a, by):
     pairs = []
     for yh in range(2):
@@ -272,18 +261,20 @@
 
 
 def local(queries, keys, values, doc_ids, replica_of, step_query, step_key, step_value, out_weight):
-    half = lax.all_to_all(pick(keys, values), ("yh", "z1"), 0, 0)
-    far = lax.all_gather(half, "c", axis=0)
+    half = lax.all_to_all(pick(keys, values, 4), "z1", 0, 0)
+    far = lax.all_gather(half, ("yh", "c"), axis=0).reshape(2, 2, 4, ROWS, HD)
     near = from_sides(far, 1)
-    across = from_sides(lax.dynamic_slice_in_dim(far, lax.axis_index("c") * 4, 4, 1), 2)
-    both = jnp.concatenate(lax.optimization_barrier((near, across)), axis=1)
+    across = from_sides(lax.dynamic_slice_in_dim(far, lax.axis_index("c"), 1, 0), 2)
+    both = jnp.concatenate(lax.optimization_barrier((near, across)), axis=0)
     other = lax.ppermute(both, "c", [(0, 1), (1, 0)])
     parts = [far, near, across, other]
     blocks = doc_ids.reshape(NB, ROWS)
     terms = decode(blocks, step_query, step_key, step_value, out_weight, parts)
     summed = lax.all_to_all(terms, TP, 0, 0)
     context, replica_keys, replica_values = prefill(replica_of, blocks, queries, parts)
-    next_hidden = finish(replica_of, summed)
+    hot = (replica_of[None, :] == jnp.arange(NB, dtype=jnp.int32)[:, None]).astype(jnp.float32)
+    projected = jnp.sum(summed.astype(jnp.float32), axis=0)
+    next_hidden = jnp.sum(hot[:, :, None] * projected[None, :NDOC], axis=1).astype(jnp.bfloat16)
     return (context, next_hidden, replica_keys[None], replica_values[None])
 
 

time: 82.8 us -> 76.9 us (0.929)
  starting transfers between devices: 18.7 us -> 16 us
  waiting for transfers between devices: 15.1 us -> 13.2 us
  Pallas kernels: 7.17 us -> 5.82 us
    all_to_all x1, blocking collectives: 33.2 us -> 28.3 us  [local(): half = lax.all_to_all(pick(keys, values, 4), 'z1', 0, 0)]
    all_gather x1, blocking collectives: 7.29 us -> 11.4 us  [local(): far = lax.all_gather(half, ('yh', 'c'), axis=0).reshape(2, 2, 4, ROWS, HD)]
    ppermute x2, starting transfers between devices: 9.11 us -> 5.85 us  [from_sides(): return lax.ppermute(a, CTX + TP, pairs)]
    pallas_call x2 -> x1, Pallas kernels: 2.69 us -> 1.45 us  [pick(): pl.pallas_call(pick_kernel, out_shape=jax.ShapeDtypeStruct((copies, ROWS,...]
    ppermute x2, waiting for transfers between devices: 9.09 us -> 8.13 us  [from_sides(): return lax.ppermute(a, CTX + TP, pairs)]
    all_to_all x1, waiting for transfers between devices: 4.12 us -> 3.25 us  [local(): summed = lax.all_to_all(terms, TP, 0, 0)]
  transfers between devices with their start and end apart: 4 -> 4, of which waited for: 3 -> 4; matrix products, arithmetic and copies ran while one was open for 0% -> 0% of each run, Pallas kernels for 3% -> 3%
where the time goes in v3:
time: 76.9 us; the launch traced here: 76.5 us
  blocking collectives  39.7 us (52%)
  starting transfers between devices  16 us (21%)
  waiting for transfers between devices  13.2 us (17%)
  Pallas kernels  5.82 us (8%)
  other arithmetic  0.86 us (1%)
    all_to_all x1, blocking collectives, local(): half = lax.all_to_all(pick(keys, values, 4), 'z1', 0, 0)  28.3 us
    all_gather x1, blocking collectives, local(): far = lax.all_gather(half, ('yh', 'c'), axis=0).reshape(2, 2, 4, ROWS, HD)  11.4 us
    ppermute x2, waiting for transfers between devices, from_sides(): return lax.ppermute(a, CTX + TP, pairs)  8.13 us
    ppermute x2, starting transfers between devices, from_sides(): return lax.ppermute(a, CTX + TP, pairs)  5.85 us
    ppermute x1, starting transfers between devices, local(): other = lax.ppermute(both, 'c', [(0, 1), (1, 0)])  5.21 us
    all_to_all x1, starting transfers between devices, local(): summed = lax.all_to_all(terms, TP, 0, 0)  4.98 us
    all_to_all x1, waiting for transfers between devices, local(): summed = lax.all_to_all(terms, TP, 0, 0)  3.25 us
    pallas_call x1, Pallas kernels, prefill(): pl.pallas_call(prefill_kernel, out_shape=(jax.ShapeDtypeStruct((ROWS, HEA...  2.66 us
  transfers between devices with their start and end apart: 4, of which 4 were waited for; matrix products, arithmetic and copies ran while one was open for 0% of the time, Pallas kernels for 3%

profile of v3, /device:TPU:1, one launch (start us, length us, event | category | flops | bytes accessed | tf_op | source)
XLA Modules:
  0.0 76.5 jit_solution(1249874523142507148)
XLA Ops:
  0.6 1.5 %pick.1 = bf16[4,128,128]{2,1,0:T(8,128)(2,1)} custom-call(bf16[128,1024]{1,0:T(8,128)(2,1)} %keys.1, bf16[128,1024]{1,0:T(8,128)(2,1)} %values.1), custom_call_target="tpu_custom_call" | custom-call | tf_op jit(solution)/shard_map/pick/pallas_call | solution.py:48
  2.1 28.3 %all_to_all.10 = bf16[4,128,128]{2,1,0:T(8,128)(2,1)S(1)} all-to-all(bf16[4,128,128]{2,1,0:T(8,128)(2,1)} %pick.1), channel_id=1, replica_groups=mesh['yh'=2,'z1'=4,'z0'=4,'x'=4,'yl'=2,'c'=2] {'z1'}, dimensions={0} | all-to-all | bytes 262144 | tf_op jit(solution)/shard_map/all_to_all | solution.py:264
  30.4 11.4 %all-gather = bf16[16,128,128]{2,1,0:T(8,128)(2,1)S(1)} all-gather(bf16[4,128,128]{2,1,0:T(8,128)(2,1)S(1)} %all_to_all.10), channel_id=2, replica_groups=mesh['yh'=2,'z1'=4,'z0'=4,'x'=4,'yl'=2,'c'=2] {'yh','c'}, dimensions={0}, use_global_device_ids=true | all-gather | bytes 655360 | tf_op jit(solution)/shard_map/all_gather | solution.py:265
  41.8 2.7 %collective-permute-start = (bf16[2,2,4,128,128]{4,3,2,1,0:T(8,128)(2,1)S(1)}, bf16[2,2,4,128,128]{4,3,2,1,0:T(8,128)(2,1)S(1)}, u32[]{:S(2)}, u32[]{:S(2)}) collective-permute-start(bf16[2,2,4,128,128]{4,3,2,1,0:T(8,128)(2,1)S(1)} %bitcast.4), channel_id=1, source_target_pairs={{16,0},{241,1},{18,2},{243,3},{20,4},{245,5},{22,6},{247,7},{24,8}... | collective-permute-start | bytes 1572872 | tf_op jit(solution)/shard_map/ppermute | solution.py:260
  44.6 0.0 copy-start.5
  44.6 0.0 copy-start
  44.6 0.0 copy-start.1
  44.6 3.2 %collective-permute-start.1 = (bf16[1,2,4,128,128]{4,3,2,1,0:T(8,128)(2,1)S(1)}, bf16[1,2,4,128,128]{4,3,2,1,0:T(8,128)(2,1)S(1)}, u32[]{:S(2)}, u32[]{:S(2)}) collective-permute-start(bf16[1,2,4,128,128]{4,3,2,1,0:T(8,128)(2,1)S(1)} %constant_dynamic-slice_fusion), channel_id=1, source_target_pairs={{32,0},{225,1},{34,2},{227,3},{36,4},{229,5},{38,6},{231,7},{40,8}... | collective-permute-start | bytes 786440 | tf_op jit(solution)/shard_map/ppermute | solution.py:260
  47.8 7.9 %collective-permute-done.1.across = bf16[1,2,4,128,128]{4,3,2,1,0:T(8,128)(2,1)S(1)} collective-permute-done((bf16[1,2,4,128,128]{4,3,2,1,0:T(8,128)(2,1)S(1)}, bf16[1,2,4,128,128]{4,3,2,1,0:T(8,128)(2,1)S(1)}, u32[]{:S(2)}, u32[]{:S(2)}) %collective-permute-start.1) | collective-permute-done | bytes 262176 | tf_op jit(solution)/shard_map/ppermute | solution.py:260
  55.7 0.2 collective-permute-done.near
  55.9 0.1 pad_maximum_fusion
  56.0 5.2 %collective-permute-start.2 = (bf16[3,2,4,128,128]{4,3,2,1,0:T(8,128)(2,1)S(1)}, bf16[3,2,4,128,128]{4,3,2,1,0:T(8,128)(2,1)S(1)}, u32[]{:S(2)}, u32[]{:S(2)}) collective-permute-start(bf16[3,2,4,128,128]{4,3,2,1,0:T(8,128)(2,1)S(1)} %pad_maximum_fusion), channel_id=1, source_target_pairs={{0,1},{1,0},{2,3},{3,2},{4,5},{5,4},{6,7},{7,6},{8,9},{9,8},{10,11... | collective-permute-start | bytes 2359304 | tf_op jit(solution)/shard_map/ppermute | solution.py:269
  61.2 0.0 copy-done.5
  61.2 0.1 fusion
  61.3 1.8 %collective-permute-done.2.other = bf16[3,2,4,128,128]{4,3,2,1,0:T(8,128)(2,1)S(1)} collective-permute-done((bf16[3,2,4,128,128]{4,3,2,1,0:T(8,128)(2,1)S(1)}, bf16[3,2,4,128,128]{4,3,2,1,0:T(8,128)(2,1)S(1)}, u32[]{:S(2)}, u32[]{:S(2)}) %collective-permute-start.2) | collective-permute-done | bytes 786464 | tf_op jit(solution)/shard_map/ppermute | solution.py:269
  63.1 0.0 copy-done
  63.1 0.0 copy-done.1
  63.1 0.0 copy-done.2
  63.1 0.0 copy-done.3
  63.1 1.7 %decode.1 = bf16[16,8,384]{2,1,0:T(8,128)(2,1)} custom-call(s32[32,128]{1,0:T(8,128)S(1)} %bitcast.8, bf16[4,768]{1,0:T(4,128)(2,1)S(1)} %copy-done.4, bf16[4,1024]{1,0:T(4,128)(2,1)S(1)} %copy-done.2, bf16[4,1024]{1,0:T(4,128)(2,1)S(1)} %copy-done.3, bf16[768,384]{1,0:T(8,128)(2,1)S(1)} %copy-done, bf16[2,2,4,128,128]{4,3,2,1,0:T(8,128)(2,1)S(1)} %bitcast.6, ...), custom_call_target="tpu_custom_call" | custom-call | flops 100000000 | bytes 4000000 | tf_op jit(solution)/shard_map/decode/pallas_call | solution.py:127
  64.8 5.0 %all-to-all-start.1 = ((bf16[16,8,384]{2,1,0:T(8,128)(2,1)}), bf16[16,8,384]{2,1,0:T(8,128)(2,1)S(1)}, u32[]{:S(2)}, u32[]{:S(2)}) async-start(bf16[16,8,384]{2,1,0:T(8,128)(2,1)} %decode.1), calls=%async_computation.1 | async-start | bytes 196608 | tf_op jit(solution)/shard_map/all_to_all | solution.py:273
  69.8 2.7 %prefill.1 = (bf16[128,768]{1,0:T(8,128)(2,1)}, bf16[64,2560]{1,0:T(8,128)(2,1)}, bf16[64,2560]{1,0:T(8,128)(2,1)}) custom-call(s32[4]{0:T(128)S(1)} %copy-done.5, s32[32,128]{1,0:T(8,128)S(1)} %bitcast.9, bf16[128,768]{1,0:T(8,128)(2,1)S(1)} %copy-done.6, bf16[2,2,4,128,128]{4,3,2,1,0:T(8,128)(2,1)S(1)} %bitcast.7, ...), custom_call_target="tpu_custom_call" | custom-call | flops 2000000000 | bytes 4000000 | tf_op jit(solution)/shard_map/prefill/pallas_call | solution.py:233
  72.5 3.2 %all-to-all-done.1 = bf16[16,8,384]{2,1,0:T(8,128)(2,1)S(1)} async-done(((bf16[16,8,384]{2,1,0:T(8,128)(2,1)}), bf16[16,8,384]{2,1,0:T(8,128)(2,1)S(1)}, u32[]{:S(2)}, u32[]{:S(2)}) %all-to-all-start.1) | async-done | bytes 98336 | tf_op jit(solution)/shard_map/all_to_all | solution.py:273
  75.8 0.7 multiply_reduce_fusion
  (9 shorter events, 0.1 us)
Async XLA Ops:
  41.8 14.1 %collective-permute-start = (bf16[2,2,4,128,128]{4,3,2,1,0:T(8,128)(2,1)S(1)}, bf16[2,2,4,128,128]{4,3,2,1,0:T(8,128)(2,1)S(1)}, u32[]{:S(2)}, u32[]{:S(2)}) collective-permute-start(bf16[2,2,4,128,128]{4,3,2,1,0:T(8,128)(2,1)S(1)} %bitcast.4), channel_id=1, source_target_pairs={{16,0},{241,1},{18,2},{243,3},{20,4},{245,5},{22,6},{247,7},{24,8}... | collective-permute-start | bytes 1572872 | tf_op jit(solution)/shard_map/ppermute | solution.py:260
  44.6 16.6 %copy-start.5 = (s32[4]{0:T(128)S(1)}, s32[4]{0:T(128)}, u32[]{:S(2)}) copy-start(s32[4]{0:T(128)} %replica_of.1) | copy-start | bytes 52
  44.6 18.5 %copy-start = (bf16[768,384]{1,0:T(8,128)(2,1)S(1)}, bf16[768,384]{1,0:T(8,128)(2,1)}, u32[]{:S(2)}) copy-start(bf16[768,384]{1,0:T(8,128)(2,1)} %weight.1) | copy-start | bytes 1769476
  44.6 18.5 %copy-start.1 = (s32[4096]{0:T(1024)S(1)}, s32[4096]{0:T(1024)}, u32[]{:S(2)}) copy-start(s32[4096]{0:T(1024)} %param.12) | copy-start | bytes 49156
  44.6 11.1 %collective-permute-start.1 = (bf16[1,2,4,128,128]{4,3,2,1,0:T(8,128)(2,1)S(1)}, bf16[1,2,4,128,128]{4,3,2,1,0:T(8,128)(2,1)S(1)}, u32[]{:S(2)}, u32[]{:S(2)}) collective-permute-start(bf16[1,2,4,128,128]{4,3,2,1,0:T(8,128)(2,1)S(1)} %constant_dynamic-slice_fusion), channel_id=1, source_target_pairs={{32,0},{225,1},{34,2},{227,3},{36,4},{229,5},{38,6},{231,7},{40,8}... | collective-permute-start | bytes 786440 | tf_op jit(solution)/shard_map/ppermute | solution.py:260
  55.9 7.2 %copy-start.2 = (bf16[4,1024]{1,0:T(4,128)(2,1)S(1)}, bf16[4,1024]{1,0:T(4,128)(2,1)}, u32[]{:S(2)}) copy-start(bf16[4,1024]{1,0:T(4,128)(2,1)} %step_key.1) | copy-start | bytes 24580
  55.9 7.2 %copy-start.3 = (bf16[4,1024]{1,0:T(4,128)(2,1)S(1)}, bf16[4,1024]{1,0:T(4,128)(2,1)}, u32[]{:S(2)}) copy-start(bf16[4,1024]{1,0:T(4,128)(2,1)} %step_value.1) | copy-start | bytes 24580
  55.9 7.2 %copy-start.4 = (bf16[4,768]{1,0:T(4,128)(2,1)S(1)}, bf16[4,768]{1,0:T(4,128)(2,1)}, u32[]{:S(2)}) copy-start(bf16[4,768]{1,0:T(4,128)(2,1)} %step_query.1) | copy-start | bytes 18436
  56.0 7.1 %collective-permute-start.2 = (bf16[3,2,4,128,128]{4,3,2,1,0:T(8,128)(2,1)S(1)}, bf16[3,2,4,128,128]{4,3,2,1,0:T(8,128)(2,1)S(1)}, u32[]{:S(2)}, u32[]{:S(2)}) collective-permute-start(bf16[3,2,4,128,128]{4,3,2,1,0:T(8,128)(2,1)S(1)} %pad_maximum_fusion), channel_id=1, source_target_pairs={{0,1},{1,0},{2,3},{3,2},{4,5},{5,4},{6,7},{7,6},{8,9},{9,8},{10,11... | collective-permute-start | bytes 2359304 | tf_op jit(solution)/shard_map/ppermute | solution.py:269
  64.8 5.0 %copy-start.6 = (bf16[128,768]{1,0:T(8,128)(2,1)S(1)}, bf16[128,768]{1,0:T(8,128)(2,1)}, u32[]{:S(2)}) copy-start(bf16[128,768]{1,0:T(8,128)(2,1)} %queries.1) | copy-start | bytes 589828
  64.8 10.9 %all-to-all-start.1 = ((bf16[16,8,384]{2,1,0:T(8,128)(2,1)}), bf16[16,8,384]{2,1,0:T(8,128)(2,1)S(1)}, u32[]{:S(2)}, u32[]{:S(2)}) async-start(bf16[16,8,384]{2,1,0:T(8,128)(2,1)} %decode.1), calls=%async_computation.1 | async-start | bytes 196608 | tf_op jit(solution)/shard_map/all_to_all | solution.py:273

commit v4 on v3

--- a/solution.py
+++ b/solution.py
@@ -29,28 +29,25 @@
     return ctx, lax.axis_index("c"), lax.axis_index("x") * 2 + lax.axis_index("yl"), z0
 
 
-def pick_kernel(keys, values, out, half, sem):
+def pick_kernel(keys, values, out, sem):
     _, core, head, _ = position()
     columns = pl.ds(pl.multiple_of(head * HD, HD), HD)
     for which, source in ((0, keys), (1, values)):
 
         @pl.when(core == which)
         def _():
-            copy = pltpu.make_async_copy(source.at[:, columns], half, sem)
+            copy = pltpu.make_async_copy(source.at[:, columns], out, sem)
             copy.start()
             copy.wait()
 
-    for g in range(out.shape[0]):
-        out[g] = half[...]
-
-
-def pick(keys, values, copies):
+
+def pick(keys, values):
     return pl.pallas_call(
         pick_kernel,
-        out_shape=jax.ShapeDtypeStruct((copies, ROWS, HD), jnp.bfloat16),
+        out_shape=jax.ShapeDtypeStruct((ROWS, HD), jnp.bfloat16),
         in_specs=[pl.BlockSpec(memory_space=pltpu.HBM)] * 2,
         out_specs=pl.BlockSpec(memory_space=pltpu.VMEM),
-        scratch_shapes=[pltpu.VMEM((ROWS, HD), jnp.bfloat16), pltpu.SemaphoreType.DMA],
+        scratch_shapes=[pltpu.SemaphoreType.DMA],
         compiler_params=pltpu.CompilerParams(vmem_limit_bytes=60 * 1024 * 1024),
         name="pick",
     )(keys, values)
@@ -261,7 +258,7 @@
 
 
 def local(queries, keys, values, doc_ids, replica_of, step_query, step_key, step_value, out_weight):
-    half = lax.all_to_all(pick(keys, values, 4), "z1", 0, 0)
+    half = lax.all_gather(pick(keys, values), "z1", axis=0)
     far = lax.all_gather(half, ("yh", "c"), axis=0).reshape(2, 2, 4, ROWS, HD)
     near = from_sides(far, 1)
     across = from_sides(lax.dynamic_slice_in_dim(far, lax.axis_index("c"), 1, 0), 2)

time: 76.9 us -> 73.2 us (0.952)
  blocking collectives: 39.7 us -> 36.3 us
    all_to_all x1 -> x0, blocking collectives: 28.3 us -> none  [local(): half = lax.all_to_all(pick(keys, values, 4), 'z1', 0, 0)]
    all_gather x0 -> x1, blocking collectives: none -> 24.1 us  [local(): half = lax.all_gather(pick(keys, values), 'z1', axis=0)]
  transfers between devices with their start and end apart: 4 -> 4, of which waited for: 4 -> 3; matrix products, arithmetic and copies ran while one was open for 0% -> 0% of each run, Pallas kernels for 3% -> 4%
where the time goes in v4:
time: 73.2 us; the launch traced here: 72.8 us
  blocking collectives  36.3 us (50%)
  starting transfers between devices  15.4 us (21%)
  waiting for transfers between devices  13.8 us (19%)
  Pallas kernels  5.77 us (8%)
  other arithmetic  0.86 us (1%)
  between operations  0.75 us (1%)
    all_gather x1, blocking collectives, local(): half = lax.all_gather(pick(keys, values), 'z1', axis=0)  24.1 us
    all_gather x1, blocking collectives, local(): far = lax.all_gather(half, ('yh', 'c'), axis=0).reshape(2, 2, 4, ROWS, HD)  12.2 us
    ppermute x2, waiting for transfers between devices, from_sides(): return lax.ppermute(a, CTX + TP, pairs)  8.73 us
    ppermute x2, starting transfers between devices, from_sides(): return lax.ppermute(a, CTX + TP, pairs)  5.87 us
    all_to_all x1, starting transfers between devices, local(): summed = lax.all_to_all(terms, TP, 0, 0)  4.98 us
    ppermute x1, starting transfers between devices, local(): other = lax.ppermute(both, 'c', [(0, 1), (1, 0)])  4.52 us
    all_to_all x1, waiting for transfers between devices, local(): summed = lax.all_to_all(terms, TP, 0, 0)  3.24 us
    pallas_call x1, Pallas kernels, prefill(): pl.pallas_call(prefill_kernel, out_shape=(jax.ShapeDtypeStruct((ROWS, HEA...  2.66 us
  transfers between devices with their start and end apart: 4, of which 3 were waited for; matrix products, arithmetic and copies ran while one was open for 0% of the time, Pallas kernels for 4%

profile of v4, /device:TPU:1, one launch (start us, length us, event | category | flops | bytes accessed | tf_op | source)
XLA Modules:
  0.0 72.8 jit_solution(3686393527911743027)
XLA Ops:
  0.6 1.4 %pick.1 = bf16[128,128]{1,0:T(8,128)(2,1)} custom-call(bf16[128,1024]{1,0:T(8,128)(2,1)} %keys.1, bf16[128,1024]{1,0:T(8,128)(2,1)} %values.1), custom_call_target="tpu_custom_call" | custom-call | tf_op jit(solution)/shard_map/pick/pallas_call | solution.py:45
  2.0 24.1 %all-gather = bf16[512,128]{1,0:T(8,128)(2,1)S(1)} all-gather(bf16[128,128]{1,0:T(8,128)(2,1)} %pick.1), channel_id=2, replica_groups=mesh['yh'=2,'z1'=4,'z0'=4,'x'=4,'yl'=2,'c'=2] {'z1'}, dimensions={0}, use_global_device_ids=true | all-gather | bytes 163840 | tf_op jit(solution)/shard_map/all_gather | solution.py:261
  26.1 12.2 %all-gather.1 = bf16[16,128,128]{2,1,0:T(8,128)(2,1)S(1)} all-gather(bf16[4,128,128]{2,1,0:T(8,128)(2,1)S(1)} %bitcast.11), channel_id=3, replica_groups=mesh['yh'=2,'z1'=4,'z0'=4,'x'=4,'yl'=2,'c'=2] {'yh','c'}, dimensions={0}, use_global_device_ids=true | all-gather | bytes 655360 | tf_op jit(solution)/shard_map/all_gather | solution.py:262
  38.3 2.6 %collective-permute-start = (bf16[2,2,4,128,128]{4,3,2,1,0:T(8,128)(2,1)S(1)}, bf16[2,2,4,128,128]{4,3,2,1,0:T(8,128)(2,1)S(1)}, u32[]{:S(2)}, u32[]{:S(2)}) collective-permute-start(bf16[2,2,4,128,128]{4,3,2,1,0:T(8,128)(2,1)S(1)} %bitcast.5), channel_id=1, source_target_pairs={{16,0},{241,1},{18,2},{243,3},{20,4},{245,5},{22,6},{247,7},{24,8}... | collective-permute-start | bytes 1572872 | tf_op jit(solution)/shard_map/ppermute | solution.py:257
  41.0 0.0 copy-start.5
  41.0 0.0 copy-start
  41.0 0.0 copy-start.1
  41.0 3.2 %collective-permute-start.1 = (bf16[1,2,4,128,128]{4,3,2,1,0:T(8,128)(2,1)S(1)}, bf16[1,2,4,128,128]{4,3,2,1,0:T(8,128)(2,1)S(1)}, u32[]{:S(2)}, u32[]{:S(2)}) collective-permute-start(bf16[1,2,4,128,128]{4,3,2,1,0:T(8,128)(2,1)S(1)} %constant_dynamic-slice_fusion), channel_id=1, source_target_pairs={{32,0},{225,1},{34,2},{227,3},{36,4},{229,5},{38,6},{231,7},{40,8}... | collective-permute-start | bytes 786440 | tf_op jit(solution)/shard_map/ppermute | solution.py:257
  44.2 8.7 %collective-permute-done.1.across = bf16[1,2,4,128,128]{4,3,2,1,0:T(8,128)(2,1)S(1)} collective-permute-done((bf16[1,2,4,128,128]{4,3,2,1,0:T(8,128)(2,1)S(1)}, bf16[1,2,4,128,128]{4,3,2,1,0:T(8,128)(2,1)S(1)}, u32[]{:S(2)}, u32[]{:S(2)}) %collective-permute-start.1) | collective-permute-done | bytes 262176 | tf_op jit(solution)/shard_map/ppermute | solution.py:257
  53.0 0.0 collective-permute-done.near
  53.0 0.1 pad_maximum_fusion
  53.1 4.5 %collective-permute-start.2 = (bf16[3,2,4,128,128]{4,3,2,1,0:T(8,128)(2,1)S(1)}, bf16[3,2,4,128,128]{4,3,2,1,0:T(8,128)(2,1)S(1)}, u32[]{:S(2)}, u32[]{:S(2)}) collective-permute-start(bf16[3,2,4,128,128]{4,3,2,1,0:T(8,128)(2,1)S(1)} %pad_maximum_fusion), channel_id=1, source_target_pairs={{0,1},{1,0},{2,3},{3,2},{4,5},{5,4},{6,7},{7,6},{8,9},{9,8},{10,11... | collective-permute-start | bytes 2359304 | tf_op jit(solution)/shard_map/ppermute | solution.py:266
  57.6 0.0 copy-done.5
  57.6 0.1 fusion
  57.7 1.8 %collective-permute-done.2.other = bf16[3,2,4,128,128]{4,3,2,1,0:T(8,128)(2,1)S(1)} collective-permute-done((bf16[3,2,4,128,128]{4,3,2,1,0:T(8,128)(2,1)S(1)}, bf16[3,2,4,128,128]{4,3,2,1,0:T(8,128)(2,1)S(1)}, u32[]{:S(2)}, u32[]{:S(2)}) %collective-permute-start.2) | collective-permute-done | bytes 786464 | tf_op jit(solution)/shard_map/ppermute | solution.py:266
  59.5 0.0 copy-done
  59.5 0.0 copy-done.1
  59.5 0.0 copy-done.3
  59.5 1.7 %decode.1 = bf16[16,8,384]{2,1,0:T(8,128)(2,1)} custom-call(s32[32,128]{1,0:T(8,128)S(1)} %bitcast.9, bf16[4,768]{1,0:T(4,128)(2,1)S(1)} %copy-done.4, bf16[4,1024]{1,0:T(4,128)(2,1)S(1)} %copy-done.2, bf16[4,1024]{1,0:T(4,128)(2,1)S(1)} %copy-done.3, bf16[768,384]{1,0:T(8,128)(2,1)S(1)} %copy-done, bf16[2,2,4,128,128]{4,3,2,1,0:T(8,128)(2,1)S(1)} %bitcast.7, ...), custom_call_target="tpu_custom_call" | custom-call | flops 100000000 | bytes 4000000 | tf_op jit(solution)/shard_map/decode/pallas_call | solution.py:124
  61.2 5.0 %all-to-all-start = ((bf16[16,8,384]{2,1,0:T(8,128)(2,1)}), bf16[16,8,384]{2,1,0:T(8,128)(2,1)S(1)}, u32[]{:S(2)}, u32[]{:S(2)}) async-start(bf16[16,8,384]{2,1,0:T(8,128)(2,1)} %decode.1), calls=%async_computation | async-start | bytes 196608 | tf_op jit(solution)/shard_map/all_to_all | solution.py:270
  66.2 0.0 copy-done.6
  66.2 2.7 %prefill.1 = (bf16[128,768]{1,0:T(8,128)(2,1)}, bf16[64,2560]{1,0:T(8,128)(2,1)}, bf16[64,2560]{1,0:T(8,128)(2,1)}) custom-call(s32[4]{0:T(128)S(1)} %copy-done.5, s32[32,128]{1,0:T(8,128)S(1)} %bitcast.10, bf16[128,768]{1,0:T(8,128)(2,1)S(1)} %copy-done.6, bf16[2,2,4,128,128]{4,3,2,1,0:T(8,128)(2,1)S(1)} %bitcast.8, ...), custom_call_target="tpu_custom_call" | custom-call | flops 2000000000 | bytes 4000000 | tf_op jit(solution)/shard_map/prefill/pallas_call | solution.py:230
  68.9 3.2 %all-to-all-done = bf16[16,8,384]{2,1,0:T(8,128)(2,1)S(1)} async-done(((bf16[16,8,384]{2,1,0:T(8,128)(2,1)}), bf16[16,8,384]{2,1,0:T(8,128)(2,1)S(1)}, u32[]{:S(2)}, u32[]{:S(2)}) %all-to-all-start) | async-done | bytes 98336 | tf_op jit(solution)/shard_map/all_to_all | solution.py:270
  72.1 0.7 multiply_reduce_fusion
  (9 shorter events, 0.1 us)
Async XLA Ops:
  38.3 14.7 %collective-permute-start = (bf16[2,2,4,128,128]{4,3,2,1,0:T(8,128)(2,1)S(1)}, bf16[2,2,4,128,128]{4,3,2,1,0:T(8,128)(2,1)S(1)}, u32[]{:S(2)}, u32[]{:S(2)}) collective-permute-start(bf16[2,2,4,128,128]{4,3,2,1,0:T(8,128)(2,1)S(1)} %bitcast.5), channel_id=1, source_target_pairs={{16,0},{241,1},{18,2},{243,3},{20,4},{245,5},{22,6},{247,7},{24,8}... | collective-permute-start | bytes 1572872 | tf_op jit(solution)/shard_map/ppermute | solution.py:257
  41.0 16.6 %copy-start.5 = (s32[4]{0:T(128)S(1)}, s32[4]{0:T(128)}, u32[]{:S(2)}) copy-start(s32[4]{0:T(128)} %replica_of.1) | copy-start | bytes 52
  41.0 18.5 %copy-start = (bf16[768,384]{1,0:T(8,128)(2,1)S(1)}, bf16[768,384]{1,0:T(8,128)(2,1)}, u32[]{:S(2)}) copy-start(bf16[768,384]{1,0:T(8,128)(2,1)} %weight.1) | copy-start | bytes 1769476
  41.0 18.5 %copy-start.1 = (s32[4096]{0:T(1024)S(1)}, s32[4096]{0:T(1024)}, u32[]{:S(2)}) copy-start(s32[4096]{0:T(1024)} %param.12) | copy-start | bytes 49156
  41.0 12.0 %collective-permute-start.1 = (bf16[1,2,4,128,128]{4,3,2,1,0:T(8,128)(2,1)S(1)}, bf16[1,2,4,128,128]{4,3,2,1,0:T(8,128)(2,1)S(1)}, u32[]{:S(2)}, u32[]{:S(2)}) collective-permute-start(bf16[1,2,4,128,128]{4,3,2,1,0:T(8,128)(2,1)S(1)} %constant_dynamic-slice_fusion), channel_id=1, source_target_pairs={{32,0},{225,1},{34,2},{227,3},{36,4},{229,5},{38,6},{231,7},{40,8}... | collective-permute-start | bytes 786440 | tf_op jit(solution)/shard_map/ppermute | solution.py:257
  53.0 6.5 %copy-start.2 = (bf16[4,1024]{1,0:T(4,128)(2,1)S(1)}, bf16[4,1024]{1,0:T(4,128)(2,1)}, u32[]{:S(2)}) copy-start(bf16[4,1024]{1,0:T(4,128)(2,1)} %step_key.1) | copy-start | bytes 24580
  53.0 6.5 %copy-start.3 = (bf16[4,1024]{1,0:T(4,128)(2,1)S(1)}, bf16[4,1024]{1,0:T(4,128)(2,1)}, u32[]{:S(2)}) copy-start(bf16[4,1024]{1,0:T(4,128)(2,1)} %step_value.1) | copy-start | bytes 24580
  53.0 6.5 %copy-start.4 = (bf16[4,768]{1,0:T(4,128)(2,1)S(1)}, bf16[4,768]{1,0:T(4,128)(2,1)}, u32[]{:S(2)}) copy-start(bf16[4,768]{1,0:T(4,128)(2,1)} %step_query.1) | copy-start | bytes 18436
  53.1 6.4 %collective-permute-start.2 = (bf16[3,2,4,128,128]{4,3,2,1,0:T(8,128)(2,1)S(1)}, bf16[3,2,4,128,128]{4,3,2,1,0:T(8,128)(2,1)S(1)}, u32[]{:S(2)}, u32[]{:S(2)}) collective-permute-start(bf16[3,2,4,128,128]{4,3,2,1,0:T(8,128)(2,1)S(1)} %pad_maximum_fusion), channel_id=1, source_target_pairs={{0,1},{1,0},{2,3},{3,2},{4,5},{5,4},{6,7},{7,6},{8,9},{9,8},{10,11... | collective-permute-start | bytes 2359304 | tf_op jit(solution)/shard_map/ppermute | solution.py:266
  61.2 5.0 %copy-start.6 = (bf16[128,768]{1,0:T(8,128)(2,1)S(1)}, bf16[128,768]{1,0:T(8,128)(2,1)}, u32[]{:S(2)}) copy-start(bf16[128,768]{1,0:T(8,128)(2,1)} %queries.1) | copy-start | bytes 589828
  61.2 10.9 %all-to-all-start = ((bf16[16,8,384]{2,1,0:T(8,128)(2,1)}), bf16[16,8,384]{2,1,0:T(8,128)(2,1)S(1)}, u32[]{:S(2)}, u32[]{:S(2)}) async-start(bf16[16,8,384]{2,1,0:T(8,128)(2,1)} %decode.1), calls=%async_computation | async-start | bytes 196608 | tf_op jit(solution)/shard_map/all_to_all | solution.py:270

commit v5 on v4

--- a/solution.py
+++ b/solution.py
@@ -63,72 +63,104 @@
 PAD = 32
 
 
-def decode_kernel(
-    doc_ids, step_query, step_key, step_value, weight, far, near, across, other, terms, query, own_key, own_value
-):
-    _, core, head, z0 = position()
-    columns = pl.ds(pl.multiple_of(head * HD, HD), HD)
-    side = 1 - 2 * core
+def combine(parts):
+    top = parts[0][1]
+    for _, weight in parts[1:]:
+        top = jnp.maximum(top, weight)
+    shares = [jnp.exp(weight - top) for _, weight in parts]
+    return sum(share * mixed for share, (mixed, _) in zip(shares, parts)) / sum(shares)
+
+
+def class_part_kernel(doc_ids, step_query, far, out, query):
+    z0 = position()[3]
+    query[...] = jnp.zeros_like(query)
+    steps = step_query[...].astype(jnp.float32)
+    for h in range(HEADS):
+        query[h * NDOC : (h + 1) * NDOC, :] = steps[:, h * HD : (h + 1) * HD]
+    narrow = query[...].astype(jnp.bfloat16)
     starts, ends = doc_bounds(doc_ids)
-    steps = step_query[...].astype(jnp.float32)
-    step_keys = step_key[:, columns].astype(jnp.float32)
-    step_values = step_value[:, columns].astype(jnp.float32)
-    for ref in (query, own_key, own_value):
-        ref[ROW:PAD, :] = jnp.zeros((PAD - ROW, HD), jnp.float32)
-    for h in range(HEADS):
-        rows = slice(h * NDOC, (h + 1) * NDOC)
-        query[rows, :] = steps[:, h * HD : (h + 1) * HD]
-        own_key[rows, :] = step_keys
-        own_value[rows, :] = step_values
-    q = query[...]
     document = lax.broadcasted_iota(jnp.int32, (PAD, 1), 0) % NDOC
     low = jnp.zeros((PAD, 1), jnp.int32)
     high = jnp.zeros((PAD, 1), jnp.int32)
     for d in range(NDOC):
         low = jnp.where(document == d, starts[d], low)
         high = jnp.where(document == d, ends[d], high)
-    narrow = q.astype(jnp.bfloat16)
-    groups = [(far, 0, z0, 0), (far, 1, z0, 1), (near, 0, z0 + 4 + side, 0), (near, 1, z0 + 4 + side, 1)]
-    groups += [(other, 0, z0 + 4 - side, 0), (other, 1, z0 + 4 - side, 1), (across, 0, z0 + 2, core), (other, 2, z0 + 2, 1 - core)]
     at = lax.broadcasted_iota(jnp.int32, (1, 4 * ROWS), 1)
-    at = at // ROWS * (4 * ROWS) + at % ROWS
-    nums, tops = [], []
-    for ref, index, kind, yh in groups:
-        place = at + (yh * (16 * ROWS) + lax.rem(kind, 4) * ROWS)
-        keys = ref[index, 0].reshape(4 * ROWS, HD)
+    at = at // ROWS * (4 * ROWS) + at % ROWS + z0 * ROWS
+    scores, seen = [], []
+    top = jnp.full((PAD, 1), NEG, jnp.float32)
+    for yh in range(2):
+        place = at + yh * (16 * ROWS)
+        mask = (place >= low) & (place < high)
+        keys = far[yh, 0].reshape(4 * ROWS, HD)
         s = lax.dot_general(narrow, keys, (((1,), (1,)), ((), ())), preferred_element_type=jnp.float32)
-        s = jnp.where((place >= low) & (place < high), s * SCALE, NEG)
-        nums.append(s)
-        tops.append(jnp.max(s, axis=1, keepdims=True))
-    own_score = jnp.sum(q * own_key[...], axis=1, keepdims=True) * SCALE
-    top = own_score
-    for t in tops:
-        top = jnp.maximum(top, t)
-    own_prob = jnp.exp(own_score - top)
-    total = own_prob
-    mixed = own_prob.astype(jnp.bfloat16).astype(jnp.float32) * own_value[...]
-    for s, (ref, index, _, _) in zip(nums, groups):
-        p = jnp.exp(s - top)
+        s = jnp.where(mask, s * SCALE, NEG)
+        top = jnp.maximum(top, jnp.max(s, axis=1, keepdims=True))
+        scores.append(s)
+        seen.append(mask)
+    total = jnp.zeros((PAD, 1), jnp.float32)
+    mixed = jnp.zeros((PAD, HD), jnp.float32)
+    for yh in range(2):
+        p = jnp.where(seen[yh], jnp.exp(scores[yh] - top), 0.0)
         total = total + jnp.sum(p, axis=1, keepdims=True)
-        values = ref[index, 1].reshape(4 * ROWS, HD)
+        values = far[yh, 1].reshape(4 * ROWS, HD)
         mixed = mixed + jnp.dot(p.astype(jnp.bfloat16), values, preferred_element_type=jnp.float32)
-    query[...] = mixed / total
-    wide = jnp.concatenate([query[h * NDOC : (h + 1) * NDOC, :] for h in range(HEADS)], axis=1)
+    some = total > 0.0
+    safe = jnp.where(some, total, 1.0)
+    weight = jnp.where(some, top + jnp.log(safe), NEG)
+    sub = lax.broadcasted_iota(jnp.int32, (PAD, HD), 0)
+    lane = lax.broadcasted_iota(jnp.int32, (PAD, HD), 1)
+    line = jnp.sum(jnp.where(sub == lane, weight, 0.0), axis=0, keepdims=True)
+    out[...] = jnp.where(sub == ROW, line, mixed / safe)
+
+
+def class_part(doc_ids, step_query, far):
+    return pl.pallas_call(
+        class_part_kernel,
+        out_shape=jax.ShapeDtypeStruct((PAD, HD), jnp.float32),
+        scratch_shapes=[pltpu.VMEM((PAD, HD), jnp.float32)],
+        compiler_params=pltpu.CompilerParams(vmem_limit_bytes=8 * 1024 * 1024),
+        cost_estimate=pl.CostEstimate(flops=3 * 10**7, bytes_accessed=10**6, transcendentals=4 * 10**4),
+        name="class_part",
+    )(doc_ids, step_query, far)
+
+
+def project_kernel(parts, step_query, step_key, step_value, weight, terms, product, mixed):
+    head = position()[2]
+    columns = pl.ds(pl.multiple_of(head * HD, HD), HD)
+    steps = step_query[...].astype(jnp.float32)
+    step_keys = step_key[:, columns].astype(jnp.float32)
+    step_values = step_value[:, columns].astype(jnp.float32)
+    for ref in (product, mixed):
+        ref[ROW:PAD, :] = jnp.zeros((PAD - ROW, HD), jnp.float32)
+    for h in range(HEADS):
+        rows = slice(h * NDOC, (h + 1) * NDOC)
+        product[rows, :] = steps[:, h * HD : (h + 1) * HD] * step_keys
+        mixed[rows, :] = step_values
+    sub = lax.broadcasted_iota(jnp.int32, (PAD, HD), 0)
+    lane = lax.broadcasted_iota(jnp.int32, (PAD, HD), 1)
+    found = [(mixed[...], jnp.sum(product[...], axis=1, keepdims=True) * SCALE)]
+    for k in range(parts.shape[0]):
+        part = parts[k]
+        line = jnp.sum(jnp.where(sub == ROW, part, 0.0), axis=0, keepdims=True)
+        found.append((part, jnp.sum(jnp.where(sub == lane, line, 0.0), axis=1, keepdims=True)))
+    mixed[...] = combine(found)
+    wide = jnp.concatenate([mixed[h * NDOC : (h + 1) * NDOC, :] for h in range(HEADS)], axis=1)
     wide = jnp.concatenate([wide, jnp.zeros_like(wide)], axis=0)
     term = jnp.dot(wide.astype(jnp.bfloat16), weight[...], preferred_element_type=jnp.float32).astype(terms.dtype)
     for k in range(16):
         terms[k] = term
 
 
-def decode(doc_ids, step_query, step_key, step_value, weight, parts):
+def project(parts, step_query, step_key, step_value, weight):
     return pl.pallas_call(
-        decode_kernel,
+        project_kernel,
         out_shape=jax.ShapeDtypeStruct((16, 8, weight.shape[1]), jnp.bfloat16),
-        scratch_shapes=[pltpu.VMEM((PAD, HD), jnp.float32)] * 3,
-        compiler_params=pltpu.CompilerParams(vmem_limit_bytes=12 * 1024 * 1024),
-        cost_estimate=pl.CostEstimate(flops=10**8, bytes_accessed=4 * 10**6, transcendentals=2 * 10**5),
-        name="decode",
-    )(doc_ids, step_query, step_key, step_value, weight, *parts)
+        scratch_shapes=[pltpu.VMEM((PAD, HD), jnp.float32)] * 2,
+        compiler_params=pltpu.CompilerParams(vmem_limit_bytes=8 * 1024 * 1024),
+        cost_estimate=pl.CostEstimate(flops=10**7, bytes_accessed=10**6, transcendentals=10**3),
+        name="project",
+    )(parts, step_query, step_key, step_value, weight)
 
 
 STEP = 4
@@ -136,7 +168,7 @@
 
 def prefill_kernel(
     replica_of, doc_ids, queries, far, near, across, other,
-    context, replica_keys, replica_values,
+    context, replica_keys, replica_values, hot,
     cache, flat, acc,
 ):
     ctx, core, _, z0 = position()
@@ -193,6 +225,13 @@
     for h in range(HEADS):
         context[:, h * HD : (h + 1) * HD] = jnp.transpose(mixed[:, h * ROWS : (h + 1) * ROWS]).astype(jnp.bfloat16)
 
+    replica = lax.broadcasted_iota(jnp.int32, hot.shape, 0)
+    document = lax.broadcasted_iota(jnp.int32, hot.shape, 1) % 8
+    found = jnp.zeros(hot.shape, jnp.float32)
+    for d in range(NDOC):
+        found = jnp.where((document == d) & (replica == replica_of[d]), 1.0, found)
+    hot[...] = found.astype(hot.dtype)
+
     asked = jnp.int32(0)
     start = jnp.int32(0)
     length = jnp.int32(0)
@@ -233,6 +272,7 @@
             jax.ShapeDtypeStruct((ROWS, HEADS * HD), jnp.bfloat16),
             jax.ShapeDtypeStruct((HD // 2, MOST), jnp.bfloat16),
             jax.ShapeDtypeStruct((HD // 2, MOST), jnp.bfloat16),
+            jax.ShapeDtypeStruct((NB, 16 * 8), jnp.bfloat16),
         ),
         in_specs=[pl.BlockSpec(memory_space=pltpu.SMEM)] + [vmem] * 6,
         scratch_shapes=[
@@ -241,7 +281,7 @@
             pltpu.VMEM((HD, HEADS * ROWS), jnp.float32),
         ],
         compiler_params=pltpu.CompilerParams(vmem_limit_bytes=16 * 1024 * 1024),
-        cost_estimate=pl.CostEstimate(flops=2 * 10**9, bytes_accessed=4 * 10**6, transcendentals=2 * 10**6),
+        cost_estimate=pl.CostEstimate(flops=10**6, bytes_accessed=10**5, transcendentals=10**3),
         name="prefill",
     )(replica_of, doc_ids, queries, *parts)
 
@@ -262,16 +302,16 @@
     far = lax.all_gather(half, ("yh", "c"), axis=0).reshape(2, 2, 4, ROWS, HD)
     near = from_sides(far, 1)
     across = from_sides(lax.dynamic_slice_in_dim(far, lax.axis_index("c"), 1, 0), 2)
-    both = jnp.concatenate(lax.optimization_barrier((near, across)), axis=0)
+    blocks = doc_ids.reshape(NB, ROWS)
+    decoded = lax.all_to_all(jnp.broadcast_to(class_part(blocks, step_query, far)[None], (4, PAD, HD)), "z0", 0, 0)
+    terms = project(decoded, step_query, step_key, step_value, out_weight)
+    near, across, terms = lax.optimization_barrier((near, across, terms))
+    both = jnp.concatenate((near, across), axis=0)
     other = lax.ppermute(both, "c", [(0, 1), (1, 0)])
     parts = [far, near, across, other]
-    blocks = doc_ids.reshape(NB, ROWS)
-    terms = decode(blocks, step_query, step_key, step_value, out_weight, parts)
     summed = lax.all_to_all(terms, TP, 0, 0)
-    context, replica_keys, replica_values = prefill(replica_of, blocks, queries, parts)
-    hot = (replica_of[None, :] == jnp.arange(NB, dtype=jnp.int32)[:, None]).astype(jnp.float32)
-    projected = jnp.sum(summed.astype(jnp.float32), axis=0)
-    next_hidden = jnp.sum(hot[:, :, None] * projected[None, :NDOC], axis=1).astype(jnp.bfloat16)
+    context, replica_keys, replica_values, hot = prefill(replica_of, blocks, queries, parts)
+    next_hidden = jnp.dot(hot, summed.reshape(16 * 8, -1), preferred_element_type=jnp.float32).astype(jnp.bfloat16)
     return (context, next_hidden, replica_keys[None], replica_values[None])
 
 

time: 73.2 us -> 71.9 us (0.982)
  waiting for transfers between devices: 13.8 us -> 3.23 us
  blocking collectives: 36.3 us -> 45.9 us
  other arithmetic: 0.86 us -> 0.07 us
  matrix products: 0 us -> 0.75 us
    all_to_all x0 -> x1, blocking collectives: none -> 9.52 us  [local(): lax.all_to_all(jnp.broadcast_to(class_part(blocks, step_query, far)[None]...]
    ppermute x2, waiting for transfers between devices: 8.73 us -> 0.01 us  [from_sides(): return lax.ppermute(a, CTX + TP, pairs)]
    ppermute x1, waiting for transfers between devices: 1.81 us -> 0.01 us  [local(): other = lax.ppermute(both, 'c', [(0, 1), (1, 0)])]
    dot_general x0 -> x1, matrix products: none -> 0.75 us  [local(): jnp.dot(hot, summed.reshape(16 * 8, -1), preferred_element_type=jnp.float32)]
    pallas_call x1 -> x2, Pallas kernels: 1.71 us -> 1.36 us  [the longest x1 0.94 us: project(): pl.pallas_call(project_kernel, out_shape=jax.ShapeDtypeStruct((16, 8, wei...]
  transfers between devices with their start and end apart: 4 -> 4, of which waited for: 3 -> 1; matrix products, arithmetic and copies ran while one was open for 0% -> 0% of each run, Pallas kernels for 4% -> 6%
where the time goes in v5:
time: 71.9 us; the launch traced here: 71.5 us
  blocking collectives  45.9 us (64%)
  starting transfers between devices  15.3 us (21%)
  Pallas kernels  5.42 us (8%)
  waiting for transfers between devices  3.23 us (4%)
  between operations  0.77 us (1%)
  matrix products  0.75 us (1%)
    all_gather x1, blocking collectives, local(): half = lax.all_gather(pick(keys, values), 'z1', axis=0)  24.1 us
    all_gather x1, blocking collectives, local(): far = lax.all_gather(half, ('yh', 'c'), axis=0).reshape(2, 2, 4, ROWS, HD)  12.3 us
    all_to_all x1, blocking collectives, local(): lax.all_to_all(jnp.broadcast_to(class_part(blocks, step_query, far)[None]...  9.52 us
    ppermute x2, starting transfers between devices, from_sides(): return lax.ppermute(a, CTX + TP, pairs)  5.87 us
    ppermute x1, starting transfers between devices, local(): other = lax.ppermute(both, 'c', [(0, 1), (1, 0)])  4.8 us
    all_to_all x1, starting transfers between devices, local(): summed = lax.all_to_all(terms, TP, 0, 0)  4.59 us
    all_to_all x1, waiting for transfers between devices, local(): summed = lax.all_to_all(terms, TP, 0, 0)  3.23 us
    pallas_call x1, Pallas kernels, prefill(): pl.pallas_call(prefill_kernel, out_shape=(jax.ShapeDtypeStruct((ROWS, HEA...  2.66 us
  transfers between devices with their start and end apart: 4, of which 1 were waited for; matrix products, arithmetic and copies ran while one was open for 0% of the time, Pallas kernels for 6%

profile of v5, /device:TPU:1, one launch (start us, length us, event | category | flops | bytes accessed | tf_op | source)
XLA Modules:
  0.0 71.5 jit_solution(202846512949955060)
XLA Ops:
  0.6 1.4 %pick.1 = bf16[128,128]{1,0:T(8,128)(2,1)} custom-call(bf16[128,1024]{1,0:T(8,128)(2,1)} %keys.1, bf16[128,1024]{1,0:T(8,128)(2,1)} %values.1), custom_call_target="tpu_custom_call" | custom-call | tf_op jit(solution)/shard_map/pick/pallas_call | solution.py:45
  2.0 24.1 %all-gather = bf16[512,128]{1,0:T(8,128)(2,1)S(1)} all-gather(bf16[128,128]{1,0:T(8,128)(2,1)} %pick.1), channel_id=2, replica_groups=mesh['yh'=2,'z1'=4,'z0'=4,'x'=4,'yl'=2,'c'=2] {'z1'}, dimensions={0}, use_global_device_ids=true | all-gather | bytes 163840 | tf_op jit(solution)/shard_map/all_gather | solution.py:301
  26.1 12.3 %all-gather.1 = bf16[16,128,128]{2,1,0:T(8,128)(2,1)S(1)} all-gather(bf16[4,128,128]{2,1,0:T(8,128)(2,1)S(1)} %bitcast.15), channel_id=3, replica_groups=mesh['yh'=2,'z1'=4,'z0'=4,'x'=4,'yl'=2,'c'=2] {'yh','c'}, dimensions={0}, use_global_device_ids=true | all-gather | bytes 655360 | tf_op jit(solution)/shard_map/all_gather | solution.py:302
  38.4 2.6 %collective-permute-start = (bf16[2,2,4,128,128]{4,3,2,1,0:T(8,128)(2,1)S(1)}, bf16[2,2,4,128,128]{4,3,2,1,0:T(8,128)(2,1)S(1)}, u32[]{:S(2)}, u32[]{:S(2)}) collective-permute-start(bf16[2,2,4,128,128]{4,3,2,1,0:T(8,128)(2,1)S(1)} %bitcast.9), channel_id=1, source_target_pairs={{16,0},{241,1},{18,2},{243,3},{20,4},{245,5},{22,6},{247,7},{24,8}... | collective-permute-start | bytes 1572872 | tf_op jit(solution)/shard_map/ppermute | solution.py:297
  41.1 0.0 copy-start
  41.1 3.2 %collective-permute-start.1 = (bf16[1,2,4,128,128]{4,3,2,1,0:T(8,128)(2,1)S(1)}, bf16[1,2,4,128,128]{4,3,2,1,0:T(8,128)(2,1)S(1)}, u32[]{:S(2)}, u32[]{:S(2)}) collective-permute-start(bf16[1,2,4,128,128]{4,3,2,1,0:T(8,128)(2,1)S(1)} %constant_dynamic-slice_fusion), channel_id=1, source_target_pairs={{32,0},{225,1},{34,2},{227,3},{36,4},{229,5},{38,6},{231,7},{40,8}... | collective-permute-start | bytes 786440 | tf_op jit(solution)/shard_map/ppermute | solution.py:297
  44.4 0.0 copy-done.2
  44.4 0.0 copy-done.3
  44.4 0.4 class_part.1
  44.8 0.0 copy-start.4
  44.8 0.0 copy-start.5
  44.8 9.5 %all_to_all.10.parts = f32[4,32,128]{2,1,0:T(8,128)S(1)} all-to-all(f32[4,32,128]{2,1,0:T(8,128)S(1)} %broadcast_in_dim.12), channel_id=1, replica_groups=mesh['yh'=2,'z1'=4,'z0'=4,'x'=4,'yl'=2,'c'=2] {'z0'}, dimensions={0} | all-to-all | bytes 131072 | tf_op jit(solution)/shard_map/all_to_all | solution.py:306
  54.4 0.0 copy-done
  54.4 0.9 %project.1 = bf16[16,8,384]{2,1,0:T(8,128)(2,1)} custom-call(f32[4,32,128]{2,1,0:T(8,128)S(1)} %all_to_all.10.parts, bf16[4,768]{1,0:T(4,128)(2,1)S(1)} %copy-done.3, bf16[4,1024]{1,0:T(4,128)(2,1)S(1)} %copy-done.4, bf16[4,1024]{1,0:T(4,128)(2,1)S(1)} %copy-done.5, bf16[768,384]{1,0:T(8,128)(2,1)S(1)} %copy-done), custom_call_target="tpu_custom_call" | custom-call | flops 10000000 | bytes 1000000 | tf_op jit(solution)/shard_map/project/pallas_call | solution.py:156
  55.3 0.0 collective-permute-done.1.across
  55.3 0.0 collective-permute-done.near
  55.3 0.1 pad_maximum_fusion
  55.4 0.0 copy-start.1
  55.4 4.8 %collective-permute-start.2 = (bf16[3,2,4,128,128]{4,3,2,1,0:T(8,128)(2,1)S(1)}, bf16[3,2,4,128,128]{4,3,2,1,0:T(8,128)(2,1)S(1)}, u32[]{:S(2)}, u32[]{:S(2)}) collective-permute-start(bf16[3,2,4,128,128]{4,3,2,1,0:T(8,128)(2,1)S(1)} %pad_maximum_fusion), channel_id=1, source_target_pairs={{0,1},{1,0},{2,3},{3,2},{4,5},{5,4},{6,7},{7,6},{8,9},{9,8},{10,11... | collective-permute-start | bytes 2359304 | tf_op jit(solution)/shard_map/ppermute | solution.py:310
  60.2 4.6 %all-to-all-start.1 = ((bf16[16,8,384]{2,1,0:T(8,128)(2,1)}), bf16[16,8,384]{2,1,0:T(8,128)(2,1)S(1)}, u32[]{:S(2)}, u32[]{:S(2)}) async-start(bf16[16,8,384]{2,1,0:T(8,128)(2,1)} %project.1), calls=%async_computation.1 | async-start | bytes 196608 | tf_op jit(solution)/shard_map/all_to_all | solution.py:312
  64.8 0.0 collective-permute-done.2.other
  64.8 2.7 %prefill.1 = (bf16[128,768]{1,0:T(8,128)(2,1)}, bf16[64,2560]{1,0:T(8,128)(2,1)}, bf16[64,2560]{1,0:T(8,128)(2,1)}, bf16[32,128]{1,0:T(8,128)(2,1)S(1)}) custom-call(s32[4]{0:T(128)S(1)} %copy-done.6, s32[32,128]{1,0:T(8,128)S(1)} %bitcast.14, bf16[128,768]{1,0:T(8,128)(2,1)S(1)} %copy-done.1, bf16[2,2,4,128,128]{4,3,2,1,0:T(8,128)(2,1)S(1)} %bitcast.12, ...), custom_call_target="tpu_custom_call" | custom-call | flops 1000000 | bytes 100000 | tf_op jit(solution)/shard_map/prefill/pallas_call | solution.py:269
  67.5 3.2 %all-to-all-done.1 = bf16[16,8,384]{2,1,0:T(8,128)(2,1)S(1)} async-done(((bf16[16,8,384]{2,1,0:T(8,128)(2,1)}), bf16[16,8,384]{2,1,0:T(8,128)(2,1)S(1)}, u32[]{:S(2)}, u32[]{:S(2)}) %all-to-all-start.1) | async-done | bytes 98336 | tf_op jit(solution)/shard_map/all_to_all | solution.py:312
  70.7 0.7 %convolution_convert_fusion = bf16[32,384]{1,0:T(8,128)(2,1)} fusion(bf16[32,128]{1,0:T(8,128)(2,1)S(1)} %get-tuple-element.14, bf16[16,8,384]{2,1,0:T(8,128)(2,1)S(1)} %all-to-all-done.1), kind=kOutput, calls=%fused_computation | convolution fusion | flops 3158016 | bytes 131072 | tf_op jit(solution)/shard_map/dot_general | solution.py:314
  (9 shorter events, 0.0 us)
Async XLA Ops:
  26.1 18.2 %copy-start.2 = (s32[4096]{0:T(1024)S(1)}, s32[4096]{0:T(1024)}, u32[]{:S(2)}) copy-start(s32[4096]{0:T(1024)} %param.12) | copy-start | bytes 49156
  26.1 18.2 %copy-start.3 = (bf16[4,768]{1,0:T(4,128)(2,1)S(1)}, bf16[4,768]{1,0:T(4,128)(2,1)}, u32[]{:S(2)}) copy-start(bf16[4,768]{1,0:T(4,128)(2,1)} %step_query.3) | copy-start | bytes 18436
  38.4 16.9 %collective-permute-start = (bf16[2,2,4,128,128]{4,3,2,1,0:T(8,128)(2,1)S(1)}, bf16[2,2,4,128,128]{4,3,2,1,0:T(8,128)(2,1)S(1)}, u32[]{:S(2)}, u32[]{:S(2)}) collective-permute-start(bf16[2,2,4,128,128]{4,3,2,1,0:T(8,128)(2,1)S(1)} %bitcast.9), channel_id=1, source_target_pairs={{16,0},{241,1},{18,2},{243,3},{20,4},{245,5},{22,6},{247,7},{24,8}... | collective-permute-start | bytes 1572872 | tf_op jit(solution)/shard_map/ppermute | solution.py:297
  41.1 13.3 %copy-start = (bf16[768,384]{1,0:T(8,128)(2,1)S(1)}, bf16[768,384]{1,0:T(8,128)(2,1)}, u32[]{:S(2)}) copy-start(bf16[768,384]{1,0:T(8,128)(2,1)} %weight.1) | copy-start | bytes 1769476
  41.1 14.2 %collective-permute-start.1 = (bf16[1,2,4,128,128]{4,3,2,1,0:T(8,128)(2,1)S(1)}, bf16[1,2,4,128,128]{4,3,2,1,0:T(8,128)(2,1)S(1)}, u32[]{:S(2)}, u32[]{:S(2)}) collective-permute-start(bf16[1,2,4,128,128]{4,3,2,1,0:T(8,128)(2,1)S(1)} %constant_dynamic-slice_fusion), channel_id=1, source_target_pairs={{32,0},{225,1},{34,2},{227,3},{36,4},{229,5},{38,6},{231,7},{40,8}... | collective-permute-start | bytes 786440 | tf_op jit(solution)/shard_map/ppermute | solution.py:297
  44.8 9.5 %copy-start.4 = (bf16[4,1024]{1,0:T(4,128)(2,1)S(1)}, bf16[4,1024]{1,0:T(4,128)(2,1)}, u32[]{:S(2)}) copy-start(bf16[4,1024]{1,0:T(4,128)(2,1)} %step_key.1) | copy-start | bytes 24580
  44.8 9.5 %copy-start.5 = (bf16[4,1024]{1,0:T(4,128)(2,1)S(1)}, bf16[4,1024]{1,0:T(4,128)(2,1)}, u32[]{:S(2)}) copy-start(bf16[4,1024]{1,0:T(4,128)(2,1)} %step_value.1) | copy-start | bytes 24580
  55.3 9.5 %copy-start.6 = (s32[4]{0:T(128)S(1)}, s32[4]{0:T(128)}, u32[]{:S(2)}) copy-start(s32[4]{0:T(128)} %replica_of.1) | copy-start | bytes 52
  55.4 9.4 %copy-start.1 = (bf16[128,768]{1,0:T(8,128)(2,1)S(1)}, bf16[128,768]{1,0:T(8,128)(2,1)}, u32[]{:S(2)}) copy-start(bf16[128,768]{1,0:T(8,128)(2,1)} %queries.1) | copy-start | bytes 589828
  55.4 9.4 %collective-permute-start.2 = (bf16[3,2,4,128,128]{4,3,2,1,0:T(8,128)(2,1)S(1)}, bf16[3,2,4,128,128]{4,3,2,1,0:T(8,128)(2,1)S(1)}, u32[]{:S(2)}, u32[]{:S(2)}) collective-permute-start(bf16[3,2,4,128,128]{4,3,2,1,0:T(8,128)(2,1)S(1)} %pad_maximum_fusion), channel_id=1, source_target_pairs={{0,1},{1,0},{2,3},{3,2},{4,5},{5,4},{6,7},{7,6},{8,9},{9,8},{10,11... | collective-permute-start | bytes 2359304 | tf_op jit(solution)/shard_map/ppermute | solution.py:310
  60.2 10.5 %all-to-all-start.1 = ((bf16[16,8,384]{2,1,0:T(8,128)(2,1)}), bf16[16,8,384]{2,1,0:T(8,128)(2,1)S(1)}, u32[]{:S(2)}, u32[]{:S(2)}) async-start(bf16[16,8,384]{2,1,0:T(8,128)(2,1)} %project.1), calls=%async_computation.1 | async-start | bytes 196608 | tf_op jit(solution)/shard_map/all_to_all | solution.py:312

commit v6 on v5

--- a/solution.py
+++ b/solution.py
@@ -167,7 +167,7 @@
 
 
 def prefill_kernel(
-    replica_of, doc_ids, queries, far, near, across, other,
+    replica_of, doc_ids, queries, far, near, across, other0, other1,
     context, replica_keys, replica_values, hot,
     cache, flat, acc,
 ):
@@ -179,10 +179,8 @@
                 at = yh * 16 + g * 4
                 cache[which, at + z0] = far[yh, which, g]
                 cache[which, at + lax.rem(z0 + 4 + side, 4)] = near[yh, which, g]
-                cache[which, at + lax.rem(z0 + 4 - side, 4)] = other[yh, which, g]
-            at = g * 4 + lax.rem(z0 + 2, 4)
-            cache[which, at + core * 16] = across[0, which, g]
-            cache[which, at + (1 - core) * 16] = other[2, which, g]
+                cache[which, at + lax.rem(z0 + 4 - side, 4)] = (other0, other1)[yh][1 - core, which, g]
+                cache[which, at + lax.rem(z0 + 2, 4)] = across[yh, which, g]
         for b in range(NB, NB + STEP - 1):
             cache[which, b] = jnp.zeros((ROWS, HD), jnp.bfloat16)
     starts, ends = doc_bounds(doc_ids)
@@ -274,7 +272,7 @@
             jax.ShapeDtypeStruct((HD // 2, MOST), jnp.bfloat16),
             jax.ShapeDtypeStruct((NB, 16 * 8), jnp.bfloat16),
         ),
-        in_specs=[pl.BlockSpec(memory_space=pltpu.SMEM)] + [vmem] * 6,
+        in_specs=[pl.BlockSpec(memory_space=pltpu.SMEM)] + [vmem] * 7,
         scratch_shapes=[
             pltpu.VMEM((2, NB + STEP - 1, ROWS, HD), jnp.bfloat16),
             pltpu.VMEM((HEADS * ROWS, HD), jnp.bfloat16),
@@ -301,15 +299,16 @@
     half = lax.all_gather(pick(keys, values), "z1", axis=0)
     far = lax.all_gather(half, ("yh", "c"), axis=0).reshape(2, 2, 4, ROWS, HD)
     near = from_sides(far, 1)
+    blocks = doc_ids.reshape(NB, ROWS)
+    part = class_part(blocks, step_query, far)
+    decoded = lax.all_to_all(jnp.broadcast_to(part[None], (4, PAD, HD)), "z0", 0, 0)
     across = from_sides(lax.dynamic_slice_in_dim(far, lax.axis_index("c"), 1, 0), 2)
-    blocks = doc_ids.reshape(NB, ROWS)
-    decoded = lax.all_to_all(jnp.broadcast_to(class_part(blocks, step_query, far)[None], (4, PAD, HD)), "z0", 0, 0)
     terms = project(decoded, step_query, step_key, step_value, out_weight)
-    near, across, terms = lax.optimization_barrier((near, across, terms))
-    both = jnp.concatenate((near, across), axis=0)
-    other = lax.ppermute(both, "c", [(0, 1), (1, 0)])
-    parts = [far, near, across, other]
+    others = [lax.all_gather(near[yh], "c", axis=0) for yh in range(2)]
     summed = lax.all_to_all(terms, TP, 0, 0)
+    across, *others = lax.optimization_barrier((across, *others))
+    across, summed = lax.optimization_barrier((lax.all_gather(across[0], "c", axis=0), summed))
+    parts = [far, near, across, *others]
     context, replica_keys, replica_values, hot = prefill(replica_of, blocks, queries, parts)
     next_hidden = jnp.dot(hot, summed.reshape(16 * 8, -1), preferred_element_type=jnp.float32).astype(jnp.bfloat16)
     return (context, next_hidden, replica_keys[None], replica_values[None])

time: 71.9 us -> 69.3 us (0.964)
  the two profiles are of different devices: /device:TPU:1 before, /device:TPU:57 now
where the time goes in v6:
time: 69.3 us; the launch traced here: 68.8 us
  blocking collectives  40.5 us (58%)
  starting transfers between devices  18.2 us (26%)
  Pallas kernels  7.89 us (11%)
  matrix products  0.75 us (1%)
  between operations  0.74 us (1%)
  local copies, waits for them, and re-layouts  0.73 us (1%)
    all_gather x1, blocking collectives, local(): half = lax.all_gather(pick(keys, values), 'z1', axis=0)  22.4 us
    all_gather x1, blocking collectives, local(): far = lax.all_gather(half, ('yh', 'c'), axis=0).reshape(2, 2, 4, ROWS, HD)  11.4 us
    all_to_all x1, starting transfers between devices, local(): summed = lax.all_to_all(terms, TP, 0, 0)  7.63 us
    ppermute x2, starting transfers between devices, from_sides(): return lax.ppermute(a, CTX + TP, pairs)  6.63 us
    pallas_call x1, Pallas kernels, prefill(): pl.pallas_call(prefill_kernel, out_shape=(jax.ShapeDtypeStruct((ROWS, HEA...  5.12 us
    all_gather x2, blocking collectives, local(): others = [lax.all_gather(near[yh], 'c', axis=0) for yh in range(2)]  4.35 us
    all_to_all x1, starting transfers between devices, local(): lax.all_to_all(jnp.broadcast_to(part[None], (4, PAD, HD)), 'z0', 0, 0)  3.98 us
    all_gather x1, blocking collectives, local(): lax.all_gather(across[0], 'c', axis=0)  2.31 us
  transfers between devices with their start and end apart: 4, of which 0 were waited for; matrix products, arithmetic and copies ran while one was open for 1% of the time, Pallas kernels for 2%

profile of v6, /device:TPU:57, one launch (start us, length us, event | category | flops | bytes accessed | tf_op | source)
XLA Modules:
  0.0 68.8 jit_solution(8987768832069556470)
XLA Ops:
  0.6 1.4 %pick.1 = bf16[128,128]{1,0:T(8,128)(2,1)} custom-call(bf16[128,1024]{1,0:T(8,128)(2,1)} %keys.1, bf16[128,1024]{1,0:T(8,128)(2,1)} %values.1), custom_call_target="tpu_custom_call" | custom-call | tf_op jit(solution)/shard_map/pick/pallas_call | solution.py:45
  2.0 22.4 %all-gather = bf16[512,128]{1,0:T(8,128)(2,1)S(1)} all-gather(bf16[128,128]{1,0:T(8,128)(2,1)} %pick.1), channel_id=2, replica_groups=mesh['yh'=2,'z1'=4,'z0'=4,'x'=4,'yl'=2,'c'=2] {'z1'}, dimensions={0}, use_global_device_ids=true | all-gather | bytes 163840 | tf_op jit(solution)/shard_map/all_gather | solution.py:299
  24.4 11.4 %all-gather.1 = bf16[16,128,128]{2,1,0:T(8,128)(2,1)S(1)} all-gather(bf16[4,128,128]{2,1,0:T(8,128)(2,1)S(1)} %bitcast.15), channel_id=3, replica_groups=mesh['yh'=2,'z1'=4,'z0'=4,'x'=4,'yl'=2,'c'=2] {'yh','c'}, dimensions={0}, use_global_device_ids=true | all-gather | bytes 655360 | tf_op jit(solution)/shard_map/all_gather | solution.py:300
  35.8 2.6 %collective-permute-start = (bf16[2,2,4,128,128]{4,3,2,1,0:T(8,128)(2,1)S(1)}, bf16[2,2,4,128,128]{4,3,2,1,0:T(8,128)(2,1)S(1)}, u32[]{:S(2)}, u32[]{:S(2)}) collective-permute-start(bf16[2,2,4,128,128]{4,3,2,1,0:T(8,128)(2,1)S(1)} %bitcast.9), channel_id=1, source_target_pairs={{16,0},{241,1},{18,2},{243,3},{20,4},{245,5},{22,6},{247,7},{24,8}... | collective-permute-start | bytes 1572872 | tf_op jit(solution)/shard_map/ppermute | solution.py:295
  38.5 0.0 copy-done.2
  38.5 0.0 copy-done.3
  38.5 0.0 copy-start
  38.5 0.4 class_part.1
  38.9 0.6 broadcast_in_dim.12
  39.6 4.0 %all-to-all-start = ((f32[4,32,128]{2,1,0:T(8,128)}), f32[4,32,128]{2,1,0:T(8,128)S(1)}, u32[]{:S(2)}, u32[]{:S(2)}) async-start(f32[4,32,128]{2,1,0:T(8,128)} %broadcast_in_dim.12), calls=%async_computation | async-start | bytes 131072 | tf_op jit(solution)/shard_map/all_to_all | solution.py:304
  43.6 4.0 %collective-permute-start.1 = (bf16[1,2,4,128,128]{4,3,2,1,0:T(8,128)(2,1)S(1)}, bf16[1,2,4,128,128]{4,3,2,1,0:T(8,128)(2,1)S(1)}, u32[]{:S(2)}, u32[]{:S(2)}) collective-permute-start(bf16[1,2,4,128,128]{4,3,2,1,0:T(8,128)(2,1)S(1)} %constant_dynamic-slice_fusion), channel_id=1, source_target_pairs={{32,0},{225,1},{34,2},{227,3},{36,4},{229,5},{38,6},{231,7},{40,8}... | collective-permute-start | bytes 786440 | tf_op jit(solution)/shard_map/ppermute | solution.py:295
  47.6 0.0 all-to-all-done.parts
  47.6 0.0 copy-done
  47.6 0.0 copy-done.4
  47.6 0.9 %project.1 = bf16[16,8,384]{2,1,0:T(8,128)(2,1)} custom-call(f32[4,32,128]{2,1,0:T(8,128)S(1)} %all-to-all-done.parts, bf16[4,768]{1,0:T(4,128)(2,1)S(1)} %copy-done.3, bf16[4,1024]{1,0:T(4,128)(2,1)S(1)} %copy-done.4, bf16[4,1024]{1,0:T(4,128)(2,1)S(1)} %copy-done.5, bf16[768,384]{1,0:T(8,128)(2,1)S(1)} %copy-done), custom_call_target="tpu_custom_call" | custom-call | flops 10000000 | bytes 1000000 | tf_op jit(solution)/shard_map/project/pallas_call | solution.py:156
  48.6 7.6 %all-to-all-start.1 = ((bf16[16,8,384]{2,1,0:T(8,128)(2,1)}), bf16[16,8,384]{2,1,0:T(8,128)(2,1)S(1)}, u32[]{:S(2)}, u32[]{:S(2)}) async-start(bf16[16,8,384]{2,1,0:T(8,128)(2,1)} %project.1), calls=%async_computation.1 | async-start | bytes 196608 | tf_op jit(solution)/shard_map/all_to_all | solution.py:308
  56.2 0.0 collective-permute-done.near
  56.3 2.2 %all_gather.26.other1 = bf16[2,2,4,128,128]{4,3,2,1,0:T(8,128)(2,1)S(1)} all-gather(bf16[1,2,4,128,128]{4,3,2,1,0:T(8,128)(2,1)S(1)} %get-tuple-element.22), channel_id=1, replica_groups=mesh['yh'=2,'z1'=4,'z0'=4,'x'=4,'yl'=2,'c'=2] {'c'}, dimensions={0}, use_global_device_ids=true | all-gather | bytes 786432 | tf_op jit(solution)/shard_map/all_gather | solution.py:307
  58.4 2.2 %all_gather.25.other0 = bf16[2,2,4,128,128]{4,3,2,1,0:T(8,128)(2,1)S(1)} all-gather(bf16[1,2,4,128,128]{4,3,2,1,0:T(8,128)(2,1)S(1)} %get-tuple-element.23), channel_id=1, replica_groups=mesh['yh'=2,'z1'=4,'z0'=4,'x'=4,'yl'=2,'c'=2] {'c'}, dimensions={0}, use_global_device_ids=true | all-gather | bytes 786432 | tf_op jit(solution)/shard_map/all_gather | solution.py:307
  60.6 0.0 collective-permute-done.1
  60.6 2.3 %all_gather.27.across = bf16[2,2,4,128,128]{4,3,2,1,0:T(8,128)(2,1)S(1)} all-gather(bf16[1,2,4,128,128]{4,3,2,1,0:T(8,128)(2,1)S(1)} %collective-permute-done.1), channel_id=1, replica_groups=mesh['yh'=2,'z1'=4,'z0'=4,'x'=4,'yl'=2,'c'=2] {'c'}, dimensions={0}, use_global_device_ids=true | all-gather | bytes 786432 | tf_op jit(solution)/shard_map/all_gather | solution.py:310
  62.9 0.0 all-to-all-done.1
  62.9 5.1 %prefill.1 = (bf16[128,768]{1,0:T(8,128)(2,1)}, bf16[64,2560]{1,0:T(8,128)(2,1)}, bf16[64,2560]{1,0:T(8,128)(2,1)}, bf16[32,128]{1,0:T(8,128)(2,1)S(1)}) custom-call(s32[4]{0:T(128)S(1)} %copy-done.6, s32[32,128]{1,0:T(8,128)S(1)} %bitcast.14, bf16[128,768]{1,0:T(8,128)(2,1)S(1)} %copy-done.1, bf16[2,2,4,128,128]{4,3,2,1,0:T(8,128)(2,1)S(1)} %bitcast.12, ...), custom_call_target="tpu_custom_call" | custom-call | flops 1000000 | bytes 100000 | tf_op jit(solution)/shard_map/prefill/pallas_call | solution.py:267
  68.1 0.7 %convolution_convert_fusion = bf16[32,384]{1,0:T(8,128)(2,1)} fusion(bf16[32,128]{1,0:T(8,128)(2,1)S(1)} %get-tuple-element.18, bf16[16,8,384]{2,1,0:T(8,128)(2,1)S(1)} %all-to-all-done.1), kind=kOutput, calls=%fused_computation | convolution fusion | flops 3158016 | bytes 131072 | tf_op jit(solution)/shard_map/dot_general | solution.py:313
  (11 shorter events, 0.1 us)
Async XLA Ops:
  24.4 14.1 %copy-start.2 = (s32[4096]{0:T(1024)S(1)}, s32[4096]{0:T(1024)}, u32[]{:S(2)}) copy-start(s32[4096]{0:T(1024)} %param.12) | copy-start | bytes 49156
  24.4 14.1 %copy-start.3 = (bf16[4,768]{1,0:T(4,128)(2,1)S(1)}, bf16[4,768]{1,0:T(4,128)(2,1)}, u32[]{:S(2)}) copy-start(bf16[4,768]{1,0:T(4,128)(2,1)} %step_query.3) | copy-start | bytes 18436
  35.8 20.4 %collective-permute-start = (bf16[2,2,4,128,128]{4,3,2,1,0:T(8,128)(2,1)S(1)}, bf16[2,2,4,128,128]{4,3,2,1,0:T(8,128)(2,1)S(1)}, u32[]{:S(2)}, u32[]{:S(2)}) collective-permute-start(bf16[2,2,4,128,128]{4,3,2,1,0:T(8,128)(2,1)S(1)} %bitcast.9), channel_id=1, source_target_pairs={{16,0},{241,1},{18,2},{243,3},{20,4},{245,5},{22,6},{247,7},{24,8}... | collective-permute-start | bytes 1572872 | tf_op jit(solution)/shard_map/ppermute | solution.py:295
  38.5 9.1 %copy-start = (bf16[768,384]{1,0:T(8,128)(2,1)S(1)}, bf16[768,384]{1,0:T(8,128)(2,1)}, u32[]{:S(2)}) copy-start(bf16[768,384]{1,0:T(8,128)(2,1)} %weight.1) | copy-start | bytes 1769476
  39.6 8.0 %all-to-all-start = ((f32[4,32,128]{2,1,0:T(8,128)}), f32[4,32,128]{2,1,0:T(8,128)S(1)}, u32[]{:S(2)}, u32[]{:S(2)}) async-start(f32[4,32,128]{2,1,0:T(8,128)} %broadcast_in_dim.12), calls=%async_computation | async-start | bytes 131072 | tf_op jit(solution)/shard_map/all_to_all | solution.py:304
  43.6 4.1 %copy-start.4 = (bf16[4,1024]{1,0:T(4,128)(2,1)S(1)}, bf16[4,1024]{1,0:T(4,128)(2,1)}, u32[]{:S(2)}) copy-start(bf16[4,1024]{1,0:T(4,128)(2,1)} %step_key.1) | copy-start | bytes 24580
  43.6 4.1 %copy-start.5 = (bf16[4,1024]{1,0:T(4,128)(2,1)S(1)}, bf16[4,1024]{1,0:T(4,128)(2,1)}, u32[]{:S(2)}) copy-start(bf16[4,1024]{1,0:T(4,128)(2,1)} %step_value.1) | copy-start | bytes 24580
  43.6 17.0 %collective-permute-start.1 = (bf16[1,2,4,128,128]{4,3,2,1,0:T(8,128)(2,1)S(1)}, bf16[1,2,4,128,128]{4,3,2,1,0:T(8,128)(2,1)S(1)}, u32[]{:S(2)}, u32[]{:S(2)}) collective-permute-start(bf16[1,2,4,128,128]{4,3,2,1,0:T(8,128)(2,1)S(1)} %constant_dynamic-slice_fusion), channel_id=1, source_target_pairs={{32,0},{225,1},{34,2},{227,3},{36,4},{229,5},{38,6},{231,7},{40,8}... | collective-permute-start | bytes 786440 | tf_op jit(solution)/shard_map/ppermute | solution.py:295
  48.6 14.4 %all-to-all-start.1 = ((bf16[16,8,384]{2,1,0:T(8,128)(2,1)}), bf16[16,8,384]{2,1,0:T(8,128)(2,1)S(1)}, u32[]{:S(2)}, u32[]{:S(2)}) async-start(bf16[16,8,384]{2,1,0:T(8,128)(2,1)} %project.1), calls=%async_computation.1 | async-start | bytes 196608 | tf_op jit(solution)/shard_map/all_to_all | solution.py:308
  60.6 2.3 %copy-start.1 = (bf16[128,768]{1,0:T(8,128)(2,1)S(1)}, bf16[128,768]{1,0:T(8,128)(2,1)}, u32[]{:S(2)}) copy-start(bf16[128,768]{1,0:T(8,128)(2,1)} %queries.1) | copy-start | bytes 589828
  60.6 2.3 %copy-start.6 = (s32[4]{0:T(128)S(1)}, s32[4]{0:T(128)}, u32[]{:S(2)}) copy-start(s32[4]{0:T(128)} %replica_of.1) | copy-start | bytes 52

commit v7 on v6

--- a/solution.py
+++ b/solution.py
@@ -111,13 +111,15 @@
     sub = lax.broadcasted_iota(jnp.int32, (PAD, HD), 0)
     lane = lax.broadcasted_iota(jnp.int32, (PAD, HD), 1)
     line = jnp.sum(jnp.where(sub == lane, weight, 0.0), axis=0, keepdims=True)
-    out[...] = jnp.where(sub == ROW, line, mixed / safe)
+    part = jnp.where(sub == ROW, line, mixed / safe)
+    for k in range(out.shape[0]):
+        out[k] = part
 
 
 def class_part(doc_ids, step_query, far):
     return pl.pallas_call(
         class_part_kernel,
-        out_shape=jax.ShapeDtypeStruct((PAD, HD), jnp.float32),
+        out_shape=jax.ShapeDtypeStruct((4, PAD, HD), jnp.float32),
         scratch_shapes=[pltpu.VMEM((PAD, HD), jnp.float32)],
         compiler_params=pltpu.CompilerParams(vmem_limit_bytes=8 * 1024 * 1024),
         cost_estimate=pl.CostEstimate(flops=3 * 10**7, bytes_accessed=10**6, transcendentals=4 * 10**4),
@@ -163,12 +165,12 @@
     )(parts, step_query, step_key, step_value, weight)
 
 
-STEP = 4
+STEP = 6
 
 
 def prefill_kernel(
-    replica_of, doc_ids, queries, far, near, across, other0, other1,
-    context, replica_keys, replica_values, hot,
+    replica_of, doc_ids, queries, summed, far, near, across, other0, other1,
+    context, next_hidden, replica_keys, replica_values,
     cache, flat, acc,
 ):
     ctx, core, _, z0 = position()
@@ -223,12 +225,12 @@
     for h in range(HEADS):
         context[:, h * HD : (h + 1) * HD] = jnp.transpose(mixed[:, h * ROWS : (h + 1) * ROWS]).astype(jnp.bfloat16)
 
-    replica = lax.broadcasted_iota(jnp.int32, hot.shape, 0)
-    document = lax.broadcasted_iota(jnp.int32, hot.shape, 1) % 8
-    found = jnp.zeros(hot.shape, jnp.float32)
+    projected = jnp.sum(summed[...].astype(jnp.float32), axis=0)
+    replica = lax.broadcasted_iota(jnp.int32, next_hidden.shape, 0)
+    rows = jnp.zeros(next_hidden.shape, jnp.float32)
     for d in range(NDOC):
-        found = jnp.where((document == d) & (replica == replica_of[d]), 1.0, found)
-    hot[...] = found.astype(hot.dtype)
+        rows = jnp.where(replica == replica_of[d], projected[d : d + 1], rows)
+    next_hidden[...] = rows.astype(jnp.bfloat16)
 
     asked = jnp.int32(0)
     start = jnp.int32(0)
@@ -262,17 +264,17 @@
                 out[:, i * ROWS : (i + 1) * ROWS] = jnp.where(live, moved, 0.0).astype(jnp.bfloat16)
 
 
-def prefill(replica_of, doc_ids, queries, parts):
+def prefill(replica_of, doc_ids, queries, summed, parts):
     vmem = pl.BlockSpec(memory_space=pltpu.VMEM)
     return pl.pallas_call(
         prefill_kernel,
         out_shape=(
             jax.ShapeDtypeStruct((ROWS, HEADS * HD), jnp.bfloat16),
+            jax.ShapeDtypeStruct((NB, summed.shape[2]), jnp.bfloat16),
             jax.ShapeDtypeStruct((HD // 2, MOST), jnp.bfloat16),
             jax.ShapeDtypeStruct((HD // 2, MOST), jnp.bfloat16),
-            jax.ShapeDtypeStruct((NB, 16 * 8), jnp.bfloat16),
         ),
-        in_specs=[pl.BlockSpec(memory_space=pltpu.SMEM)] + [vmem] * 7,
+        in_specs=[pl.BlockSpec(memory_space=pltpu.SMEM)] + [vmem] * 8,
         scratch_shapes=[
             pltpu.VMEM((2, NB + STEP - 1, ROWS, HD), jnp.bfloat16),
             pltpu.VMEM((HEADS * ROWS, HD), jnp.bfloat16),
@@ -281,7 +283,7 @@
         compiler_params=pltpu.CompilerParams(vmem_limit_bytes=16 * 1024 * 1024),
         cost_estimate=pl.CostEstimate(flops=10**6, bytes_accessed=10**5, transcendentals=10**3),
         name="prefill",
-    )(replica_of, doc_ids, queries, *parts)
+    )(replica_of, doc_ids, queries, summed, *parts)
 
 
 def from_sides(a, by):
@@ -300,8 +302,7 @@
     far = lax.all_gather(half, ("yh", "c"), axis=0).reshape(2, 2, 4, ROWS, HD)
     near = from_sides(far, 1)
     blocks = doc_ids.reshape(NB, ROWS)
-    part = class_part(blocks, step_query, far)
-    decoded = lax.all_to_all(jnp.broadcast_to(part[None], (4, PAD, HD)), "z0", 0, 0)
+    decoded = lax.all_to_all(class_part(blocks, step_query, far), "z0", 0, 0)
     across = from_sides(lax.dynamic_slice_in_dim(far, lax.axis_index("c"), 1, 0), 2)
     terms = project(decoded, step_query, step_key, step_value, out_weight)
     others = [lax.all_gather(near[yh], "c", axis=0) for yh in range(2)]
@@ -309,8 +310,7 @@
     across, *others = lax.optimization_barrier((across, *others))
     across, summed = lax.optimization_barrier((lax.all_gather(across[0], "c", axis=0), summed))
     parts = [far, near, across, *others]
-    context, replica_keys, replica_values, hot = prefill(replica_of, blocks, queries, parts)
-    next_hidden = jnp.dot(hot, summed.reshape(16 * 8, -1), preferred_element_type=jnp.float32).astype(jnp.bfloat16)
+    context, next_hidden, replica_keys, replica_values = prefill(replica_of, blocks, queries, summed, parts)
     return (context, next_hidden, replica_keys[None], replica_values[None])
 
 

time: 69.3 us -> 67.6 us (0.975)
  the two profiles are of different devices: /device:TPU:57 before, /device:TPU:1 now
where the time goes in v7:
time: 67.6 us; the launch traced here: 67.1 us
  blocking collectives  43 us (64%)
  starting transfers between devices  16.5 us (24%)
  Pallas kernels  6.35 us (9%)
  between operations  0.74 us (1%)
    all_gather x1, blocking collectives, local(): half = lax.all_gather(pick(keys, values), 'z1', axis=0)  24.1 us
    all_gather x1, blocking collectives, local(): far = lax.all_gather(half, ('yh', 'c'), axis=0).reshape(2, 2, 4, ROWS, HD)  12.3 us
    ppermute x2, starting transfers between devices, from_sides(): return lax.ppermute(a, CTX + TP, pairs)  6.83 us
    all_to_all x1, starting transfers between devices, local(): summed = lax.all_to_all(terms, TP, 0, 0)  6.38 us
    all_gather x2, blocking collectives, local(): others = [lax.all_gather(near[yh], 'c', axis=0) for yh in range(2)]  4.35 us
    all_to_all x1, starting transfers between devices, local(): decoded = lax.all_to_all(class_part(blocks, step_query, far), 'z0', 0, 0)  3.28 us
    pallas_call x1, Pallas kernels, prefill(): pl.pallas_call(prefill_kernel, out_shape=(jax.ShapeDtypeStruct((ROWS, HEA...  2.94 us
    all_gather x1, blocking collectives, local(): lax.all_gather(across[0], 'c', axis=0)  2.31 us
  transfers between devices with their start and end apart: 4, of which 1 were waited for; matrix products, arithmetic and copies ran while one was open for 0% of the time, Pallas kernels for 3%

profile of v7, /device:TPU:1, one launch (start us, length us, event | category | flops | bytes accessed | tf_op | source)
XLA Modules:
  0.0 67.1 jit_solution(858700019148151968)
XLA Ops:
  0.6 1.4 %pick.1 = bf16[128,128]{1,0:T(8,128)(2,1)} custom-call(bf16[128,1024]{1,0:T(8,128)(2,1)} %keys.1, bf16[128,1024]{1,0:T(8,128)(2,1)} %values.1), custom_call_target="tpu_custom_call" | custom-call | tf_op jit(solution)/shard_map/pick/pallas_call | solution.py:45
  2.0 24.1 %all-gather = bf16[512,128]{1,0:T(8,128)(2,1)S(1)} all-gather(bf16[128,128]{1,0:T(8,128)(2,1)} %pick.1), channel_id=2, replica_groups=mesh['yh'=2,'z1'=4,'z0'=4,'x'=4,'yl'=2,'c'=2] {'z1'}, dimensions={0}, use_global_device_ids=true | all-gather | bytes 163840 | tf_op jit(solution)/shard_map/all_gather | solution.py:301
  26.1 12.3 %all-gather.1 = bf16[16,128,128]{2,1,0:T(8,128)(2,1)S(1)} all-gather(bf16[4,128,128]{2,1,0:T(8,128)(2,1)S(1)} %bitcast.11), channel_id=3, replica_groups=mesh['yh'=2,'z1'=4,'z0'=4,'x'=4,'yl'=2,'c'=2] {'yh','c'}, dimensions={0}, use_global_device_ids=true | all-gather | bytes 655360 | tf_op jit(solution)/shard_map/all_gather | solution.py:302
  38.4 2.6 %collective-permute-start.1 = (bf16[2,2,4,128,128]{4,3,2,1,0:T(8,128)(2,1)S(1)}, bf16[2,2,4,128,128]{4,3,2,1,0:T(8,128)(2,1)S(1)}, u32[]{:S(2)}, u32[]{:S(2)}) collective-permute-start(bf16[2,2,4,128,128]{4,3,2,1,0:T(8,128)(2,1)S(1)} %bitcast.5), channel_id=1, source_target_pairs={{16,0},{241,1},{18,2},{243,3},{20,4},{245,5},{22,6},{247,7},{24,8}... | collective-permute-start | bytes 1572872 | tf_op jit(solution)/shard_map/ppermute | solution.py:297
  41.1 0.0 copy-done.2
  41.1 0.0 copy-done.3
  41.1 0.0 copy-start
  41.1 1.1 %class_part.1 = f32[4,32,128]{2,1,0:T(8,128)} custom-call(s32[32,128]{1,0:T(8,128)S(1)} %bitcast.9, bf16[4,768]{1,0:T(4,128)(2,1)S(1)} %copy-done.3, bf16[2,2,4,128,128]{4,3,2,1,0:T(8,128)(2,1)S(1)} %bitcast.6), custom_call_target="tpu_custom_call" | custom-call | flops 30000000 | bytes 1000000 | tf_op jit(solution)/shard_map/class_part/pallas_call | solution.py:120
  42.2 3.3 %all-to-all-start = ((f32[4,32,128]{2,1,0:T(8,128)}), f32[4,32,128]{2,1,0:T(8,128)S(1)}, u32[]{:S(2)}, u32[]{:S(2)}) async-start(f32[4,32,128]{2,1,0:T(8,128)} %class_part.1), calls=%async_computation | async-start | bytes 131072 | tf_op jit(solution)/shard_map/all_to_all | solution.py:305
  45.5 0.0 copy-start.4
  45.5 0.0 copy-start.5
  45.5 4.2 %collective-permute-start = (bf16[1,2,4,128,128]{4,3,2,1,0:T(8,128)(2,1)S(1)}, bf16[1,2,4,128,128]{4,3,2,1,0:T(8,128)(2,1)S(1)}, u32[]{:S(2)}, u32[]{:S(2)}) collective-permute-start(bf16[1,2,4,128,128]{4,3,2,1,0:T(8,128)(2,1)S(1)} %constant_dynamic-slice_fusion), channel_id=1, source_target_pairs={{32,0},{225,1},{34,2},{227,3},{36,4},{229,5},{38,6},{231,7},{40,8}... | collective-permute-start | bytes 786440 | tf_op jit(solution)/shard_map/ppermute | solution.py:297
  49.7 0.3 all-to-all-done.parts
  50.1 0.0 copy-done
  50.1 0.0 copy-done.5
  50.1 0.9 %project.1 = bf16[16,8,384]{2,1,0:T(8,128)(2,1)} custom-call(f32[4,32,128]{2,1,0:T(8,128)S(1)} %all-to-all-done.parts, bf16[4,768]{1,0:T(4,128)(2,1)S(1)} %copy-done.3, bf16[4,1024]{1,0:T(4,128)(2,1)S(1)} %copy-done.4, bf16[4,1024]{1,0:T(4,128)(2,1)S(1)} %copy-done.5, bf16[768,384]{1,0:T(8,128)(2,1)S(1)} %copy-done), custom_call_target="tpu_custom_call" | custom-call | flops 10000000 | bytes 1000000 | tf_op jit(solution)/shard_map/project/pallas_call | solution.py:158
  51.0 6.4 %all-to-all-start.1 = ((bf16[16,8,384]{2,1,0:T(8,128)(2,1)}), bf16[16,8,384]{2,1,0:T(8,128)(2,1)S(1)}, u32[]{:S(2)}, u32[]{:S(2)}) async-start(bf16[16,8,384]{2,1,0:T(8,128)(2,1)} %project.1), calls=%async_computation.1 | async-start | bytes 196608 | tf_op jit(solution)/shard_map/all_to_all | solution.py:309
  57.4 0.0 collective-permute-done.1.near
  57.4 2.2 %all_gather.26.other1 = bf16[2,2,4,128,128]{4,3,2,1,0:T(8,128)(2,1)S(1)} all-gather(bf16[1,2,4,128,128]{4,3,2,1,0:T(8,128)(2,1)S(1)} %get-tuple-element.22), channel_id=1, replica_groups=mesh['yh'=2,'z1'=4,'z0'=4,'x'=4,'yl'=2,'c'=2] {'c'}, dimensions={0}, use_global_device_ids=true | all-gather | bytes 786432 | tf_op jit(solution)/shard_map/all_gather | solution.py:308
  59.6 2.2 %all_gather.25.other0 = bf16[2,2,4,128,128]{4,3,2,1,0:T(8,128)(2,1)S(1)} all-gather(bf16[1,2,4,128,128]{4,3,2,1,0:T(8,128)(2,1)S(1)} %get-tuple-element.23), channel_id=1, replica_groups=mesh['yh'=2,'z1'=4,'z0'=4,'x'=4,'yl'=2,'c'=2] {'c'}, dimensions={0}, use_global_device_ids=true | all-gather | bytes 786432 | tf_op jit(solution)/shard_map/all_gather | solution.py:308
  61.8 0.0 collective-permute-done
  61.8 2.3 %all_gather.27.across = bf16[2,2,4,128,128]{4,3,2,1,0:T(8,128)(2,1)S(1)} all-gather(bf16[1,2,4,128,128]{4,3,2,1,0:T(8,128)(2,1)S(1)} %collective-permute-done), channel_id=1, replica_groups=mesh['yh'=2,'z1'=4,'z0'=4,'x'=4,'yl'=2,'c'=2] {'c'}, dimensions={0}, use_global_device_ids=true | all-gather | bytes 786432 | tf_op jit(solution)/shard_map/all_gather | solution.py:311
  64.1 0.0 all-to-all-done.1.summed
  64.1 2.9 %prefill.1 = (bf16[128,768]{1,0:T(8,128)(2,1)}, bf16[32,384]{1,0:T(8,128)(2,1)}, bf16[64,2560]{1,0:T(8,128)(2,1)}, bf16[64,2560]{1,0:T(8,128)(2,1)}) custom-call(s32[4]{0:T(128)S(1)} %copy-done.6, s32[32,128]{1,0:T(8,128)S(1)} %bitcast.10, bf16[128,768]{1,0:T(8,128)(2,1)S(1)} %copy-done.1, bf16[16,8,384]{2,1,0:T(8,128)(2,1)S(1)} %all-to-all-done.1.summed, ...), custom_call_target="tpu_custom_call" | custom-call | flops 1000000 | bytes 100000 | tf_op jit(solution)/shard_map/prefill/pallas_call | solution.py:269
  (9 shorter events, 0.1 us)
Async XLA Ops:
  26.1 14.9 %copy-start.2 = (s32[4096]{0:T(1024)S(1)}, s32[4096]{0:T(1024)}, u32[]{:S(2)}) copy-start(s32[4096]{0:T(1024)} %param.12) | copy-start | bytes 49156
  26.1 14.9 %copy-start.3 = (bf16[4,768]{1,0:T(4,128)(2,1)S(1)}, bf16[4,768]{1,0:T(4,128)(2,1)}, u32[]{:S(2)}) copy-start(bf16[4,768]{1,0:T(4,128)(2,1)} %step_query.3) | copy-start | bytes 18436
  38.4 19.0 %collective-permute-start.1 = (bf16[2,2,4,128,128]{4,3,2,1,0:T(8,128)(2,1)S(1)}, bf16[2,2,4,128,128]{4,3,2,1,0:T(8,128)(2,1)S(1)}, u32[]{:S(2)}, u32[]{:S(2)}) collective-permute-start(bf16[2,2,4,128,128]{4,3,2,1,0:T(8,128)(2,1)S(1)} %bitcast.5), channel_id=1, source_target_pairs={{16,0},{241,1},{18,2},{243,3},{20,4},{245,5},{22,6},{247,7},{24,8}... | collective-permute-start | bytes 1572872 | tf_op jit(solution)/shard_map/ppermute | solution.py:297
  41.1 9.0 %copy-start = (bf16[768,384]{1,0:T(8,128)(2,1)S(1)}, bf16[768,384]{1,0:T(8,128)(2,1)}, u32[]{:S(2)}) copy-start(bf16[768,384]{1,0:T(8,128)(2,1)} %weight.1) | copy-start | bytes 1769476
  42.2 7.9 %all-to-all-start = ((f32[4,32,128]{2,1,0:T(8,128)}), f32[4,32,128]{2,1,0:T(8,128)S(1)}, u32[]{:S(2)}, u32[]{:S(2)}) async-start(f32[4,32,128]{2,1,0:T(8,128)} %class_part.1), calls=%async_computation | async-start | bytes 131072 | tf_op jit(solution)/shard_map/all_to_all | solution.py:305
  45.5 4.6 %copy-start.4 = (bf16[4,1024]{1,0:T(4,128)(2,1)S(1)}, bf16[4,1024]{1,0:T(4,128)(2,1)}, u32[]{:S(2)}) copy-start(bf16[4,1024]{1,0:T(4,128)(2,1)} %step_key.1) | copy-start | bytes 24580
  45.5 4.6 %copy-start.5 = (bf16[4,1024]{1,0:T(4,128)(2,1)S(1)}, bf16[4,1024]{1,0:T(4,128)(2,1)}, u32[]{:S(2)}) copy-start(bf16[4,1024]{1,0:T(4,128)(2,1)} %step_value.1) | copy-start | bytes 24580
  45.5 16.3 %collective-permute-start = (bf16[1,2,4,128,128]{4,3,2,1,0:T(8,128)(2,1)S(1)}, bf16[1,2,4,128,128]{4,3,2,1,0:T(8,128)(2,1)S(1)}, u32[]{:S(2)}, u32[]{:S(2)}) collective-permute-start(bf16[1,2,4,128,128]{4,3,2,1,0:T(8,128)(2,1)S(1)} %constant_dynamic-slice_fusion), channel_id=1, source_target_pairs={{32,0},{225,1},{34,2},{227,3},{36,4},{229,5},{38,6},{231,7},{40,8}... | collective-permute-start | bytes 786440 | tf_op jit(solution)/shard_map/ppermute | solution.py:297
  51.0 13.1 %all-to-all-start.1 = ((bf16[16,8,384]{2,1,0:T(8,128)(2,1)}), bf16[16,8,384]{2,1,0:T(8,128)(2,1)S(1)}, u32[]{:S(2)}, u32[]{:S(2)}) async-start(bf16[16,8,384]{2,1,0:T(8,128)(2,1)} %project.1), calls=%async_computation.1 | async-start | bytes 196608 | tf_op jit(solution)/shard_map/all_to_all | solution.py:309
  61.8 2.3 %copy-start.1 = (bf16[128,768]{1,0:T(8,128)(2,1)S(1)}, bf16[128,768]{1,0:T(8,128)(2,1)}, u32[]{:S(2)}) copy-start(bf16[128,768]{1,0:T(8,128)(2,1)} %queries.1) | copy-start | bytes 589828
  61.8 2.3 %copy-start.6 = (s32[4]{0:T(128)S(1)}, s32[4]{0:T(128)}, u32[]{:S(2)}) copy-start(s32[4]{0:T(128)} %replica_of.1) | copy-start | bytes 52

commit v8 on v7

--- a/solution.py
+++ b/solution.py
@@ -44,7 +44,7 @@
 def pick(keys, values):
     return pl.pallas_call(
         pick_kernel,
-        out_shape=jax.ShapeDtypeStruct((ROWS, HD), jnp.bfloat16),
+        out_shape=pltpu.VMEM((ROWS, HD), jnp.bfloat16),
         in_specs=[pl.BlockSpec(memory_space=pltpu.HBM)] * 2,
         out_specs=pl.BlockSpec(memory_space=pltpu.VMEM),
         scratch_shapes=[pltpu.SemaphoreType.DMA],
@@ -119,7 +119,7 @@
 def class_part(doc_ids, step_query, far):
     return pl.pallas_call(
         class_part_kernel,
-        out_shape=jax.ShapeDtypeStruct((4, PAD, HD), jnp.float32),
+        out_shape=pltpu.VMEM((4, PAD, HD), jnp.float32),
         scratch_shapes=[pltpu.VMEM((PAD, HD), jnp.float32)],
         compiler_params=pltpu.CompilerParams(vmem_limit_bytes=8 * 1024 * 1024),
         cost_estimate=pl.CostEstimate(flops=3 * 10**7, bytes_accessed=10**6, transcendentals=4 * 10**4),
@@ -157,7 +157,7 @@
 def project(parts, step_query, step_key, step_value, weight):
     return pl.pallas_call(
         project_kernel,
-        out_shape=jax.ShapeDtypeStruct((16, 8, weight.shape[1]), jnp.bfloat16),
+        out_shape=pltpu.VMEM((16, 8, weight.shape[1]), jnp.bfloat16),
         scratch_shapes=[pltpu.VMEM((PAD, HD), jnp.float32)] * 2,
         compiler_params=pltpu.CompilerParams(vmem_limit_bytes=8 * 1024 * 1024),
         cost_estimate=pl.CostEstimate(flops=10**7, bytes_accessed=10**6, transcendentals=10**3),

time: 67.6 us -> 66.7 us (0.987)
  no operation moved by 1% of the time
where the time goes in v8:
time: 66.7 us; the launch traced here: 66.2 us
  blocking collectives  42.8 us (64%)
  starting transfers between devices  16.5 us (25%)
  Pallas kernels  5.74 us (9%)
  between operations  0.74 us (1%)
    all_gather x1, blocking collectives, local(): half = lax.all_gather(pick(keys, values), 'z1', axis=0)  23.9 us
    all_gather x1, blocking collectives, local(): far = lax.all_gather(half, ('yh', 'c'), axis=0).reshape(2, 2, 4, ROWS, HD)  12.3 us
    ppermute x2, starting transfers between devices, from_sides(): return lax.ppermute(a, CTX + TP, pairs)  6.83 us
    all_to_all x1, starting transfers between devices, local(): summed = lax.all_to_all(terms, TP, 0, 0)  6.38 us
    all_gather x2, blocking collectives, local(): others = [lax.all_gather(near[yh], 'c', axis=0) for yh in range(2)]  4.35 us
    all_to_all x1, starting transfers between devices, local(): decoded = lax.all_to_all(class_part(blocks, step_query, far), 'z0', 0, 0)  3.28 us
    pallas_call x1, Pallas kernels, prefill(): pl.pallas_call(prefill_kernel, out_shape=(jax.ShapeDtypeStruct((ROWS, HEA...  2.94 us
    all_gather x1, blocking collectives, local(): lax.all_gather(across[0], 'c', axis=0)  2.31 us
  transfers between devices with their start and end apart: 4, of which 1 were waited for; matrix products, arithmetic and copies ran while one was open for 0% of the time, Pallas kernels for 3%

profile of v8, /device:TPU:1, one launch (start us, length us, event | category | flops | bytes accessed | tf_op | source)
XLA Modules:
  0.0 66.2 jit_solution(15991940491273869085)
XLA Ops:
  0.6 0.8 %pick.1 = bf16[128,128]{1,0:T(8,128)(2,1)S(1)} custom-call(bf16[128,1024]{1,0:T(8,128)(2,1)} %keys.1, bf16[128,1024]{1,0:T(8,128)(2,1)} %values.1), custom_call_target="tpu_custom_call" | custom-call | tf_op jit(solution)/shard_map/pick/pallas_call | solution.py:45
  1.4 23.9 %all-gather = bf16[512,128]{1,0:T(8,128)(2,1)S(1)} all-gather(bf16[128,128]{1,0:T(8,128)(2,1)S(1)} %pick.1), channel_id=2, replica_groups=mesh['yh'=2,'z1'=4,'z0'=4,'x'=4,'yl'=2,'c'=2] {'z1'}, dimensions={0}, use_global_device_ids=true | all-gather | bytes 163840 | tf_op jit(solution)/shard_map/all_gather | solution.py:301
  25.3 12.3 %all-gather.1 = bf16[16,128,128]{2,1,0:T(8,128)(2,1)S(1)} all-gather(bf16[4,128,128]{2,1,0:T(8,128)(2,1)S(1)} %bitcast.11), channel_id=3, replica_groups=mesh['yh'=2,'z1'=4,'z0'=4,'x'=4,'yl'=2,'c'=2] {'yh','c'}, dimensions={0}, use_global_device_ids=true | all-gather | bytes 655360 | tf_op jit(solution)/shard_map/all_gather | solution.py:302
  37.6 2.6 %collective-permute-start.1 = (bf16[2,2,4,128,128]{4,3,2,1,0:T(8,128)(2,1)S(1)}, bf16[2,2,4,128,128]{4,3,2,1,0:T(8,128)(2,1)S(1)}, u32[]{:S(2)}, u32[]{:S(2)}) collective-permute-start(bf16[2,2,4,128,128]{4,3,2,1,0:T(8,128)(2,1)S(1)} %bitcast.5), channel_id=1, source_target_pairs={{16,0},{241,1},{18,2},{243,3},{20,4},{245,5},{22,6},{247,7},{24,8}... | collective-permute-start | bytes 1572872 | tf_op jit(solution)/shard_map/ppermute | solution.py:297
  40.2 0.0 copy-done.2
  40.2 0.0 copy-done.3
  40.3 0.0 copy-start
  40.3 1.1 %class_part.1 = f32[4,32,128]{2,1,0:T(8,128)} custom-call(s32[32,128]{1,0:T(8,128)S(1)} %bitcast.9, bf16[4,768]{1,0:T(4,128)(2,1)S(1)} %copy-done.3, bf16[2,2,4,128,128]{4,3,2,1,0:T(8,128)(2,1)S(1)} %bitcast.6), custom_call_target="tpu_custom_call" | custom-call | flops 30000000 | bytes 1000000 | tf_op jit(solution)/shard_map/class_part/pallas_call | solution.py:120
  41.3 3.3 %all-to-all-start = ((f32[4,32,128]{2,1,0:T(8,128)}), f32[4,32,128]{2,1,0:T(8,128)S(1)}, u32[]{:S(2)}, u32[]{:S(2)}) async-start(f32[4,32,128]{2,1,0:T(8,128)} %class_part.1), calls=%async_computation | async-start | bytes 131072 | tf_op jit(solution)/shard_map/all_to_all | solution.py:305
  44.6 0.0 copy-start.4
  44.6 0.0 copy-start.5
  44.7 4.2 %collective-permute-start = (bf16[1,2,4,128,128]{4,3,2,1,0:T(8,128)(2,1)S(1)}, bf16[1,2,4,128,128]{4,3,2,1,0:T(8,128)(2,1)S(1)}, u32[]{:S(2)}, u32[]{:S(2)}) collective-permute-start(bf16[1,2,4,128,128]{4,3,2,1,0:T(8,128)(2,1)S(1)} %constant_dynamic-slice_fusion), channel_id=1, source_target_pairs={{32,0},{225,1},{34,2},{227,3},{36,4},{229,5},{38,6},{231,7},{40,8}... | collective-permute-start | bytes 786440 | tf_op jit(solution)/shard_map/ppermute | solution.py:297
  48.9 0.3 all-to-all-done.parts
  49.2 0.0 copy-done
  49.2 0.0 copy-done.5
  49.2 0.9 %project.1 = bf16[16,8,384]{2,1,0:T(8,128)(2,1)} custom-call(f32[4,32,128]{2,1,0:T(8,128)S(1)} %all-to-all-done.parts, bf16[4,768]{1,0:T(4,128)(2,1)S(1)} %copy-done.3, bf16[4,1024]{1,0:T(4,128)(2,1)S(1)} %copy-done.4, bf16[4,1024]{1,0:T(4,128)(2,1)S(1)} %copy-done.5, bf16[768,384]{1,0:T(8,128)(2,1)S(1)} %copy-done), custom_call_target="tpu_custom_call" | custom-call | flops 10000000 | bytes 1000000 | tf_op jit(solution)/shard_map/project/pallas_call | solution.py:158
  50.2 6.4 %all-to-all-start.1 = ((bf16[16,8,384]{2,1,0:T(8,128)(2,1)}), bf16[16,8,384]{2,1,0:T(8,128)(2,1)S(1)}, u32[]{:S(2)}, u32[]{:S(2)}) async-start(bf16[16,8,384]{2,1,0:T(8,128)(2,1)} %project.1), calls=%async_computation.1 | async-start | bytes 196608 | tf_op jit(solution)/shard_map/all_to_all | solution.py:309
  56.6 0.0 collective-permute-done.1.near
  56.6 2.2 %all_gather.26.other1 = bf16[2,2,4,128,128]{4,3,2,1,0:T(8,128)(2,1)S(1)} all-gather(bf16[1,2,4,128,128]{4,3,2,1,0:T(8,128)(2,1)S(1)} %get-tuple-element.22), channel_id=1, replica_groups=mesh['yh'=2,'z1'=4,'z0'=4,'x'=4,'yl'=2,'c'=2] {'c'}, dimensions={0}, use_global_device_ids=true | all-gather | bytes 786432 | tf_op jit(solution)/shard_map/all_gather | solution.py:308
  58.8 2.2 %all_gather.25.other0 = bf16[2,2,4,128,128]{4,3,2,1,0:T(8,128)(2,1)S(1)} all-gather(bf16[1,2,4,128,128]{4,3,2,1,0:T(8,128)(2,1)S(1)} %get-tuple-element.23), channel_id=1, replica_groups=mesh['yh'=2,'z1'=4,'z0'=4,'x'=4,'yl'=2,'c'=2] {'c'}, dimensions={0}, use_global_device_ids=true | all-gather | bytes 786432 | tf_op jit(solution)/shard_map/all_gather | solution.py:308
  61.0 0.0 collective-permute-done
  61.0 2.3 %all_gather.27.across = bf16[2,2,4,128,128]{4,3,2,1,0:T(8,128)(2,1)S(1)} all-gather(bf16[1,2,4,128,128]{4,3,2,1,0:T(8,128)(2,1)S(1)} %collective-permute-done), channel_id=1, replica_groups=mesh['yh'=2,'z1'=4,'z0'=4,'x'=4,'yl'=2,'c'=2] {'c'}, dimensions={0}, use_global_device_ids=true | all-gather | bytes 786432 | tf_op jit(solution)/shard_map/all_gather | solution.py:311
  63.3 0.0 all-to-all-done.1.summed
  63.3 2.9 %prefill.1 = (bf16[128,768]{1,0:T(8,128)(2,1)}, bf16[32,384]{1,0:T(8,128)(2,1)}, bf16[64,2560]{1,0:T(8,128)(2,1)}, bf16[64,2560]{1,0:T(8,128)(2,1)}) custom-call(s32[4]{0:T(128)S(1)} %copy-done.6, s32[32,128]{1,0:T(8,128)S(1)} %bitcast.10, bf16[128,768]{1,0:T(8,128)(2,1)S(1)} %copy-done.1, bf16[16,8,384]{2,1,0:T(8,128)(2,1)S(1)} %all-to-all-done.1.summed, ...), custom_call_target="tpu_custom_call" | custom-call | flops 1000000 | bytes 100000 | tf_op jit(solution)/shard_map/prefill/pallas_call | solution.py:269
  (9 shorter events, 0.1 us)
Async XLA Ops:
  25.3 14.9 %copy-start.2 = (s32[4096]{0:T(1024)S(1)}, s32[4096]{0:T(1024)}, u32[]{:S(2)}) copy-start(s32[4096]{0:T(1024)} %param.12) | copy-start | bytes 49156
  25.3 14.9 %copy-start.3 = (bf16[4,768]{1,0:T(4,128)(2,1)S(1)}, bf16[4,768]{1,0:T(4,128)(2,1)}, u32[]{:S(2)}) copy-start(bf16[4,768]{1,0:T(4,128)(2,1)} %step_query.3) | copy-start | bytes 18436
  37.6 19.0 %collective-permute-start.1 = (bf16[2,2,4,128,128]{4,3,2,1,0:T(8,128)(2,1)S(1)}, bf16[2,2,4,128,128]{4,3,2,1,0:T(8,128)(2,1)S(1)}, u32[]{:S(2)}, u32[]{:S(2)}) collective-permute-start(bf16[2,2,4,128,128]{4,3,2,1,0:T(8,128)(2,1)S(1)} %bitcast.5), channel_id=1, source_target_pairs={{16,0},{241,1},{18,2},{243,3},{20,4},{245,5},{22,6},{247,7},{24,8}... | collective-permute-start | bytes 1572872 | tf_op jit(solution)/shard_map/ppermute | solution.py:297
  40.3 9.0 %copy-start = (bf16[768,384]{1,0:T(8,128)(2,1)S(1)}, bf16[768,384]{1,0:T(8,128)(2,1)}, u32[]{:S(2)}) copy-start(bf16[768,384]{1,0:T(8,128)(2,1)} %weight.1) | copy-start | bytes 1769476
  41.3 7.9 %all-to-all-start = ((f32[4,32,128]{2,1,0:T(8,128)}), f32[4,32,128]{2,1,0:T(8,128)S(1)}, u32[]{:S(2)}, u32[]{:S(2)}) async-start(f32[4,32,128]{2,1,0:T(8,128)} %class_part.1), calls=%async_computation | async-start | bytes 131072 | tf_op jit(solution)/shard_map/all_to_all | solution.py:305
  44.6 4.6 %copy-start.4 = (bf16[4,1024]{1,0:T(4,128)(2,1)S(1)}, bf16[4,1024]{1,0:T(4,128)(2,1)}, u32[]{:S(2)}) copy-start(bf16[4,1024]{1,0:T(4,128)(2,1)} %step_key.1) | copy-start | bytes 24580
  44.6 4.6 %copy-start.5 = (bf16[4,1024]{1,0:T(4,128)(2,1)S(1)}, bf16[4,1024]{1,0:T(4,128)(2,1)}, u32[]{:S(2)}) copy-start(bf16[4,1024]{1,0:T(4,128)(2,1)} %step_value.1) | copy-start | bytes 24580
  44.7 16.3 %collective-permute-start = (bf16[1,2,4,128,128]{4,3,2,1,0:T(8,128)(2,1)S(1)}, bf16[1,2,4,128,128]{4,3,2,1,0:T(8,128)(2,1)S(1)}, u32[]{:S(2)}, u32[]{:S(2)}) collective-permute-start(bf16[1,2,4,128,128]{4,3,2,1,0:T(8,128)(2,1)S(1)} %constant_dynamic-slice_fusion), channel_id=1, source_target_pairs={{32,0},{225,1},{34,2},{227,3},{36,4},{229,5},{38,6},{231,7},{40,8}... | collective-permute-start | bytes 786440 | tf_op jit(solution)/shard_map/ppermute | solution.py:297
  50.2 13.1 %all-to-all-start.1 = ((bf16[16,8,384]{2,1,0:T(8,128)(2,1)}), bf16[16,8,384]{2,1,0:T(8,128)(2,1)S(1)}, u32[]{:S(2)}, u32[]{:S(2)}) async-start(bf16[16,8,384]{2,1,0:T(8,128)(2,1)} %project.1), calls=%async_computation.1 | async-start | bytes 196608 | tf_op jit(solution)/shard_map/all_to_all | solution.py:309
  61.0 2.3 %copy-start.1 = (bf16[128,768]{1,0:T(8,128)(2,1)S(1)}, bf16[128,768]{1,0:T(8,128)(2,1)}, u32[]{:S(2)}) copy-start(bf16[128,768]{1,0:T(8,128)(2,1)} %queries.1) | copy-start | bytes 589828
  61.0 2.3 %copy-start.6 = (s32[4]{0:T(128)S(1)}, s32[4]{0:T(128)}, u32[]{:S(2)}) copy-start(s32[4]{0:T(128)} %replica_of.1) | copy-start | bytes 52
